TPU v7x, 256 devices: a whole 4x4x8 slice. The times are simulated.
256 devices in a mesh: row: 32 (over z_hi, y, core), col: 8 (over z_lo, x).
Axes of the slice: x: 4, y: 4, z: 8 (z_hi: 4, z_lo: 2; z = z_hi * 2 + z_lo), core: 2. Of those that a mesh axis runs over, the one named last changes fastest.
Arguments:
- acts: bfloat16 [131072, 4096], P(('row', 'col')), may hold values from -6 to 6
- key_cotangent: bfloat16 [131072, 512], P(('row', 'col')), may hold values from -4 to 4
- error_rows: bfloat16 [32, 8, 512, 4096], P('row', 'col'), may hold values from -12 to 12
- error_cols: float32 [8, 512, 4096], P('col', None, 'row'), may hold values from -2 to 2
Outputs:
- averaged: bfloat16 [512, 4096], P(None, 'row')
- new_error_rows: bfloat16 [32, 8, 512, 4096], P('row', 'col')
- new_error_cols: float32 [8, 512, 4096], P('col', None, 'row')
All inputs are finite; a program needn't handle non-finite values. Where the computation divides by a largest or mean magnitude, that divisor is 1e-20 or more.
Results may differ from a plain program's by a relative error of at most 0.025.
Values may be sent and summed in bfloat16 or wider, within the bound.
No kernel may reach another device: no remote copies, remote signals or barrier semaphores. Data moves between devices by JAX's collectives and lax.ppermute only.
A program may use at most 128 MiB of HBM per device.

v0:
```python
import jax
import jax.numpy as jnp
from jax import lax
from jax.sharding import PartitionSpec as P

BLK = 128


def compress(values):
    rows, cols = values.shape
    blocks = values.reshape(rows, cols // BLK, BLK)
    scale = jnp.mean(jnp.abs(blocks), axis=-1, keepdims=True) + 1e-06
    quant = (scale * jnp.tanh(blocks / scale)).reshape(rows, cols).astype(jnp.bfloat16)
    return lax.optimization_barrier(quant).astype(jnp.float32)


def project(grads_out, inputs):
    return lax.dot_general(
        grads_out, inputs, (((0,), (0,)), ((), ())), preferred_element_type=jnp.float32
    )


def body(acts, key_cotangent, error_rows, error_cols):
    rows_count = lax.axis_size("row")
    cols_count = lax.axis_size("col")
    residual = error_rows[0, 0].astype(jnp.float32)
    carried = project(key_cotangent, acts) + residual
    sent = compress(carried)
    summed = lax.psum_scatter(
        sent.astype(jnp.bfloat16), "row", scatter_dimension=1, tiled=True
    ).astype(jnp.float32)
    new_residual = carried - sent
    row_mean = summed / rows_count
    carried_two = row_mean + error_cols[0]
    sent_two = compress(carried_two)
    new_cols = (carried_two - sent_two)[None]
    partial_sum = lax.psum_scatter(
        sent_two.astype(jnp.bfloat16), "col", scatter_dimension=0, tiled=True
    ).astype(jnp.float32)
    block_mean = (partial_sum / cols_count).astype(jnp.bfloat16)
    averaged = lax.all_gather(block_mean, "col", axis=0, tiled=True)
    return (averaged, new_residual.astype(jnp.bfloat16)[None, None], new_cols)


def solution(mesh):
    in_specs = (
        P(("row", "col"), None),
        P(("row", "col"), None),
        P("row", "col", None, None),
        P("col", None, "row"),
    )
    out_specs = (P(None, "row"), P("row", "col", None, None), P("col", None, "row"))
    return jax.shard_map(body, mesh=mesh, in_specs=in_specs, out_specs=out_specs, check_vma=False)
```

profile of v0, /device:TPU:32, one launch (start us, length us, event | category | flops | bytes accessed | tf_op | source)
XLA Modules:
  0.0 226.3 jit_solution(1184811853256080962)
XLA Ops:
  7.2 0.0 copy-start
  7.2 0.0 reduce-scatter.7.cloned.1.call-start
  7.2 1.0 copy-done
  8.2 6.0 %convert_add_fusion = f32[512,4096]{1,0:T(8,128)S(1)} fusion(bf16[512,512]{1,0:T(8,128)(2,1)S(1)} %copy-done, bf16[512,4096]{1,0:T(8,128)(2,1)} %param.4, bf16[1,1,512,4096]{3,2,1,0:T(8,128)(2,1)} %param.6), kind=kOutput, calls=%fused_computation.4 | convolution fusion | flops 2151677952 | bytes 17301504 | tf_op jit(solution)/shard_map/dot_general | solution.py:18
  14.2 1.5 abs_bitcast_fusion
  15.7 1.7 copy-done.1
  17.4 5.0 %copy.9 = f32[64,8,32,128]{3,2,1,0:T(8,128)} copy(f32[64,8,32,128]{3,1,2,0:T(8,128)S(1)} %abs_bitcast_fusion) | data formatting | bytes 16777216
  22.4 5.6 %reduce_sum.18 = f32[512,32]{1,0:T(8,128)S(1)} reduce(f32[512,32,128]{2,1,0:T(8,128)} %bitcast.32, f32[]{:T(128)} %constant.5.clone.1), dimensions={2}, to_apply=%region_0.0 | reduce | flops 2080768 | bytes 8454148 | tf_op jit(solution)/shard_map/reduce_sum | solution.py:12
  28.1 2.5 %mul.20 = f32[512,32,128]{2,1,0:T(8,128)S(1)} broadcast(f32[512,32]{1,0:T(8,128)S(1)} %multiply_add_fusion), dimensions={0,1} | broadcast | bytes 8454144 | tf_op jit(solution)/shard_map/mul | solution.py:13
  30.6 11.2 %fusion.1 = bf16[512,4096]{1,0:T(8,128)(2,1)} fusion(f32[512,4096]{1,0:T(8,128)} %copy-done.1, f32[64,8,32,128]{3,2,1,0:T(8,128)S(1)} %bitcast.33), kind=kLoop, calls=%fused_computation.3 | loop fusion | flops 6291456 | bytes 20971520 | tf_op jit(solution)/shard_map/convert_element_type | solution.py:13
  41.8 6.6 %copy.7 = bf16[512,4096]{0,1:T(8,128)(2,1)} copy(bf16[512,4096]{1,0:T(8,128)(2,1)} %fusion.1) | data formatting | bytes 8388608
  48.4 0.0 reduce-scatter.7.cloned.1.call-update
  48.4 0.0 reduce-scatter.5.cloned.1.call-start
  48.5 101.2 %reduce-scatter.7.cloned.1.call-done = bf16[128,512]{1,0:T(8,128)(2,1)} async-done(((bf16[4096,512]{1,0:T(8,128)(2,1)}), bf16[128,512]{1,0:T(8,128)(2,1)}) %reduce-scatter.7.cloned.1.call-update) | async-done | bytes 131088
  149.7 1.0 copy.8
  150.7 0.1 abs_reduce_fusion
  150.9 0.8 multiply_convert_fusion
  151.7 0.0 reduce-scatter.5.cloned.1.call-update
  151.8 8.0 %fusion.2 = bf16[1,1,512,4096]{3,2,1,0:T(8,128)(2,1)} fusion(f32[512,4096]{1,0:T(8,128)} %copy-done.1, bf16[512,4096]{1,0:T(8,128)(2,1)} %fusion.1), kind=kLoop, calls=%fused_computation.7 | loop fusion | flops 6291456 | bytes 16777216 | tf_op jit(solution)/shard_map/broadcast_in_dim | solution.py:42
  159.8 0.7 subtract_bitcast_fusion
  160.6 29.4 %reduce-scatter.5.cloned.1.call-done = bf16[64,128]{1,0:T(8,128)(2,1)} async-done(((bf16[512,128]{1,0:T(8,128)(2,1)}), bf16[64,128]{1,0:T(8,128)(2,1)}) %reduce-scatter.5.cloned.1.call-update) | async-done | bytes 16400 | tf_op jit(solution)/shard_map/reduce_scatter | solution.py:37
  189.9 0.7 multiply_convert_fusion.1
  190.7 28.2 %all_gather.3 = bf16[512,128]{1,0:T(8,128)(2,1)S(1)} all-gather(bf16[64,128]{1,0:T(8,128)(2,1)S(1)} %multiply_convert_fusion.1), channel_id=1, replica_groups=mesh['row'=32,'col'=8] {'col'}, dimensions={0}, use_global_device_ids=true | all-gather | bytes 147456 | tf_op jit(solution)/shard_map/all_gather | solution.py:41
  218.8 0.7 copy.13
  (7 shorter events, 0.0 us)
Async XLA Ops:
  7.2 1.0 copy-start
  7.2 142.5 %reduce-scatter.7.cloned.1.call-start = ((), (), s32[]{:S(2)}) async-start(), calls=%async_computation.3 | async-start | bytes 4325376
  14.2 3.2 %copy-start.1 = (f32[512,4096]{1,0:T(8,128)}, f32[512,4096]{1,0:T(8,128)S(1)}, u32[]{:S(2)}) copy-start(f32[512,4096]{1,0:T(8,128)S(1)} %convert_add_fusion) | copy-start | bytes 25165828
  41.8 108.9 %copy-start.2 = (f32[1,512,128]{2,1,0:T(8,128)S(1)}, f32[1,512,128]{2,1,0:T(8,128)}, u32[]{:S(2)}) copy-start(f32[1,512,128]{2,1,0:T(8,128)} %param.7) | copy-start | bytes 786436
  48.4 141.5 %reduce-scatter.5.cloned.1.call-start = ((), (), s32[]{:S(2)}) async-start(), calls=%async_computation.2 | async-start | bytes 147456 | tf_op jit(solution)/shard_map/reduce_scatter | solution.py:37
  151.7 8.1 %copy-start.3 = (bf16[512,128]{1,0:T(8,128)(2,1)S(1)}, bf16[512,128]{1,0:T(8,128)(2,1)}, u32[]{:S(2)}) copy-start(bf16[512,128]{1,0:T(8,128)(2,1)} %multiply_convert_fusion) | copy-start | bytes 393220
Sparse Core Ops, SparseCore 0:
  48.6 101.1 reduce-scatter.6
  152.9 36.9 reduce-scatter.4
where the time goes:
time: 228 us; the launch traced here: 226 us
  waiting for transfers between devices  131 us (57%)
  other arithmetic  28.8 us (13%)
  blocking collectives  28.2 us (12%)
  local copies, waits for them, and re-layouts  18.5 us (8%)
  between operations  14.1 us (6%)
  matrix products  5.97 us (3%)
    unnamed x3, waiting for transfers between devices  101 us
    reduce_scatter x1, waiting for transfers between devices, body(): lax.psum_scatter(sent_two.astype(jnp.bfloat16), 'col', scatter_dimension=...  29.4 us
    all_gather x1, blocking collectives, body(): averaged = lax.all_gather(block_mean, 'col', axis=0, tiled=True)  28.2 us
    unnamed x12, local copies, waits for them, and re-layouts  16 us
    convert_element_type x2, other arithmetic, compress(): (scale * jnp.tanh(blocks / scale)).reshape(rows, cols).astype(jnp.bfloat16)  12 us
    broadcast_in_dim x1, other arithmetic, body(): return (averaged, new_residual.astype(jnp.bfloat16)[None, None], new_cols)  8.04 us
    dot_general x1, matrix products, project(): lax.dot_general(grads_out, inputs, (((0,), (0,)), ((), ())), preferred_el...  5.97 us
    reduce_sum x2, other arithmetic, compress(): scale = jnp.mean(jnp.abs(blocks), axis=-1, keepdims=True) + 1e-06  5.77 us
  transfers between devices with their start and end apart: 2, of which 2 were waited for; matrix products, arithmetic and copies ran while one was open for 4% of the time, Pallas kernels for 0%

commit v1 on v0

v1 whole, which is shorter than its diff:
```python
import functools

import jax
import jax.numpy as jnp
from jax import lax
from jax.experimental import pallas as pl
from jax.experimental.pallas import tpu as pltpu
from jax.sharding import Mesh
from jax.sharding import PartitionSpec as P

BLK = 128
BF = jnp.bfloat16
F32 = jnp.float32
MIB = 2**20
FIRST = ((2, 0), (2, 1), (1, 2), (1, 3), (2, 2), (2, 3), (3, 0), (3, 1))
SECOND = ((1, 0), (1, 1), (3, 2), (3, 3), (0, 0), (0, 1), (0, 2), (0, 3))


def squash(v):
    m = jnp.sum(jnp.abs(v), axis=1, keepdims=True) * (1.0 / BLK) + 1e-6
    return (m * jnp.tanh(v * (1.0 / m))).astype(BF)


def grad_kernel(pos, kc, acts, err, _, newerr, send, keep, kcv, kct, av, ev, sv, kv, gv, ksem, asem, esem, osem, *, table):
    n = len(table)
    zh, y, core = pos[0], pos[1], pos[2]
    kcp = pltpu.make_async_copy(kc, kcv, ksem)
    kcp.start()
    ins, cols = [], []
    for i, (dy, dz) in enumerate(table):
        col = pl.multiple_of((lax.rem(zh + dz, 4) * 4 + lax.rem(y + dy, 4)) * 256, 256)
        cols.append(col)
        a = pltpu.make_async_copy(acts.at[:, pl.ds(col, 256)], av.at[i], asem.at[i])
        e = pltpu.make_async_copy(err.at[:, pl.ds(col, 256)], ev.at[i], esem.at[i])
        a.start()
        e.start()
        ins.append((a, e))
    kcp.wait()
    kct[...] = kcv[...].T

    def product(i):
        for copy in ins[i]:
            copy.wait()
        gv[i % 2] = jnp.dot(kct[...], av[i], preferred_element_type=F32)

    outs = []
    product(0)
    for i in range(n):
        if i + 1 < n:
            product(i + 1)
        g = gv[i % 2]
        q = []
        for k in range(2):
            s = slice(k * BLK, (k + 1) * BLK)
            v = g[:, s] + ev[i, :, s].astype(F32)
            q.append(squash(v))
            ev[i, :, s] = (v - q[k].astype(F32)).astype(BF)
        kv[i] = jnp.where(core == 0, q[0], q[1])
        sv[i] = jnp.where(core == 0, q[1], q[0])
        pairs = (
            (sv.at[i], send.at[i]),
            (kv.at[i], keep.at[i]),
            (ev.at[i], newerr.at[:, pl.ds(cols[i], 256)]),
        )
        for k, (src, dst) in enumerate(pairs):
            copy = pltpu.make_async_copy(src, dst, osem.at[i, k])
            copy.start()
            outs.append(copy)
    for copy in outs:
        copy.wait()


def grad_part(table, pos, kc, acts, err, newerr):
    n = len(table)
    any_space = pl.BlockSpec(memory_space=pl.ANY)
    half = jax.ShapeDtypeStruct((n, 512, BLK), BF)
    body = functools.partial(grad_kernel, table=table)
    operands = (pos, kc, acts, err, newerr)
    aliases = {4: 0}
    if newerr is None:
        operands, aliases = operands[:4], {}
        body = lambda *refs: grad_kernel(*refs[:4], None, *refs[4:], table=table)
    return pl.pallas_call(
        body,
        in_specs=[pl.BlockSpec(memory_space=pltpu.SMEM)] + [any_space] * (len(operands) - 1),
        out_specs=[any_space] * 3,
        out_shape=[jax.ShapeDtypeStruct((512, 4096), BF), half, half],
        scratch_shapes=[
            pltpu.VMEM((512, 512), BF),
            pltpu.VMEM((512, 512), BF),
            pltpu.VMEM((n, 512, 256), BF),
            pltpu.VMEM((n, 512, 256), BF),
            pltpu.VMEM((n, 512, BLK), BF),
            pltpu.VMEM((n, 512, BLK), BF),
            pltpu.VMEM((2, 512, 256), F32),
            pltpu.SemaphoreType.DMA,
            pltpu.SemaphoreType.DMA((n,)),
            pltpu.SemaphoreType.DMA((n,)),
            pltpu.SemaphoreType.DMA((n, 3)),
        ],
        input_output_aliases=aliases,
        compiler_params=pltpu.CompilerParams(vmem_limit_bytes=40 * MIB),
        cost_estimate=pl.CostEstimate(
            flops=2 * 512 * 512 * 256 * n, bytes_accessed=n * MIB, transcendentals=0
        ),
    )(*operands)


def step(x, axis, distance):
    size = lax.axis_size(axis)
    return lax.ppermute(x, axis, [(i, (i + distance) % size) for i in range(size)])


def add(*terms):
    total = terms[0].astype(F32)
    for term in terms[1:]:
        total = total + term.astype(F32)
    return total


def body(acts, key_cotangent, error_rows, error_cols):
    pos = jnp.stack([lax.axis_index("zh"), lax.axis_index("y"), lax.axis_index("core")]).astype(jnp.int32)
    err = error_rows[0, 0]
    newerr, send_1, keep_1 = grad_part(FIRST, pos, key_cotangent, acts, err, None)
    got_1 = step(send_1, "core", 1)
    newerr, send_2, keep_2 = grad_part(SECOND, pos, key_cotangent, acts, err, newerr)
    got_2 = step(send_2, "core", 1)
    up_1 = step(add(keep_1[:4], got_1[:4]).astype(BF), "y", 1)
    down_1 = step(add(keep_1[4:], got_1[4:]).astype(BF), "y", -1)
    up_2 = step(add(keep_2[:2], got_2[:2], up_1[:2]).astype(BF), "y", 1)
    down_2 = step(add(keep_2[2:4], got_2[2:4], down_1[:2]).astype(BF), "y", -1)
    low = add(keep_2[4:6], got_2[4:6], down_1[2:], up_2)
    high = add(keep_2[6:], got_2[6:], up_1[2:], down_2)
    near = step(low[1].astype(BF), "zh", 1)
    far = step(high[0].astype(BF), "zh", 2)
    back = step(high[1].astype(BF), "zh", -1)
    summed = add(low[0], near, far, back)

    carried_two = summed * (1.0 / 32.0) + error_cols[0]
    sent_two = lax.optimization_barrier(squash(carried_two))
    new_cols = (carried_two - sent_two.astype(F32))[None]
    copies = jnp.broadcast_to(sent_two[None], (8, 512, BLK))
    parts = lax.all_to_all(copies, ("zl", "x"), 0, 0, tiled=True)
    averaged = (jnp.sum(parts.astype(F32), axis=0) * 0.125).astype(BF)
    return averaged, newerr[None, None], new_cols


def solution(mesh):
    fine = Mesh(mesh.devices.reshape(4, 4, 2, 2, 4), ("zh", "y", "core", "zl", "x"))
    row, col = ("zh", "y", "core"), ("zl", "x")
    in_specs = (
        P(row + col, None),
        P(row + col, None),
        P(row, col, None, None),
        P(col, None, row),
    )
    out_specs = (P(None, row), P(row, col, None, None), P(col, None, row))
    return jax.shard_map(body, mesh=fine, in_specs=in_specs, out_specs=out_specs, check_vma=False)
```

time: 228 us -> 95 us (0.42)
  waiting for transfers between devices: 131 us -> 44.4 us
  blocking collectives: 28.2 us -> 0 us
  other arithmetic: 28.8 us -> 2.79 us
  starting transfers between devices: 0.08 us -> 21.9 us
  Pallas kernels: 0 us -> 17.6 us
  between operations: 14.1 us -> 0.71 us
  local copies, waits for them, and re-layouts: 18.5 us -> 6.57 us
  matrix products: 5.97 us -> 0 us
    unnamed x3 -> x0, waiting for transfers between devices: 101 us -> none
    ppermute x0 -> x9, waiting for transfers between devices: none -> 31.2 us  [step(): lax.ppermute(x, axis, [(i, (i + distance) % size) for i in range(size)])]
    reduce_scatter x1 -> x0, waiting for transfers between devices: 29.4 us -> none  [body(): lax.psum_scatter(sent_two.astype(jnp.bfloat16), 'col', scatter_dimension=...]
    all_gather x1 -> x0, blocking collectives: 28.2 us -> none  [body(): averaged = lax.all_gather(block_mean, 'col', axis=0, tiled=True)]
    pallas_call x0 -> x2, Pallas kernels: none -> 17.6 us  [grad_part(): pl.pallas_call(body, in_specs=[pl.BlockSpec(memory_space=pltpu.SMEM)] + [...]
    ppermute x0 -> x9, starting transfers between devices: none -> 15.4 us  [step(): lax.ppermute(x, axis, [(i, (i + distance) % size) for i in range(size)])]
    all_to_all x0 -> x1, waiting for transfers between devices: none -> 13.2 us  [body(): parts = lax.all_to_all(copies, ('zl', 'x'), 0, 0, tiled=True)]
    convert_element_type x3 -> x4, other arithmetic: 12.8 us -> 1.27 us  [the longest x1 0.67 us: body(): averaged = (jnp.sum(parts.astype(F32), axis=0) * 0.125).astype(BF)]
  transfers between devices with their start and end apart: 2 -> 10, of which waited for: 2 -> 6; matrix products, arithmetic and copies ran while one was open for 4% -> 1% of each run, Pallas kernels for 0% -> 9%
where the time goes in v1:
time: 95 us; the launch traced here: 94 us
  waiting for transfers between devices  44.4 us (47%)
  starting transfers between devices  21.9 us (23%)
  Pallas kernels  17.6 us (19%)
  local copies, waits for them, and re-layouts  6.57 us (7%)
  other arithmetic  2.79 us (3%)
    ppermute x9, waiting for transfers between devices, step(): lax.ppermute(x, axis, [(i, (i + distance) % size) for i in range(size)])  31.2 us
    pallas_call x2, Pallas kernels, grad_part(): pl.pallas_call(body, in_specs=[pl.BlockSpec(memory_space=pltpu.SMEM)] + [...  17.6 us
    ppermute x9, starting transfers between devices, step(): lax.ppermute(x, axis, [(i, (i + distance) % size) for i in range(size)])  15.4 us
    all_to_all x1, waiting for transfers between devices, body(): parts = lax.all_to_all(copies, ('zl', 'x'), 0, 0, tiled=True)  13.2 us
    all_to_all x1, starting transfers between devices, body(): parts = lax.all_to_all(copies, ('zl', 'x'), 0, 0, tiled=True)  6.51 us
    unnamed x8, local copies, waits for them, and re-layouts  5.42 us
  transfers between devices with their start and end apart: 10, of which 6 were waited for; matrix products, arithmetic and copies ran while one was open for 1% of the time, Pallas kernels for 9%

profile of v1, /device:TPU:32, one launch (start us, length us, event | category | flops | bytes accessed | tf_op | source)
XLA Modules:
  0.0 94.0 jit_solution(1953302616985936360)
XLA Ops:
  0.7 2.2 %copy-done = bf16[512,4096]{1,0:T(8,128)(2,1)S(1)} copy-done((bf16[512,4096]{1,0:T(8,128)(2,1)S(1)}, bf16[512,4096]{1,0:T(8,128)(2,1)}, u32[]{:S(2)}) %copy-start) | copy-done | bytes 4194328
  2.9 2.2 %copy-done.1 = bf16[1,1,512,4096]{3,2,1,0:T(8,128)(2,1)S(1)} copy-done((bf16[1,1,512,4096]{3,2,1,0:T(8,128)(2,1)S(1)}, bf16[1,1,512,4096]{3,2,1,0:T(8,128)(2,1)}, u32[]{:S(2)}) %copy-start.1) | copy-done | bytes 4194328
  5.1 1.0 %copy-done.2 = bf16[512,512]{1,0:T(8,128)(2,1)S(1)} copy-done((bf16[512,512]{1,0:T(8,128)(2,1)S(1)}, bf16[512,512]{1,0:T(8,128)(2,1)}, u32[]{:S(2)}) %copy-start.2) | copy-done | bytes 524312
  6.1 8.8 %shard_map.67 = (bf16[512,4096]{1,0:T(8,128)(2,1)}, bf16[8,512,128]{2,1,0:T(8,128)(2,1)S(1)}, bf16[8,512,128]{2,1,0:T(8,128)(2,1)S(1)}) custom-call(s32[3]{0:T(128)S(1)} %pad_add_fusion.refs_0_.pos, bf16[512,512]{1,0:T(8,128)(2,1)S(1)} %copy-done.2, bf16[512,4096]{1,0:T(8,128)(2,1)S(1)} %copy-done, bf16[512,4096]{1,0:T(8,128)(2,1)S(1)} %bitcast.29), custom_call_target="tpu_custom_call" | custom-call | flops 1073741824 | bytes 8388608 | tf_op jit(solution)/shard_map/pallas_call | solution.py:83
  15.0 8.8 %shard_map.68 = (bf16[512,4096]{1,0:T(8,128)(2,1)}, bf16[8,512,128]{2,1,0:T(8,128)(2,1)S(1)}, bf16[8,512,128]{2,1,0:T(8,128)(2,1)S(1)}) custom-call(s32[3]{0:T(128)S(1)} %pad_add_fusion.refs_0_.pos, bf16[512,512]{1,0:T(8,128)(2,1)S(1)} %copy-done.2, bf16[512,4096]{1,0:T(8,128)(2,1)S(1)} %copy-done, ...), custom_call_target="tpu_custom_call", output_to_operand_aliasing={{0}: (4, {})} | custom-call | flops 1073741824 | bytes 8388608 | tf_op jit(solution)/shard_map/pallas_call | solution.py:83
  23.8 0.6 collective-permute-start
  24.4 0.3 add_convert_fusion
  24.7 1.7 %collective-permute-start.3 = (bf16[4,512,128]{2,1,0:T(8,128)(2,1)S(1)}, bf16[4,512,128]{2,1,0:T(8,128)(2,1)S(1)}, u32[]{:S(2)}, u32[]{:S(2)}) collective-permute-start(bf16[4,512,128]{2,1,0:T(8,128)(2,1)S(1)} %get-tuple-element.19), channel_id=1, source_target_pairs={{0,16},{16,32},{32,48},{48,0},{1,17},{17,33},{33,49},{49,1},{2,18}... | collective-permute-start | bytes 1572872 | tf_op jit(solution)/shard_map/ppermute | solution.py:111
  26.3 1.7 %collective-permute-start.2 = (bf16[4,512,128]{2,1,0:T(8,128)(2,1)S(1)}, bf16[4,512,128]{2,1,0:T(8,128)(2,1)S(1)}, u32[]{:S(2)}, u32[]{:S(2)}) collective-permute-start(bf16[4,512,128]{2,1,0:T(8,128)(2,1)S(1)} %get-tuple-element.20), channel_id=1, source_target_pairs={{0,48},{16,0},{32,16},{48,32},{1,49},{17,1},{33,17},{49,33},{2,50}... | collective-permute-start | bytes 1572872 | tf_op jit(solution)/shard_map/ppermute | solution.py:111
  28.0 11.9 %collective-permute-done.3 = bf16[4,512,128]{2,1,0:T(8,128)(2,1)S(1)} collective-permute-done((bf16[4,512,128]{2,1,0:T(8,128)(2,1)S(1)}, bf16[4,512,128]{2,1,0:T(8,128)(2,1)S(1)}, u32[]{:S(2)}, u32[]{:S(2)}) %collective-permute-start.3) | collective-permute-done | bytes 524320 | tf_op jit(solution)/shard_map/ppermute | solution.py:111
  40.0 0.6 collective-permute-start.4
  40.6 8.4 %collective-permute-done.4 = bf16[2,512,128]{2,1,0:T(8,128)(2,1)S(1)} collective-permute-done((bf16[2,512,128]{2,1,0:T(8,128)(2,1)S(1)}, bf16[2,512,128]{2,1,0:T(8,128)(2,1)S(1)}, u32[]{:S(2)}, u32[]{:S(2)}) %collective-permute-start.4) | collective-permute-done | bytes 262176 | tf_op jit(solution)/shard_map/ppermute | solution.py:111
  49.2 0.5 collective-permute-start.6
  49.7 3.4 %collective-permute-start.5 = (bf16[512,128]{1,0:T(8,128)(2,1)S(1)}, bf16[512,128]{1,0:T(8,128)(2,1)S(1)}, u32[]{:S(2)}, u32[]{:S(2)}) collective-permute-start(bf16[512,128]{1,0:T(8,128)(2,1)S(1)} %fusion.5), channel_id=1, source_target_pairs={{0,64},{64,128},{128,192},{192,0},{1,65},{65,129},{129,193},{193,1... | collective-permute-start | bytes 393224 | tf_op jit(solution)/shard_map/ppermute | solution.py:111
  53.1 2.7 %collective-permute-done.6 = bf16[2,512,128]{2,1,0:T(8,128)(2,1)S(1)} collective-permute-done((bf16[2,512,128]{2,1,0:T(8,128)(2,1)S(1)}, bf16[2,512,128]{2,1,0:T(8,128)(2,1)S(1)}, u32[]{:S(2)}, u32[]{:S(2)}) %collective-permute-start.6) | collective-permute-done | bytes 262176 | tf_op jit(solution)/shard_map/ppermute | solution.py:111
  56.0 6.4 %collective-permute-start.7 = (bf16[512,128]{1,0:T(8,128)(2,1)S(1)}, bf16[512,128]{1,0:T(8,128)(2,1)S(1)}, u32[]{:S(2)}, u32[]{:S(2)}) collective-permute-start(bf16[512,128]{1,0:T(8,128)(2,1)S(1)} %get-tuple-element.21), channel_id=1, source_target_pairs={{0,128},{64,192},{128,0},{192,64},{1,129},{65,193},{129,1},{193,65... | collective-permute-start | bytes 393224 | tf_op jit(solution)/shard_map/ppermute | solution.py:111
  62.3 0.6 collective-permute-start.8
  62.9 4.6 %collective-permute-done.7 = bf16[512,128]{1,0:T(8,128)(2,1)S(1)} collective-permute-done((bf16[512,128]{1,0:T(8,128)(2,1)S(1)}, bf16[512,128]{1,0:T(8,128)(2,1)S(1)}, u32[]{:S(2)}, u32[]{:S(2)}) %collective-permute-start.7) | collective-permute-done | bytes 131104 | tf_op jit(solution)/shard_map/ppermute | solution.py:111
  67.5 3.7 %collective-permute-done.8 = bf16[512,128]{1,0:T(8,128)(2,1)S(1)} collective-permute-done((bf16[512,128]{1,0:T(8,128)(2,1)S(1)}, bf16[512,128]{1,0:T(8,128)(2,1)S(1)}, u32[]{:S(2)}, u32[]{:S(2)}) %collective-permute-start.8) | collective-permute-done | bytes 131104 | tf_op jit(solution)/shard_map/ppermute | solution.py:111
  71.6 1.1 %broadcast_in_dim.6 = bf16[8,512,128]{2,1,0:T(8,128)(2,1)} broadcast(bf16[512,128]{1,0:T(8,128)(2,1)S(1)} %multiply_convert_fusion.1), dimensions={1,2} | broadcast | bytes 1179648 | tf_op jit(solution)/shard_map/broadcast_in_dim | solution.py:142
  72.7 6.5 %all-to-all-start = ((bf16[8,512,128]{2,1,0:T(8,128)(2,1)}), bf16[8,512,128]{2,1,0:T(8,128)(2,1)S(1)}, u32[]{:S(2)}, u32[]{:S(2)}) async-start(bf16[8,512,128]{2,1,0:T(8,128)(2,1)} %broadcast_in_dim.6), calls=%async_computation | async-start | bytes 2097152 | tf_op jit(solution)/shard_map/all_to_all | solution.py:143
  79.2 0.7 subtract_bitcast_fusion
  79.9 13.2 %all-to-all-done = bf16[8,512,128]{2,1,0:T(8,128)(2,1)S(1)} async-done(((bf16[8,512,128]{2,1,0:T(8,128)(2,1)}), bf16[8,512,128]{2,1,0:T(8,128)(2,1)S(1)}, u32[]{:S(2)}, u32[]{:S(2)}) %all-to-all-start) | async-done | bytes 1048608 | tf_op jit(solution)/shard_map/all_to_all | solution.py:143
  93.3 0.7 multiply_convert_fusion
  (20 shorter events, 1.3 us)
Async XLA Ops:
  0.7 2.2 %copy-start = (bf16[512,4096]{1,0:T(8,128)(2,1)S(1)}, bf16[512,4096]{1,0:T(8,128)(2,1)}, u32[]{:S(2)}) copy-start(bf16[512,4096]{1,0:T(8,128)(2,1)} %acts.1) | copy-start | bytes 12582916
  2.9 2.2 %copy-start.1 = (bf16[1,1,512,4096]{3,2,1,0:T(8,128)(2,1)S(1)}, bf16[1,1,512,4096]{3,2,1,0:T(8,128)(2,1)}, u32[]{:S(2)}) copy-start(bf16[1,1,512,4096]{3,2,1,0:T(8,128)(2,1)} %param.6) | copy-start | bytes 12582916
  5.1 1.0 %copy-start.2 = (bf16[512,512]{1,0:T(8,128)(2,1)S(1)}, bf16[512,512]{1,0:T(8,128)(2,1)}, u32[]{:S(2)}) copy-start(bf16[512,512]{1,0:T(8,128)(2,1)} %kc.1) | copy-start | bytes 1572868
  14.9 9.5 %collective-permute-start.1 = (bf16[8,512,128]{2,1,0:T(8,128)(2,1)S(1)}, bf16[8,512,128]{2,1,0:T(8,128)(2,1)S(1)}, u32[]{:S(2)}, u32[]{:S(2)}) collective-permute-start(bf16[8,512,128]{2,1,0:T(8,128)(2,1)S(1)} %get-tuple-element.13), channel_id=1, source_target_pairs={{0,8},{8,0},{1,9},{9,1},{2,10},{10,2},{3,11},{11,3},{4,12},{12,4},... | collective-permute-start | bytes 3145736 | tf_op jit(solution)/shard_map/ppermute | solution.py:111
  23.8 4.2 %collective-permute-start = (bf16[8,512,128]{2,1,0:T(8,128)(2,1)S(1)}, bf16[8,512,128]{2,1,0:T(8,128)(2,1)S(1)}, u32[]{:S(2)}, u32[]{:S(2)}) collective-permute-start(bf16[8,512,128]{2,1,0:T(8,128)(2,1)S(1)} %get-tuple-element.11), channel_id=1, source_target_pairs={{0,8},{8,0},{1,9},{9,1},{2,10},{10,2},{3,11},{11,3},{4,12},{12,4},... | collective-permute-start | bytes 3145736 | tf_op jit(solution)/shard_map/ppermute | solution.py:111
  24.4 46.8 %copy-start.3 = (f32[1,512,128]{2,1,0:T(8,128)S(1)}, f32[1,512,128]{2,1,0:T(8,128)}, u32[]{:S(2)}) copy-start(f32[1,512,128]{2,1,0:T(8,128)} %param.7) | copy-start | bytes 786436
  24.7 15.2 %collective-permute-start.3 = (bf16[4,512,128]{2,1,0:T(8,128)(2,1)S(1)}, bf16[4,512,128]{2,1,0:T(8,128)(2,1)S(1)}, u32[]{:S(2)}, u32[]{:S(2)}) collective-permute-start(bf16[4,512,128]{2,1,0:T(8,128)(2,1)S(1)} %get-tuple-element.19), channel_id=1, source_target_pairs={{0,16},{16,32},{32,48},{48,0},{1,17},{17,33},{33,49},{49,1},{2,18}... | collective-permute-start | bytes 1572872 | tf_op jit(solution)/shard_map/ppermute | solution.py:111
  26.3 14.2 %collective-permute-start.2 = (bf16[4,512,128]{2,1,0:T(8,128)(2,1)S(1)}, bf16[4,512,128]{2,1,0:T(8,128)(2,1)S(1)}, u32[]{:S(2)}, u32[]{:S(2)}) collective-permute-start(bf16[4,512,128]{2,1,0:T(8,128)(2,1)S(1)} %get-tuple-element.20), channel_id=1, source_target_pairs={{0,48},{16,0},{32,16},{48,32},{1,49},{17,1},{33,17},{49,33},{2,50}... | collective-permute-start | bytes 1572872 | tf_op jit(solution)/shard_map/ppermute | solution.py:111
  40.0 8.9 %collective-permute-start.4 = (bf16[2,512,128]{2,1,0:T(8,128)(2,1)S(1)}, bf16[2,512,128]{2,1,0:T(8,128)(2,1)S(1)}, u32[]{:S(2)}, u32[]{:S(2)}) collective-permute-start(bf16[2,512,128]{2,1,0:T(8,128)(2,1)S(1)} %add_convert_fusion.4), channel_id=1, source_target_pairs={{0,16},{16,32},{32,48},{48,0},{1,17},{17,33},{33,49},{49,1},{2,18}... | collective-permute-start | bytes 786440 | tf_op jit(solution)/shard_map/ppermute | solution.py:111
  49.2 6.6 %collective-permute-start.6 = (bf16[2,512,128]{2,1,0:T(8,128)(2,1)S(1)}, bf16[2,512,128]{2,1,0:T(8,128)(2,1)S(1)}, u32[]{:S(2)}, u32[]{:S(2)}) collective-permute-start(bf16[2,512,128]{2,1,0:T(8,128)(2,1)S(1)} %get-tuple-element.18), channel_id=1, source_target_pairs={{0,48},{16,0},{32,16},{48,32},{1,49},{17,1},{33,17},{49,33},{2,50}... | collective-permute-start | bytes 786440 | tf_op jit(solution)/shard_map/ppermute | solution.py:111
  49.7 13.2 %collective-permute-start.5 = (bf16[512,128]{1,0:T(8,128)(2,1)S(1)}, bf16[512,128]{1,0:T(8,128)(2,1)S(1)}, u32[]{:S(2)}, u32[]{:S(2)}) collective-permute-start(bf16[512,128]{1,0:T(8,128)(2,1)S(1)} %fusion.5), channel_id=1, source_target_pairs={{0,64},{64,128},{128,192},{192,0},{1,65},{65,129},{129,193},{193,1... | collective-permute-start | bytes 393224 | tf_op jit(solution)/shard_map/ppermute | solution.py:111
  56.0 11.6 %collective-permute-start.7 = (bf16[512,128]{1,0:T(8,128)(2,1)S(1)}, bf16[512,128]{1,0:T(8,128)(2,1)S(1)}, u32[]{:S(2)}, u32[]{:S(2)}) collective-permute-start(bf16[512,128]{1,0:T(8,128)(2,1)S(1)} %get-tuple-element.21), channel_id=1, source_target_pairs={{0,128},{64,192},{128,0},{192,64},{1,129},{65,193},{129,1},{193,65... | collective-permute-start | bytes 393224 | tf_op jit(solution)/shard_map/ppermute | solution.py:111
  62.3 8.8 %collective-permute-start.8 = (bf16[512,128]{1,0:T(8,128)(2,1)S(1)}, bf16[512,128]{1,0:T(8,128)(2,1)S(1)}, u32[]{:S(2)}, u32[]{:S(2)}) collective-permute-start(bf16[512,128]{1,0:T(8,128)(2,1)S(1)} %get-tuple-element.22), channel_id=1, source_target_pairs={{0,192},{64,0},{128,64},{192,128},{1,193},{65,1},{129,65},{193,129... | collective-permute-start | bytes 393224 | tf_op jit(solution)/shard_map/ppermute | solution.py:111
  72.7 20.4 %all-to-all-start = ((bf16[8,512,128]{2,1,0:T(8,128)(2,1)}), bf16[8,512,128]{2,1,0:T(8,128)(2,1)S(1)}, u32[]{:S(2)}, u32[]{:S(2)}) async-start(bf16[8,512,128]{2,1,0:T(8,128)(2,1)} %broadcast_in_dim.6), calls=%async_computation | async-start | bytes 2097152 | tf_op jit(solution)/shard_map/all_to_all | solution.py:143

commit v2 on v1

v2 whole, which is shorter than its diff:
```python
import functools

import jax
import jax.numpy as jnp
from jax import lax
from jax.experimental import pallas as pl
from jax.experimental.pallas import tpu as pltpu
from jax.sharding import Mesh
from jax.sharding import PartitionSpec as P

BLK = 128
BF = jnp.bfloat16
F32 = jnp.float32
MIB = 2**20
CHUNKS = ((0, 512),)


def partner(which, i, core):
    flip = lax.bitwise_xor(i, 1)
    turn = 3 - i
    return jnp.where(core == which, flip, turn)


def ring_pairs(which, shape, ring, core):
    def linear(pos):
        out = 0
        for p, n in zip(pos, shape):
            out = out * n + p
        return out

    pairs = []
    for r in range(4):
        for c in range(2):
            src, dst = [0, 0], [0, 0]
            src[ring], src[core] = r, c
            dst[ring], dst[core] = (r ^ 1 if c == which else 3 - r), c
            pairs.append((linear(src), linear(dst)))
    return pairs


def squash(v):
    m = jnp.sum(jnp.abs(v), axis=1, keepdims=True) * (1.0 / BLK) + 1e-6
    return (m * jnp.tanh(v * (1.0 / m))).astype(BF)


def grad_kernel(pos, kc, acts, err, newerr, send, keep, kcv, kct, av, ev, sv, kv, gv, ksem, asem, osem, *, rows):
    n = 8
    row0, count = rows
    kcp = pltpu.make_async_copy(kc.at[:, pl.ds(row0, count)], kcv, ksem)
    kcp.start()
    ins, cols = [], []
    for i in range(n):
        ins.append([])
        cols.append([])
        for side in range(2):
            col = pl.multiple_of(pos[side * n + i] * BLK, BLK)
            cols[i].append(col)
            half = pl.ds(side * BLK, BLK)
            a = pltpu.make_async_copy(acts.at[:, pl.ds(col, BLK)], av.at[i, :, half], asem.at[i, side, 0])
            e = pltpu.make_async_copy(
                err.at[pl.ds(row0, count), pl.ds(col, BLK)], ev.at[i, :, half], asem.at[i, side, 1]
            )
            a.start()
            e.start()
            ins[i] += [a, e]
    kcp.wait()
    kct[...] = kcv[...].T

    def product(i):
        for copy in ins[i]:
            copy.wait()
        gv[i % 2] = jnp.dot(kct[...], av[i], preferred_element_type=F32)

    outs = []
    product(0)
    for i in range(n):
        if i + 1 < n:
            product(i + 1)
        g = gv[i % 2]
        for k, out in enumerate((kv, sv)):
            s = slice(k * BLK, (k + 1) * BLK)
            v = g[:, s] + ev[i, :, s].astype(F32)
            q = squash(v)
            out[i] = q
            ev[i, :, s] = (v - q.astype(F32)).astype(BF)
        pairs = [(sv.at[i], send.at[i]), (kv.at[i], keep.at[i])]
        for side in range(2):
            half = pl.ds(side * BLK, BLK)
            pairs.append((ev.at[i, :, half], newerr.at[pl.ds(row0, count), pl.ds(cols[i][side], BLK)]))
        for k, (src, dst) in enumerate(pairs):
            copy = pltpu.make_async_copy(src, dst, osem.at[i, k])
            copy.start()
            outs.append(copy)
    for copy in outs:
        copy.wait()


def grad_part(pos, kc, acts, err, newerr, rows, limit):
    n = 8
    count = rows[1]
    in_hbm = pl.BlockSpec(memory_space=pltpu.HBM)
    free = pl.BlockSpec(memory_space=pl.ANY)
    half = jax.ShapeDtypeStruct((n, count, BLK), BF)
    operands, aliases = (pos, kc, acts, err), {}
    body = functools.partial(grad_kernel, rows=rows)
    if newerr is not None:
        operands, aliases = operands + (newerr,), {4: 0}
        body = lambda *refs: grad_kernel(*refs[:4], *refs[5:], rows=rows)
    return pl.pallas_call(
        body,
        in_specs=[pl.BlockSpec(memory_space=pltpu.SMEM)] + [in_hbm] * (len(operands) - 1),
        out_specs=[in_hbm, free, free],
        out_shape=[jax.ShapeDtypeStruct((512, 4096), BF), half, half],
        scratch_shapes=[
            pltpu.VMEM((512, count), BF),
            pltpu.VMEM((count, 512), BF),
            pltpu.VMEM((n, 512, 256), BF),
            pltpu.VMEM((n, count, 256), BF),
            pltpu.VMEM((n, count, BLK), BF),
            pltpu.VMEM((n, count, BLK), BF),
            pltpu.VMEM((2, count, 256), F32),
            pltpu.SemaphoreType.DMA,
            pltpu.SemaphoreType.DMA((n, 2, 2)),
            pltpu.SemaphoreType.DMA((n, 4)),
        ],
        input_output_aliases=aliases,
        compiler_params=pltpu.CompilerParams(vmem_limit_bytes=limit * MIB),
        cost_estimate=pl.CostEstimate(
            flops=2 * count * 512 * 256 * n, bytes_accessed=n * MIB, transcendentals=0
        ),
    )(*operands)


def add(*terms):
    total = terms[0].astype(F32)
    for term in terms[1:]:
        total = total + term.astype(F32)
    return total


def columns():
    zh, y, core = (lax.axis_index(a) for a in ("zh", "y", "core"))

    def blocks(which_y, c):
        z1, z2 = partner(0, zh, c), partner(1, zh, c)
        zs = (zh, z2, z1, lax.bitwise_xor(zh, 2))
        y1, y2 = partner(0, y, c), partner(1, y, c)
        ys = (y1, lax.bitwise_xor(y, 2)) if which_y == 0 else (y, y2)
        return [(z * 4 + t) * 2 + c for t in ys for z in zs]

    return [
        jnp.stack(blocks(part, core) + blocks(part, 1 - core)).astype(jnp.int32) for part in range(2)
    ]


def y_step(x, which):
    return lax.ppermute(x, ("y", "core"), ring_pairs(which, (4, 2), 0, 1))


def z_step(x, which):
    pairs = []
    for s, d in ring_pairs(which, (4, 2), 0, 1):
        for y in range(4):
            pairs.append(((s // 2 * 4 + y) * 2 + s % 2, (d // 2 * 4 + y) * 2 + d % 2))
    return lax.ppermute(x, ("zh", "y", "core"), pairs)


def x_step(x, which):
    pairs = []
    for s, d in ring_pairs(which, (2, 4), 1, 0):
        for zl in range(2):
            pairs.append(((s // 4 * 2 + zl) * 4 + s % 4, (d // 4 * 2 + zl) * 4 + d % 4))
    return lax.ppermute(x, ("core", "zl", "x"), pairs)


def swap(x, axis):
    return lax.ppermute(x, axis, [(0, 1), (1, 0)])


def body(acts, key_cotangent, error_rows, error_cols):
    first, second = columns()
    err = error_rows[0, 0]
    newerr = None
    averaged, new_cols = [], []
    for rows in CHUNKS:
        newerr, send, keep = grad_part(first, key_cotangent, acts, err, newerr, rows, 60)
        ahead = add(keep, swap(send, "core")).astype(BF)
        second, ahead = lax.optimization_barrier((second, ahead))
        got_1 = y_step(ahead, 0)
        newerr, send, keep = grad_part(second, key_cotangent, acts, err, newerr, rows, 57)
        swapped = swap(send, "core")
        mine = add(keep, swapped, got_1)
        got_2 = y_step(mine[4:].astype(BF), 1)
        mine = add(mine[:4], got_2)
        got_3 = z_step(mine[2:].astype(BF), 0)
        mine = add(mine[:2], got_3)
        got_4 = z_step(mine[1].astype(BF), 1)
        summed = add(mine[0], got_4)

        carried_two = summed * (1.0 / 32.0) + error_cols[0, rows[0] : rows[0] + rows[1]]
        sent_two = lax.optimization_barrier(squash(carried_two))
        new_cols.append(carried_two - sent_two.astype(F32))
        total = add(sent_two, swap(sent_two, "zl"))
        for which in range(2):
            total = add(total, x_step(total.astype(BF), which))
        averaged.append((total * 0.125).astype(BF))
    return jnp.concatenate(averaged), newerr[None, None], jnp.concatenate(new_cols)[None]


def solution(mesh):
    fine = Mesh(mesh.devices.reshape(4, 4, 2, 2, 4), ("zh", "y", "core", "zl", "x"))
    row, col = ("zh", "y", "core"), ("zl", "x")
    in_specs = (
        P(row + col, None),
        P(row + col, None),
        P(row, col, None, None),
        P(col, None, row),
    )
    out_specs = (P(None, row), P(row, col, None, None), P(col, None, row))
    return jax.shard_map(body, mesh=fine, in_specs=in_specs, out_specs=out_specs, check_vma=False)
```

time: 95 us -> 80.6 us (0.85)
  waiting for transfers between devices: 44.4 us -> 35.9 us
  local copies, waits for them, and re-layouts: 6.57 us -> 1.3 us
  starting transfers between devices: 21.9 us -> 20.1 us
  other arithmetic: 2.79 us -> 4.55 us
  Pallas kernels: 17.6 us -> 16.5 us
    all_to_all x1 -> x0, waiting for transfers between devices: 13.2 us -> none  [body(): parts = lax.all_to_all(copies, ('zl', 'x'), 0, 0, tiled=True)]
    all_to_all x1 -> x0, starting transfers between devices: 6.51 us -> none  [body(): parts = lax.all_to_all(copies, ('zl', 'x'), 0, 0, tiled=True)]
    unnamed x8 -> x2, local copies, waits for them, and re-layouts: 5.42 us -> 0.01 us
    ppermute x9, waiting for transfers between devices: 31.2 us -> 35.9 us  [the longest x2 10.9 us: y_step(): return lax.ppermute(x, ('y', 'core'), ring_pairs(which, (4, 2), 0, 1))]
    ppermute x9, starting transfers between devices: 15.4 us -> 20.1 us  [the longest x2 8.81 us: z_step(): return lax.ppermute(x, ('zh', 'y', 'core'), pairs)]
    add x1 -> x3, other arithmetic: 0.24 us -> 1.76 us  [add(): total = total + term.astype(F32)]
    another operation x0 -> x2, local copies, waits for them, and re-layouts: none -> 1.17 us  [columns(): jnp.stack(blocks(part, core) + blocks(part, 1 - core)).astype(jnp.int32)]
    broadcast_in_dim x1 -> x0, local copies, waits for them, and re-layouts: 1.11 us -> none  [body(): copies = jnp.broadcast_to(sent_two[None], (8, 512, BLK))]
  transfers between devices with their start and end apart: 10 -> 9, of which waited for: 6 -> 8; matrix products, arithmetic and copies ran while one was open for 1% -> 1% of each run, Pallas kernels for 9% -> 10%
where the time goes in v2:
time: 80.6 us; the launch traced here: 79.3 us
  waiting for transfers between devices  35.9 us (45%)
  starting transfers between devices  20.1 us (25%)
  Pallas kernels  16.5 us (20%)
  other arithmetic  4.55 us (6%)
  local copies, waits for them, and re-layouts  1.3 us (2%)
  between operations  0.84 us (1%)
    pallas_call x2, Pallas kernels, grad_part(): pl.pallas_call(body, in_specs=[pl.BlockSpec(memory_space=pltpu.SMEM)] + [...  16.5 us
    ppermute x2, waiting for transfers between devices, y_step(): return lax.ppermute(x, ('y', 'core'), ring_pairs(which, (4, 2), 0, 1))  10.9 us
    ppermute x2, waiting for transfers between devices, z_step(): return lax.ppermute(x, ('zh', 'y', 'core'), pairs)  10.8 us
    ppermute x2, starting transfers between devices, z_step(): return lax.ppermute(x, ('zh', 'y', 'core'), pairs)  8.81 us
    ppermute x2, waiting for transfers between devices, x_step(): return lax.ppermute(x, ('core', 'zl', 'x'), pairs)  7.55 us
    ppermute x3, waiting for transfers between devices, swap(): return lax.ppermute(x, axis, [(0, 1), (1, 0)])  6.65 us
    ppermute x2, starting transfers between devices, y_step(): return lax.ppermute(x, ('y', 'core'), ring_pairs(which, (4, 2), 0, 1))  4.77 us
    ppermute x2, starting transfers between devices, x_step(): return lax.ppermute(x, ('core', 'zl', 'x'), pairs)  4.42 us
  transfers between devices with their start and end apart: 9, of which 8 were waited for; matrix products, arithmetic and copies ran while one was open for 1% of the time, Pallas kernels for 10%

profile of v2, /device:TPU:32, one launch (start us, length us, event | category | flops | bytes accessed | tf_op | source)
XLA Modules:
  0.0 79.3 jit_solution(4280841959116877644)
XLA Ops:
  0.7 0.6 stack.135.pos
  1.3 8.3 %shard_map.67 = (bf16[512,4096]{1,0:T(8,128)(2,1)}, bf16[8,512,128]{2,1,0:T(8,128)(2,1)}, bf16[8,512,128]{2,1,0:T(8,128)(2,1)}) custom-call(s32[16]{0:T(128)} %stack.135.pos, bf16[512,512]{1,0:T(8,128)(2,1)} %refs_1_.1, bf16[512,4096]{1,0:T(8,128)(2,1)} %refs_2_.1, bf16[512,4096]{1,0:T(8,128)(2,1)} %bitcast.50), custom_call_target="tpu_custom_call" | custom-call | flops 1073741824 | bytes 8388608 | tf_op jit(solution)/shard_map/pallas_call | solution.py:109
  9.7 0.6 stack.118.refs_0_
  10.3 2.2 %collective-permute-done = bf16[8,512,128]{2,1,0:T(8,128)(2,1)S(1)} collective-permute-done((bf16[8,512,128]{2,1,0:T(8,128)(2,1)}, bf16[8,512,128]{2,1,0:T(8,128)(2,1)S(1)}, u32[]{:S(2)}, u32[]{:S(2)}) %collective-permute-start) | collective-permute-done | bytes 1048608 | tf_op jit(solution)/shard_map/ppermute | solution.py:177
  12.5 1.5 %add_convert_fusion = bf16[8,512,128]{2,1,0:T(8,128)(2,1)S(1)} fusion(bf16[8,512,128]{2,1,0:T(8,128)(2,1)S(1)} %collective-permute-done, bf16[8,512,128]{2,1,0:T(8,128)(2,1)} %get-tuple-element.11), kind=kLoop, calls=%fused_computation.1 | loop fusion | flops 2097152 | bytes 3145728 | tf_op jit(solution)/shard_map/convert_element_type | solution.py:187
  14.0 1.7 %collective-permute-start.2 = (bf16[8,512,128]{2,1,0:T(8,128)(2,1)S(1)}, bf16[8,512,128]{2,1,0:T(8,128)(2,1)S(1)}, u32[]{:S(2)}, u32[]{:S(2)}) collective-permute-start(bf16[8,512,128]{2,1,0:T(8,128)(2,1)S(1)} %add_convert_fusion), channel_id=1, source_target_pairs={{0,16},{8,56},{16,0},{24,40},{32,48},{40,24},{48,32},{56,8},{1,17}... | collective-permute-start | bytes 3145736 | tf_op jit(solution)/shard_map/ppermute | solution.py:157
  15.7 8.3 %shard_map.68 = (bf16[512,4096]{1,0:T(8,128)(2,1)}, bf16[8,512,128]{2,1,0:T(8,128)(2,1)}, bf16[8,512,128]{2,1,0:T(8,128)(2,1)}) custom-call(s32[16]{0:T(128)} %stack.118.refs_0_, bf16[512,512]{1,0:T(8,128)(2,1)} %refs_1_.1, bf16[512,4096]{1,0:T(8,128)(2,1)} %refs_2_.1, bf16[512,4096]{1,0:T(8,128)(2,1)} %bitcast.51, ...), custom_call_target="tpu_custom_call", output_to_operand_aliasing={{0}: (4, {})} | custom-call | flops 1073741824 | bytes 8388608 | tf_op jit(solution)/shard_map/pallas_call | solution.py:109
  23.9 1.4 %collective-permute-start.1 = (bf16[8,512,128]{2,1,0:T(8,128)(2,1)}, bf16[8,512,128]{2,1,0:T(8,128)(2,1)S(1)}, u32[]{:S(2)}, u32[]{:S(2)}) collective-permute-start(bf16[8,512,128]{2,1,0:T(8,128)(2,1)} %get-tuple-element.16), channel_id=1, source_target_pairs={{0,8},{8,0},{1,9},{9,1},{2,10},{10,2},{3,11},{11,3},{4,12},{12,4},... | collective-permute-start | bytes 3145736 | tf_op jit(solution)/shard_map/ppermute | solution.py:177
  25.3 3.6 %collective-permute-done.2 = bf16[8,512,128]{2,1,0:T(8,128)(2,1)S(1)} collective-permute-done((bf16[8,512,128]{2,1,0:T(8,128)(2,1)S(1)}, bf16[8,512,128]{2,1,0:T(8,128)(2,1)S(1)}, u32[]{:S(2)}, u32[]{:S(2)}) %collective-permute-start.2) | collective-permute-done | bytes 1048608 | tf_op jit(solution)/shard_map/ppermute | solution.py:157
  28.9 1.6 %convert_add_fusion = f32[8,512,128]{2,1,0:T(8,128)S(1)} fusion(bf16[8,512,128]{2,1,0:T(8,128)(2,1)S(1)} %collective-permute-done.2, bf16[8,512,128]{2,1,0:T(8,128)(2,1)S(1)} %collective-permute-done.1, bf16[8,512,128]{2,1,0:T(8,128)(2,1)} %get-tuple-element.15), kind=kLoop, calls=%fused_computation | loop fusion | flops 2621440 | bytes 5242880 | tf_op jit(solution)/shard_map/add | solution.py:137
  30.6 3.1 %collective-permute-start.3 = (bf16[4,512,128]{2,1,0:T(8,128)(2,1)S(1)}, bf16[4,512,128]{2,1,0:T(8,128)(2,1)S(1)}, u32[]{:S(2)}, u32[]{:S(2)}) collective-permute-start(bf16[4,512,128]{2,1,0:T(8,128)(2,1)S(1)} %slice.47), channel_id=1, source_target_pairs={{0,48},{8,24},{16,32},{24,8},{32,16},{40,56},{48,0},{56,40},{1,49}... | collective-permute-start | bytes 1572872 | tf_op jit(solution)/shard_map/ppermute | solution.py:157
  33.7 7.4 %collective-permute-done.3 = bf16[4,512,128]{2,1,0:T(8,128)(2,1)S(1)} collective-permute-done((bf16[4,512,128]{2,1,0:T(8,128)(2,1)S(1)}, bf16[4,512,128]{2,1,0:T(8,128)(2,1)S(1)}, u32[]{:S(2)}, u32[]{:S(2)}) %collective-permute-start.3) | collective-permute-done | bytes 524320 | tf_op jit(solution)/shard_map/ppermute | solution.py:157
  41.2 3.4 %collective-permute-start.4 = (bf16[2,512,128]{2,1,0:T(8,128)(2,1)S(1)}, bf16[2,512,128]{2,1,0:T(8,128)(2,1)S(1)}, u32[]{:S(2)}, u32[]{:S(2)}) collective-permute-start(bf16[2,512,128]{2,1,0:T(8,128)(2,1)S(1)} %slice.48), channel_id=1, source_target_pairs={{0,64},{16,80},{32,96},{48,112},{8,200},{24,216},{40,232},{56,248}... | collective-permute-start | bytes 786440 | tf_op jit(solution)/shard_map/ppermute | solution.py:165
  44.6 6.3 %collective-permute-done.4 = bf16[2,512,128]{2,1,0:T(8,128)(2,1)S(1)} collective-permute-done((bf16[2,512,128]{2,1,0:T(8,128)(2,1)S(1)}, bf16[2,512,128]{2,1,0:T(8,128)(2,1)S(1)}, u32[]{:S(2)}, u32[]{:S(2)}) %collective-permute-start.4) | collective-permute-done | bytes 262176 | tf_op jit(solution)/shard_map/ppermute | solution.py:165
  51.0 5.5 %collective-permute-start.5 = (bf16[512,128]{1,0:T(8,128)(2,1)S(1)}, bf16[512,128]{1,0:T(8,128)(2,1)S(1)}, u32[]{:S(2)}, u32[]{:S(2)}) collective-permute-start(bf16[512,128]{1,0:T(8,128)(2,1)S(1)} %fusion.6), channel_id=1, source_target_pairs={{0,192},{16,208},{32,224},{48,240},{8,72},{24,88},{40,104},{56,120... | collective-permute-start | bytes 393224 | tf_op jit(solution)/shard_map/ppermute | solution.py:165
  56.4 4.5 %collective-permute-done.5 = bf16[512,128]{1,0:T(8,128)(2,1)S(1)} collective-permute-done((bf16[512,128]{1,0:T(8,128)(2,1)S(1)}, bf16[512,128]{1,0:T(8,128)(2,1)S(1)}, u32[]{:S(2)}, u32[]{:S(2)}) %collective-permute-start.5) | collective-permute-done | bytes 131104 | tf_op jit(solution)/shard_map/ppermute | solution.py:165
  61.1 0.2 multiply_convert_fusion.1
  61.3 0.6 collective-permute-start.6
  61.9 4.4 %collective-permute-done.6 = bf16[512,128]{1,0:T(8,128)(2,1)S(1)} collective-permute-done((bf16[512,128]{1,0:T(8,128)(2,1)S(1)}, bf16[512,128]{1,0:T(8,128)(2,1)S(1)}, u32[]{:S(2)}, u32[]{:S(2)}) %collective-permute-start.6) | collective-permute-done | bytes 131104 | tf_op jit(solution)/shard_map/ppermute | solution.py:177
  66.4 1.6 %collective-permute-start.7 = (bf16[512,128]{1,0:T(8,128)(2,1)S(1)}, bf16[512,128]{1,0:T(8,128)(2,1)S(1)}, u32[]{:S(2)}, u32[]{:S(2)}) collective-permute-start(bf16[512,128]{1,0:T(8,128)(2,1)S(1)} %fusion.4), channel_id=1, source_target_pairs={{0,1},{4,5},{8,11},{12,15},{1,0},{5,4},{9,10},{13,14},{2,3},{6,7},... | collective-permute-start | bytes 393224 | tf_op jit(solution)/shard_map/ppermute | solution.py:173
  68.0 4.1 %collective-permute-done.7 = bf16[512,128]{1,0:T(8,128)(2,1)S(1)} collective-permute-done((bf16[512,128]{1,0:T(8,128)(2,1)S(1)}, bf16[512,128]{1,0:T(8,128)(2,1)S(1)}, u32[]{:S(2)}, u32[]{:S(2)}) %collective-permute-start.7) | collective-permute-done | bytes 131104 | tf_op jit(solution)/shard_map/ppermute | solution.py:173
  72.2 2.8 %collective-permute-start.8 = (bf16[512,128]{1,0:T(8,128)(2,1)S(1)}, bf16[512,128]{1,0:T(8,128)(2,1)S(1)}, u32[]{:S(2)}, u32[]{:S(2)}) collective-permute-start(bf16[512,128]{1,0:T(8,128)(2,1)S(1)} %fusion.5), channel_id=1, source_target_pairs={{0,3},{4,7},{8,9},{12,13},{1,2},{5,6},{9,8},{13,12},{2,1},{6,5},{1... | collective-permute-start | bytes 393224 | tf_op jit(solution)/shard_map/ppermute | solution.py:173
  75.0 3.4 %collective-permute-done.8 = bf16[512,128]{1,0:T(8,128)(2,1)S(1)} collective-permute-done((bf16[512,128]{1,0:T(8,128)(2,1)S(1)}, bf16[512,128]{1,0:T(8,128)(2,1)S(1)}, u32[]{:S(2)}, u32[]{:S(2)}) %collective-permute-start.8) | collective-permute-done | bytes 131104 | tf_op jit(solution)/shard_map/ppermute | solution.py:173
  78.4 0.8 %fusion = (f32[1,512,128]{2,1,0:T(8,128)}, bf16[512,128]{1,0:T(8,128)(2,1)}) fusion(f32[512,128]{1,0:T(8,128)S(1)} %get-tuple-element.20, bf16[512,128]{1,0:T(8,128)(2,1)S(1)} %multiply_convert_fusion.1, bf16[512,128]{1,0:T(8,128)(2,1)S(1)} %collective-permute-done.8, bf16[512,128]{1,0:T(8,128)(2,1)S(1)} %collective-permute-done.7, ...), kind=kLoop, calls=%fused_computation.8 | loop fusion | flops 655360 | bytes 1179648 | tf_op jit(solution)/shard_map/broadcast_in_dim | solution.py:207
  (13 shorter events, 0.7 us)
Async XLA Ops:
  9.6 3.0 %collective-permute-start = (bf16[8,512,128]{2,1,0:T(8,128)(2,1)}, bf16[8,512,128]{2,1,0:T(8,128)(2,1)S(1)}, u32[]{:S(2)}, u32[]{:S(2)}) collective-permute-start(bf16[8,512,128]{2,1,0:T(8,128)(2,1)} %get-tuple-element.12), channel_id=1, source_target_pairs={{0,8},{8,0},{1,9},{9,1},{2,10},{10,2},{3,11},{11,3},{4,12},{12,4},... | collective-permute-start | bytes 3145736 | tf_op jit(solution)/shard_map/ppermute | solution.py:177
  14.0 14.9 %collective-permute-start.2 = (bf16[8,512,128]{2,1,0:T(8,128)(2,1)S(1)}, bf16[8,512,128]{2,1,0:T(8,128)(2,1)S(1)}, u32[]{:S(2)}, u32[]{:S(2)}) collective-permute-start(bf16[8,512,128]{2,1,0:T(8,128)(2,1)S(1)} %add_convert_fusion), channel_id=1, source_target_pairs={{0,16},{8,56},{16,0},{24,40},{32,48},{40,24},{48,32},{56,8},{1,17}... | collective-permute-start | bytes 3145736 | tf_op jit(solution)/shard_map/ppermute | solution.py:157
  23.9 5.0 %collective-permute-start.1 = (bf16[8,512,128]{2,1,0:T(8,128)(2,1)}, bf16[8,512,128]{2,1,0:T(8,128)(2,1)S(1)}, u32[]{:S(2)}, u32[]{:S(2)}) collective-permute-start(bf16[8,512,128]{2,1,0:T(8,128)(2,1)} %get-tuple-element.16), channel_id=1, source_target_pairs={{0,8},{8,0},{1,9},{9,1},{2,10},{10,2},{3,11},{11,3},{4,12},{12,4},... | collective-permute-start | bytes 3145736 | tf_op jit(solution)/shard_map/ppermute | solution.py:177
  30.5 30.4 %copy-start = (f32[1,512,128]{2,1,0:T(8,128)S(1)}, f32[1,512,128]{2,1,0:T(8,128)}, u32[]{:S(2)}) copy-start(f32[1,512,128]{2,1,0:T(8,128)} %param.7) | copy-start | bytes 786436
  30.6 10.5 %collective-permute-start.3 = (bf16[4,512,128]{2,1,0:T(8,128)(2,1)S(1)}, bf16[4,512,128]{2,1,0:T(8,128)(2,1)S(1)}, u32[]{:S(2)}, u32[]{:S(2)}) collective-permute-start(bf16[4,512,128]{2,1,0:T(8,128)(2,1)S(1)} %slice.47), channel_id=1, source_target_pairs={{0,48},{8,24},{16,32},{24,8},{32,16},{40,56},{48,0},{56,40},{1,49}... | collective-permute-start | bytes 1572872 | tf_op jit(solution)/shard_map/ppermute | solution.py:157
  41.2 9.7 %collective-permute-start.4 = (bf16[2,512,128]{2,1,0:T(8,128)(2,1)S(1)}, bf16[2,512,128]{2,1,0:T(8,128)(2,1)S(1)}, u32[]{:S(2)}, u32[]{:S(2)}) collective-permute-start(bf16[2,512,128]{2,1,0:T(8,128)(2,1)S(1)} %slice.48), channel_id=1, source_target_pairs={{0,64},{16,80},{32,96},{48,112},{8,200},{24,216},{40,232},{56,248}... | collective-permute-start | bytes 786440 | tf_op jit(solution)/shard_map/ppermute | solution.py:165
  51.0 9.9 %collective-permute-start.5 = (bf16[512,128]{1,0:T(8,128)(2,1)S(1)}, bf16[512,128]{1,0:T(8,128)(2,1)S(1)}, u32[]{:S(2)}, u32[]{:S(2)}) collective-permute-start(bf16[512,128]{1,0:T(8,128)(2,1)S(1)} %fusion.6), channel_id=1, source_target_pairs={{0,192},{16,208},{32,224},{48,240},{8,72},{24,88},{40,104},{56,120... | collective-permute-start | bytes 393224 | tf_op jit(solution)/shard_map/ppermute | solution.py:165
  61.3 5.1 %collective-permute-start.6 = (bf16[512,128]{1,0:T(8,128)(2,1)S(1)}, bf16[512,128]{1,0:T(8,128)(2,1)S(1)}, u32[]{:S(2)}, u32[]{:S(2)}) collective-permute-start(bf16[512,128]{1,0:T(8,128)(2,1)S(1)} %multiply_convert_fusion.1), channel_id=1, source_target_pairs={{0,4},{4,0},{1,5},{5,1},{2,6},{6,2},{3,7},{7,3},{8,12},{12,8},{9,1... | collective-permute-start | bytes 393224 | tf_op jit(solution)/shard_map/ppermute | solution.py:177
  66.4 5.7 %collective-permute-start.7 = (bf16[512,128]{1,0:T(8,128)(2,1)S(1)}, bf16[512,128]{1,0:T(8,128)(2,1)S(1)}, u32[]{:S(2)}, u32[]{:S(2)}) collective-permute-start(bf16[512,128]{1,0:T(8,128)(2,1)S(1)} %fusion.4), channel_id=1, source_target_pairs={{0,1},{4,5},{8,11},{12,15},{1,0},{5,4},{9,10},{13,14},{2,3},{6,7},... | collective-permute-start | bytes 393224 | tf_op jit(solution)/shard_map/ppermute | solution.py:173
  72.2 6.3 %collective-permute-start.8 = (bf16[512,128]{1,0:T(8,128)(2,1)S(1)}, bf16[512,128]{1,0:T(8,128)(2,1)S(1)}, u32[]{:S(2)}, u32[]{:S(2)}) collective-permute-start(bf16[512,128]{1,0:T(8,128)(2,1)S(1)} %fusion.5), channel_id=1, source_target_pairs={{0,3},{4,7},{8,9},{12,13},{1,2},{5,6},{9,8},{13,12},{2,1},{6,5},{1... | collective-permute-start | bytes 393224 | tf_op jit(solution)/shard_map/ppermute | solution.py:173

commit v3 on v1

v3 whole, which is shorter than its diff:
```python
import functools

import jax
import jax.numpy as jnp
from jax import lax
from jax.experimental import pallas as pl
from jax.experimental.pallas import tpu as pltpu
from jax.sharding import Mesh
from jax.sharding import PartitionSpec as P

BLK = 128
BF = jnp.bfloat16
F32 = jnp.float32
MIB = 2**20
CHUNKS = 2
DEPTH = 4


def partner(which, i, core):
    flip = lax.bitwise_xor(i, 1)
    turn = 3 - i
    return jnp.where(core == which, flip, turn)


def ring_pairs(which, shape, ring, core):
    def linear(pos):
        out = 0
        for p, n in zip(pos, shape):
            out = out * n + p
        return out

    pairs = []
    for r in range(4):
        for c in range(2):
            src, dst = [0, 0], [0, 0]
            src[ring], src[core] = r, c
            dst[ring], dst[core] = (r ^ 1 if c == which else 3 - r), c
            pairs.append((linear(src), linear(dst)))
    return pairs


def squash(v):
    m = jnp.sum(jnp.abs(v), axis=1, keepdims=True) * (1.0 / BLK) + 1e-6
    return (m * jnp.tanh(v * (1.0 / m))).astype(BF)


def grad_kernel(pos, kc, acts, err, newerr, send, keep, kcv, kct, av, ev, gv, ksem, asem, osem, *, part):
    n = 8
    zh, y, core = pos[0], pos[1], pos[2]
    other = 1 - core
    zs = (zh, partner(1, zh, core), partner(0, zh, core), lax.bitwise_xor(zh, 2))
    swapped = (0, 2, 1, 3)
    y1, y2 = partner(0, y, core), partner(1, y, core)
    if part == 0:
        whole, split, base = lax.bitwise_xor(y, 2), (y1, y2), (4, 0)
    else:
        whole, split, base = y, (y2, y1), (0, 4)
    items = [([(z * 4 + whole) * 256], base[0] + k, base[0] + swapped[k]) for k, z in enumerate(zs)]
    for k, z in enumerate(zs):
        left = ((z * 4 + split[0]) * 2 + core) * BLK
        right = ((z * 4 + split[1]) * 2 + other) * BLK
        items.append(([left, right], base[1] + k, base[1] + swapped[k]))

    def windows(i):
        starts = items[i][0]
        width = 256 // len(starts)
        for k, start in enumerate(starts):
            yield k, pl.ds(pl.multiple_of(start, width), width), pl.ds(k * width, width)

    def loads(i):
        for k, col, half in windows(i):
            yield pltpu.make_async_copy(acts.at[:, col], av.at[i, :, half], asem.at[i, k, 0])
            yield pltpu.make_async_copy(err.at[:, col], ev.at[i, :, half], asem.at[i, k, 1])

    def stores(i):
        for k, col, half in windows(i):
            yield pltpu.make_async_copy(ev.at[i, :, half], newerr.at[:, col], osem.at[i, k])

    def product(i):
        for copy in loads(i):
            copy.wait()
        gv[i % 2] = jnp.dot(kct[...], av[i], preferred_element_type=F32)

    load_kc = pltpu.make_async_copy(kc, kcv, ksem)
    load_kc.start()
    for i in range(DEPTH):
        for copy in loads(i):
            copy.start()
    load_kc.wait()
    kct[...] = kcv[...].T
    product(0)
    for i in range(n):
        if i + DEPTH < n:
            for copy in loads(i + DEPTH):
                copy.start()
        if i + 1 < n:
            product(i + 1)
        q = []
        for k in range(2):
            s = slice(k * BLK, (k + 1) * BLK)
            v = gv[i % 2, :, s] + ev[i, :, s].astype(F32)
            q.append(squash(v))
            ev[i, :, s] = (v - q[k].astype(F32)).astype(BF)
        starts, kept, sent = items[i]
        if len(starts) == 1:
            q = [jnp.where(core == 0, q[0], q[1]), jnp.where(core == 0, q[1], q[0])]
        keep[kept] = q[0]
        send[sent] = q[1]
        for copy in stores(i):
            copy.start()
    for i in range(n):
        for copy in stores(i):
            copy.wait()


def grad_part(pos, kc, acts, err, newerr, part):
    n = 8
    free = pl.BlockSpec(memory_space=pl.ANY)
    near = pl.BlockSpec(memory_space=pltpu.VMEM)
    operands, aliases = (kc, acts, err), {}
    body = functools.partial(grad_kernel, part=part)
    if newerr is not None:
        operands, aliases = operands + (newerr,), {4: 0}
        body = lambda *refs: grad_kernel(*refs[:4], *refs[5:], part=part)
    operands = [pltpu.with_memory_space_constraint(o, pltpu.HBM) for o in operands]
    half = pltpu.VMEM((n, 512, BLK), BF)
    return pl.pallas_call(
        body,
        in_specs=[pl.BlockSpec(memory_space=pltpu.SMEM)] + [free] * len(operands),
        out_specs=[free, near, near],
        out_shape=[pltpu.HBM((512, 4096), BF), half, half],
        scratch_shapes=[
            pltpu.VMEM((512, 512), BF),
            pltpu.VMEM((512, 512), BF),
            pltpu.VMEM((n, 512, 256), BF),
            pltpu.VMEM((n, 512, 256), BF),
            pltpu.VMEM((2, 512, 256), F32),
            pltpu.SemaphoreType.DMA,
            pltpu.SemaphoreType.DMA((n, 2, 2)),
            pltpu.SemaphoreType.DMA((n, 2)),
        ],
        input_output_aliases=aliases,
        compiler_params=pltpu.CompilerParams(vmem_limit_bytes=24 * MIB),
        cost_estimate=pl.CostEstimate(
            flops=2 * 512 * 512 * 256 * n, bytes_accessed=n * MIB, transcendentals=0
        ),
    )(pos, *operands)


def add(*terms):
    total = terms[0].astype(F32)
    for term in terms[1:]:
        total = total + term.astype(F32)
    return total


def y_step(x, which):
    return lax.ppermute(x, ("y", "core"), ring_pairs(which, (4, 2), 0, 1))


def z_step(x, which):
    pairs = []
    for s, d in ring_pairs(which, (4, 2), 0, 1):
        for y in range(4):
            pairs.append(((s // 2 * 4 + y) * 2 + s % 2, (d // 2 * 4 + y) * 2 + d % 2))
    return lax.ppermute(x, ("zh", "y", "core"), pairs)


def swap(x, axis):
    return lax.ppermute(x, axis, [(0, 1), (1, 0)])


def body(acts, key_cotangent, error_rows, error_cols):
    pos = jnp.stack([lax.axis_index(a) for a in ("zh", "y", "core")]).astype(jnp.int32)
    err = error_rows[0, 0]
    parts = [slice(r, r + 512 // CHUNKS) for r in range(0, 512, 512 // CHUNKS)]
    newerr, send, keep = grad_part(pos, key_cotangent, acts, err, None, 0)
    swapped = swap(send, "core")
    ahead = add(keep, swapped).astype(BF)
    pos, ahead = lax.optimization_barrier((pos, ahead))
    got = y_step(ahead, 0)
    newerr, send, keep = grad_part(pos, key_cotangent, acts, err, newerr, 1)
    swapped = swap(send, "core")
    mine = [add(keep[:, p], swapped[:, p], got[:, p]) for p in parts]
    got = [y_step(m[4:].astype(BF), 1) for m in mine]
    mine = [add(m[:4], g) for m, g in zip(mine, got)]
    got = [z_step(m[2:].astype(BF), 0) for m in mine]
    mine = [add(m[:2], g) for m, g in zip(mine, got)]
    got = [z_step(m[1].astype(BF), 1) for m in mine]
    summed = jnp.concatenate([add(m[0], g) for m, g in zip(mine, got)])

    carried_two = summed * (1.0 / 32.0) + error_cols[0]
    sent_two = lax.optimization_barrier(squash(carried_two))
    new_cols = carried_two - sent_two.astype(F32)
    total = add(sent_two, swap(sent_two, "zl"))
    near = [
        lax.ppermute(total.astype(BF), "x", [(i, (i + d) % 4) for i in range(4)]) for d in (1, 3, 2)
    ]
    averaged = (add(total, *near) * 0.125).astype(BF)
    return averaged, newerr[None, None], new_cols[None]


def solution(mesh):
    fine = Mesh(mesh.devices.reshape(4, 4, 2, 2, 4), ("zh", "y", "core", "zl", "x"))
    row, col = ("zh", "y", "core"), ("zl", "x")
    in_specs = (
        P(row + col, None),
        P(row + col, None),
        P(row, col, None, None),
        P(col, None, row),
    )
    out_specs = (P(None, row), P(row, col, None, None), P(col, None, row))
    return jax.shard_map(body, mesh=fine, in_specs=in_specs, out_specs=out_specs, check_vma=False)
```

time: 95 us -> 72.4 us (0.76)
  waiting for transfers between devices: 44.4 us -> 25.4 us
  starting transfers between devices: 21.9 us -> 29.7 us
  local copies, waits for them, and re-layouts: 6.57 us -> 0.14 us
  Pallas kernels: 17.6 us -> 14.1 us
    ppermute x9 -> x13, starting transfers between devices: 15.4 us -> 29.7 us  [the longest x4 17.9 us: z_step(): return lax.ppermute(x, ('zh', 'y', 'core'), pairs)]
    all_to_all x1 -> x0, waiting for transfers between devices: 13.2 us -> none  [body(): parts = lax.all_to_all(copies, ('zl', 'x'), 0, 0, tiled=True)]
    all_to_all x1 -> x0, starting transfers between devices: 6.51 us -> none  [body(): parts = lax.all_to_all(copies, ('zl', 'x'), 0, 0, tiled=True)]
    ppermute x9 -> x13, waiting for transfers between devices: 31.2 us -> 25.4 us  [the longest x3 9 us: y_step(): return lax.ppermute(x, ('y', 'core'), ring_pairs(which, (4, 2), 0, 1))]
    unnamed x8 -> x2, local copies, waits for them, and re-layouts: 5.42 us -> 0.01 us
    pallas_call x2, Pallas kernels: 17.6 us -> 14.1 us  [grad_part(): pl.pallas_call(body, in_specs=[pl.BlockSpec(memory_space=pltpu.SMEM)] + [...]
    broadcast_in_dim x1 -> x0, local copies, waits for them, and re-layouts: 1.11 us -> none  [body(): copies = jnp.broadcast_to(sent_two[None], (8, 512, BLK))]
  transfers between devices with their start and end apart: 10 -> 13, of which waited for: 6 -> 9; matrix products, arithmetic and copies ran while one was open for 1% -> 0% of each run, Pallas kernels for 9% -> 10%
where the time goes in v3:
time: 72.4 us; the launch traced here: 72.3 us
  starting transfers between devices  29.7 us (41%)
  waiting for transfers between devices  25.4 us (35%)
  Pallas kernels  14.1 us (19%)
  other arithmetic  2.22 us (3%)
  between operations  0.78 us (1%)
    ppermute x4, starting transfers between devices, z_step(): return lax.ppermute(x, ('zh', 'y', 'core'), pairs)  17.9 us
    pallas_call x2, Pallas kernels, grad_part(): pl.pallas_call(body, in_specs=[pl.BlockSpec(memory_space=pltpu.SMEM)] + [...  14.1 us
    ppermute x3, waiting for transfers between devices, y_step(): return lax.ppermute(x, ('y', 'core'), ring_pairs(which, (4, 2), 0, 1))  9 us
    ppermute x3, waiting for transfers between devices, swap(): return lax.ppermute(x, axis, [(0, 1), (1, 0)])  7.6 us
    ppermute x3, waiting for transfers between devices, body(): lax.ppermute(total.astype(BF), 'x', [(i, (i + d) % 4) for i in range(4)])  5.3 us
    ppermute x3, starting transfers between devices, body(): lax.ppermute(total.astype(BF), 'x', [(i, (i + d) % 4) for i in range(4)])  5.14 us
    ppermute x3, starting transfers between devices, y_step(): return lax.ppermute(x, ('y', 'core'), ring_pairs(which, (4, 2), 0, 1))  5.07 us
    ppermute x4, waiting for transfers between devices, z_step(): return lax.ppermute(x, ('zh', 'y', 'core'), pairs)  3.49 us
  transfers between devices with their start and end apart: 13, of which 9 were waited for; matrix products, arithmetic and copies ran while one was open for 0% of the time, Pallas kernels for 10%

profile of v3, /device:TPU:32, one launch (start us, length us, event | category | flops | bytes accessed | tf_op | source)
XLA Modules:
  0.0 72.3 jit_solution(957001464383772828)
XLA Ops:
  0.7 7.0 %shard_map.67 = (bf16[512,4096]{1,0:T(8,128)(2,1)}, bf16[8,512,128]{2,1,0:T(8,128)(2,1)S(1)}, bf16[8,512,128]{2,1,0:T(8,128)(2,1)S(1)}) custom-call(s32[3]{0:T(128)S(1)} %pad_add_fusion.pos.refs_0_, bf16[512,512]{1,0:T(8,128)(2,1)} %refs_1_.1, bf16[512,4096]{1,0:T(8,128)(2,1)} %refs_2_.1, bf16[512,4096]{1,0:T(8,128)(2,1)} %bitcast.27), custom_call_target="tpu_custom_call" | custom-call | flops 1073741824 | bytes 8388608 | tf_op jit(solution)/shard_map/pallas_call | solution.py:127
  7.9 2.6 %collective-permute-done = bf16[8,512,128]{2,1,0:T(8,128)(2,1)S(1)} collective-permute-done((bf16[8,512,128]{2,1,0:T(8,128)(2,1)S(1)}, bf16[8,512,128]{2,1,0:T(8,128)(2,1)S(1)}, u32[]{:S(2)}, u32[]{:S(2)}) %collective-permute-start) | collective-permute-done | bytes 1048608 | tf_op jit(solution)/shard_map/ppermute | solution.py:170
  10.8 1.7 %collective-permute-start.2 = (bf16[8,512,128]{2,1,0:T(8,128)(2,1)S(1)}, bf16[8,512,128]{2,1,0:T(8,128)(2,1)S(1)}, u32[]{:S(2)}, u32[]{:S(2)}) collective-permute-start(bf16[8,512,128]{2,1,0:T(8,128)(2,1)S(1)} %add_convert_fusion), channel_id=1, source_target_pairs={{0,16},{8,56},{16,0},{24,40},{32,48},{40,24},{48,32},{56,8},{1,17}... | collective-permute-start | bytes 3145736 | tf_op jit(solution)/shard_map/ppermute | solution.py:158
  12.5 7.0 %shard_map.68 = (bf16[512,4096]{1,0:T(8,128)(2,1)}, bf16[8,512,128]{2,1,0:T(8,128)(2,1)S(1)}, bf16[8,512,128]{2,1,0:T(8,128)(2,1)S(1)}) custom-call(s32[3]{0:T(128)S(1)} %pad_add_fusion.pos.refs_0_, bf16[512,512]{1,0:T(8,128)(2,1)} %refs_1_.1, bf16[512,4096]{1,0:T(8,128)(2,1)} %refs_2_.1, ...), custom_call_target="tpu_custom_call", output_to_operand_aliasing={{0}: (4, {})} | custom-call | flops 1073741824 | bytes 8388608 | tf_op jit(solution)/shard_map/pallas_call | solution.py:127
  19.5 1.4 %collective-permute-start.1 = (bf16[8,512,128]{2,1,0:T(8,128)(2,1)S(1)}, bf16[8,512,128]{2,1,0:T(8,128)(2,1)S(1)}, u32[]{:S(2)}, u32[]{:S(2)}) collective-permute-start(bf16[8,512,128]{2,1,0:T(8,128)(2,1)S(1)} %get-tuple-element.16), channel_id=1, source_target_pairs={{0,8},{8,0},{1,9},{9,1},{2,10},{10,2},{3,11},{11,3},{4,12},{12,4},... | collective-permute-start | bytes 3145736 | tf_op jit(solution)/shard_map/ppermute | solution.py:170
  20.9 4.8 %collective-permute-done.2 = bf16[8,512,128]{2,1,0:T(8,128)(2,1)S(1)} collective-permute-done((bf16[8,512,128]{2,1,0:T(8,128)(2,1)S(1)}, bf16[8,512,128]{2,1,0:T(8,128)(2,1)S(1)}, u32[]{:S(2)}, u32[]{:S(2)}) %collective-permute-start.2) | collective-permute-done | bytes 1048608 | tf_op jit(solution)/shard_map/ppermute | solution.py:158
  25.7 0.4 convert_add_fusion.1
  26.2 3.1 %collective-permute-start.6 = (bf16[4,256,128]{2,1,0:T(8,128)(2,1)S(1)}, bf16[4,256,128]{2,1,0:T(8,128)(2,1)S(1)}, u32[]{:S(2)}, u32[]{:S(2)}) collective-permute-start(bf16[4,256,128]{2,1,0:T(8,128)(2,1)S(1)} %slice.120), channel_id=1, source_target_pairs={{0,48},{8,24},{16,32},{24,8},{32,16},{40,56},{48,0},{56,40},{1,49}... | collective-permute-start | bytes 786440 | tf_op jit(solution)/shard_map/ppermute | solution.py:158
  29.3 0.3 collective-permute-start.3
  29.6 4.2 %collective-permute-done.6 = bf16[4,256,128]{2,1,0:T(8,128)(2,1)S(1)} collective-permute-done((bf16[4,256,128]{2,1,0:T(8,128)(2,1)S(1)}, bf16[4,256,128]{2,1,0:T(8,128)(2,1)S(1)}, u32[]{:S(2)}, u32[]{:S(2)}) %collective-permute-start.6) | collective-permute-done | bytes 262176 | tf_op jit(solution)/shard_map/ppermute | solution.py:158
  33.9 3.4 %collective-permute-start.7 = (bf16[2,256,128]{2,1,0:T(8,128)(2,1)S(1)}, bf16[2,256,128]{2,1,0:T(8,128)(2,1)S(1)}, u32[]{:S(2)}, u32[]{:S(2)}) collective-permute-start(bf16[2,256,128]{2,1,0:T(8,128)(2,1)S(1)} %slice.122), channel_id=1, source_target_pairs={{0,64},{16,80},{32,96},{48,112},{8,200},{24,216},{40,232},{56,248}... | collective-permute-start | bytes 393224 | tf_op jit(solution)/shard_map/ppermute | solution.py:166
  37.4 3.0 %collective-permute-start.4 = (bf16[2,256,128]{2,1,0:T(8,128)(2,1)S(1)}, bf16[2,256,128]{2,1,0:T(8,128)(2,1)S(1)}, u32[]{:S(2)}, u32[]{:S(2)}) collective-permute-start(bf16[2,256,128]{2,1,0:T(8,128)(2,1)S(1)} %slice.123), channel_id=1, source_target_pairs={{0,64},{16,80},{32,96},{48,112},{8,200},{24,216},{40,232},{56,248}... | collective-permute-start | bytes 393224 | tf_op jit(solution)/shard_map/ppermute | solution.py:166
  40.4 0.7 collective-permute-done.7
  41.2 5.3 %collective-permute-start.8 = (bf16[256,128]{1,0:T(8,128)(2,1)S(1)}, bf16[256,128]{1,0:T(8,128)(2,1)S(1)}, u32[]{:S(2)}, u32[]{:S(2)}) collective-permute-start(bf16[256,128]{1,0:T(8,128)(2,1)S(1)} %fusion.6), channel_id=1, source_target_pairs={{0,192},{16,208},{32,224},{48,240},{8,72},{24,88},{40,104},{56,120... | collective-permute-start | bytes 196616 | tf_op jit(solution)/shard_map/ppermute | solution.py:166
  46.6 6.1 %collective-permute-start.5 = (bf16[256,128]{1,0:T(8,128)(2,1)S(1)}, bf16[256,128]{1,0:T(8,128)(2,1)S(1)}, u32[]{:S(2)}, u32[]{:S(2)}) collective-permute-start(bf16[256,128]{1,0:T(8,128)(2,1)S(1)} %fusion.5), channel_id=1, source_target_pairs={{0,192},{16,208},{32,224},{48,240},{8,72},{24,88},{40,104},{56,120... | collective-permute-start | bytes 196616 | tf_op jit(solution)/shard_map/ppermute | solution.py:166
  52.7 2.8 %collective-permute-done.5 = bf16[256,128]{1,0:T(8,128)(2,1)S(1)} collective-permute-done((bf16[256,128]{1,0:T(8,128)(2,1)S(1)}, bf16[256,128]{1,0:T(8,128)(2,1)S(1)}, u32[]{:S(2)}, u32[]{:S(2)}) %collective-permute-start.5) | collective-permute-done | bytes 65568 | tf_op jit(solution)/shard_map/ppermute | solution.py:166
  56.0 5.0 %collective-permute-done.9 = bf16[512,128]{1,0:T(8,128)(2,1)S(1)} collective-permute-done((bf16[512,128]{1,0:T(8,128)(2,1)S(1)}, bf16[512,128]{1,0:T(8,128)(2,1)S(1)}, u32[]{:S(2)}, u32[]{:S(2)}) %collective-permute-start.9) | collective-permute-done | bytes 131104 | tf_op jit(solution)/shard_map/ppermute | solution.py:170
  61.0 3.1 %collective-permute-start.12 = (bf16[512,128]{1,0:T(8,128)(2,1)S(1)}, bf16[512,128]{1,0:T(8,128)(2,1)S(1)}, u32[]{:S(2)}, u32[]{:S(2)}) collective-permute-start(bf16[512,128]{1,0:T(8,128)(2,1)S(1)} %fusion.2), channel_id=1, source_target_pairs={{0,2},{1,3},{2,0},{3,1},{4,6},{5,7},{6,4},{7,5},{8,10},{9,11},{10,... | collective-permute-start | bytes 393224 | tf_op jit(solution)/shard_map/ppermute | solution.py:197
  64.1 1.1 %collective-permute-start.11 = (bf16[512,128]{1,0:T(8,128)(2,1)S(1)}, bf16[512,128]{1,0:T(8,128)(2,1)S(1)}, u32[]{:S(2)}, u32[]{:S(2)}) collective-permute-start(bf16[512,128]{1,0:T(8,128)(2,1)S(1)} %fusion.2), channel_id=1, source_target_pairs={{0,3},{1,0},{2,1},{3,2},{4,7},{5,4},{6,5},{7,6},{8,11},{9,8},{10,9... | collective-permute-start | bytes 393224 | tf_op jit(solution)/shard_map/ppermute | solution.py:197
  65.2 0.9 %collective-permute-start.10 = (bf16[512,128]{1,0:T(8,128)(2,1)S(1)}, bf16[512,128]{1,0:T(8,128)(2,1)S(1)}, u32[]{:S(2)}, u32[]{:S(2)}) collective-permute-start(bf16[512,128]{1,0:T(8,128)(2,1)S(1)} %fusion.2), channel_id=1, source_target_pairs={{0,1},{1,2},{2,3},{3,0},{4,5},{5,6},{6,7},{7,4},{8,9},{9,10},{10,1... | collective-permute-start | bytes 393224 | tf_op jit(solution)/shard_map/ppermute | solution.py:197
  66.1 1.4 %collective-permute-done.12 = bf16[512,128]{1,0:T(8,128)(2,1)S(1)} collective-permute-done((bf16[512,128]{1,0:T(8,128)(2,1)S(1)}, bf16[512,128]{1,0:T(8,128)(2,1)S(1)}, u32[]{:S(2)}, u32[]{:S(2)}) %collective-permute-start.12) | collective-permute-done | bytes 131104 | tf_op jit(solution)/shard_map/ppermute | solution.py:197
  67.5 1.5 %collective-permute-done.11 = bf16[512,128]{1,0:T(8,128)(2,1)S(1)} collective-permute-done((bf16[512,128]{1,0:T(8,128)(2,1)S(1)}, bf16[512,128]{1,0:T(8,128)(2,1)S(1)}, u32[]{:S(2)}, u32[]{:S(2)}) %collective-permute-start.11) | collective-permute-done | bytes 131104 | tf_op jit(solution)/shard_map/ppermute | solution.py:197
  69.1 2.4 %collective-permute-done.10 = bf16[512,128]{1,0:T(8,128)(2,1)S(1)} collective-permute-done((bf16[512,128]{1,0:T(8,128)(2,1)S(1)}, bf16[512,128]{1,0:T(8,128)(2,1)S(1)}, u32[]{:S(2)}, u32[]{:S(2)}) %collective-permute-start.10) | collective-permute-done | bytes 131104 | tf_op jit(solution)/shard_map/ppermute | solution.py:197
  71.4 0.9 %fusion = (f32[1,512,128]{2,1,0:T(8,128)}, bf16[512,128]{1,0:T(8,128)(2,1)}) fusion(bf16[512,128]{1,0:T(8,128)(2,1)S(1)} %multiply_convert_fusion.1, f32[1,512,128]{2,1,0:T(8,128)S(1)} %copy-done, f32[256,128]{1,0:T(8,128)S(1)} %fusion.3, f32[256,128]{1,0:T(8,128)S(1)} %fusion.4, bf16[512,128]{1,0:T(8,128)(2,1)S(1)} %collective-permute-done.12, ...), kind=kLoop, calls=%fused_computation.9 | loop fusion | flops 983040 | bytes 1572864 | tf_op jit(solution)/shard_map/broadcast_in_dim | solution.py:200
  (26 shorter events, 1.3 us)
Async XLA Ops:
  7.8 2.7 %collective-permute-start = (bf16[8,512,128]{2,1,0:T(8,128)(2,1)S(1)}, bf16[8,512,128]{2,1,0:T(8,128)(2,1)S(1)}, u32[]{:S(2)}, u32[]{:S(2)}) collective-permute-start(bf16[8,512,128]{2,1,0:T(8,128)(2,1)S(1)} %get-tuple-element.12), channel_id=1, source_target_pairs={{0,8},{8,0},{1,9},{9,1},{2,10},{10,2},{3,11},{11,3},{4,12},{12,4},... | collective-permute-start | bytes 3145736 | tf_op jit(solution)/shard_map/ppermute | solution.py:170
  10.8 14.9 %collective-permute-start.2 = (bf16[8,512,128]{2,1,0:T(8,128)(2,1)S(1)}, bf16[8,512,128]{2,1,0:T(8,128)(2,1)S(1)}, u32[]{:S(2)}, u32[]{:S(2)}) collective-permute-start(bf16[8,512,128]{2,1,0:T(8,128)(2,1)S(1)} %add_convert_fusion), channel_id=1, source_target_pairs={{0,16},{8,56},{16,0},{24,40},{32,48},{40,24},{48,32},{56,8},{1,17}... | collective-permute-start | bytes 3145736 | tf_op jit(solution)/shard_map/ppermute | solution.py:158
  19.5 6.2 %collective-permute-start.1 = (bf16[8,512,128]{2,1,0:T(8,128)(2,1)S(1)}, bf16[8,512,128]{2,1,0:T(8,128)(2,1)S(1)}, u32[]{:S(2)}, u32[]{:S(2)}) collective-permute-start(bf16[8,512,128]{2,1,0:T(8,128)(2,1)S(1)} %get-tuple-element.16), channel_id=1, source_target_pairs={{0,8},{8,0},{1,9},{9,1},{2,10},{10,2},{3,11},{11,3},{4,12},{12,4},... | collective-permute-start | bytes 3145736 | tf_op jit(solution)/shard_map/ppermute | solution.py:170
  26.1 29.4 %copy-start = (f32[1,512,128]{2,1,0:T(8,128)S(1)}, f32[1,512,128]{2,1,0:T(8,128)}, u32[]{:S(2)}) copy-start(f32[1,512,128]{2,1,0:T(8,128)} %param.7) | copy-start | bytes 786436
  26.2 7.7 %collective-permute-start.6 = (bf16[4,256,128]{2,1,0:T(8,128)(2,1)S(1)}, bf16[4,256,128]{2,1,0:T(8,128)(2,1)S(1)}, u32[]{:S(2)}, u32[]{:S(2)}) collective-permute-start(bf16[4,256,128]{2,1,0:T(8,128)(2,1)S(1)} %slice.120), channel_id=1, source_target_pairs={{0,48},{8,24},{16,32},{24,8},{32,16},{40,56},{48,0},{56,40},{1,49}... | collective-permute-start | bytes 786440 | tf_op jit(solution)/shard_map/ppermute | solution.py:158
  29.3 8.0 %collective-permute-start.3 = (bf16[4,256,128]{2,1,0:T(8,128)(2,1)S(1)}, bf16[4,256,128]{2,1,0:T(8,128)(2,1)S(1)}, u32[]{:S(2)}, u32[]{:S(2)}) collective-permute-start(bf16[4,256,128]{2,1,0:T(8,128)(2,1)S(1)} %slice.121), channel_id=1, source_target_pairs={{0,48},{8,24},{16,32},{24,8},{32,16},{40,56},{48,0},{56,40},{1,49}... | collective-permute-start | bytes 786440 | tf_op jit(solution)/shard_map/ppermute | solution.py:158
  33.9 7.2 %collective-permute-start.7 = (bf16[2,256,128]{2,1,0:T(8,128)(2,1)S(1)}, bf16[2,256,128]{2,1,0:T(8,128)(2,1)S(1)}, u32[]{:S(2)}, u32[]{:S(2)}) collective-permute-start(bf16[2,256,128]{2,1,0:T(8,128)(2,1)S(1)} %slice.122), channel_id=1, source_target_pairs={{0,64},{16,80},{32,96},{48,112},{8,200},{24,216},{40,232},{56,248}... | collective-permute-start | bytes 393224 | tf_op jit(solution)/shard_map/ppermute | solution.py:166
  37.4 9.2 %collective-permute-start.4 = (bf16[2,256,128]{2,1,0:T(8,128)(2,1)S(1)}, bf16[2,256,128]{2,1,0:T(8,128)(2,1)S(1)}, u32[]{:S(2)}, u32[]{:S(2)}) collective-permute-start(bf16[2,256,128]{2,1,0:T(8,128)(2,1)S(1)} %slice.123), channel_id=1, source_target_pairs={{0,64},{16,80},{32,96},{48,112},{8,200},{24,216},{40,232},{56,248}... | collective-permute-start | bytes 393224 | tf_op jit(solution)/shard_map/ppermute | solution.py:166
  41.2 11.5 %collective-permute-start.8 = (bf16[256,128]{1,0:T(8,128)(2,1)S(1)}, bf16[256,128]{1,0:T(8,128)(2,1)S(1)}, u32[]{:S(2)}, u32[]{:S(2)}) collective-permute-start(bf16[256,128]{1,0:T(8,128)(2,1)S(1)} %fusion.6), channel_id=1, source_target_pairs={{0,192},{16,208},{32,224},{48,240},{8,72},{24,88},{40,104},{56,120... | collective-permute-start | bytes 196616 | tf_op jit(solution)/shard_map/ppermute | solution.py:166
  46.6 8.9 %collective-permute-start.5 = (bf16[256,128]{1,0:T(8,128)(2,1)S(1)}, bf16[256,128]{1,0:T(8,128)(2,1)S(1)}, u32[]{:S(2)}, u32[]{:S(2)}) collective-permute-start(bf16[256,128]{1,0:T(8,128)(2,1)S(1)} %fusion.5), channel_id=1, source_target_pairs={{0,192},{16,208},{32,224},{48,240},{8,72},{24,88},{40,104},{56,120... | collective-permute-start | bytes 196616 | tf_op jit(solution)/shard_map/ppermute | solution.py:166
  55.9 5.1 %collective-permute-start.9 = (bf16[512,128]{1,0:T(8,128)(2,1)S(1)}, bf16[512,128]{1,0:T(8,128)(2,1)S(1)}, u32[]{:S(2)}, u32[]{:S(2)}) collective-permute-start(bf16[512,128]{1,0:T(8,128)(2,1)S(1)} %multiply_convert_fusion.1), channel_id=1, source_target_pairs={{0,4},{4,0},{1,5},{5,1},{2,6},{6,2},{3,7},{7,3},{8,12},{12,8},{9,1... | collective-permute-start | bytes 393224 | tf_op jit(solution)/shard_map/ppermute | solution.py:170
  61.0 6.6 %collective-permute-start.12 = (bf16[512,128]{1,0:T(8,128)(2,1)S(1)}, bf16[512,128]{1,0:T(8,128)(2,1)S(1)}, u32[]{:S(2)}, u32[]{:S(2)}) collective-permute-start(bf16[512,128]{1,0:T(8,128)(2,1)S(1)} %fusion.2), channel_id=1, source_target_pairs={{0,2},{1,3},{2,0},{3,1},{4,6},{5,7},{6,4},{7,5},{8,10},{9,11},{10,... | collective-permute-start | bytes 393224 | tf_op jit(solution)/shard_map/ppermute | solution.py:197
  64.1 5.0 %collective-permute-start.11 = (bf16[512,128]{1,0:T(8,128)(2,1)S(1)}, bf16[512,128]{1,0:T(8,128)(2,1)S(1)}, u32[]{:S(2)}, u32[]{:S(2)}) collective-permute-start(bf16[512,128]{1,0:T(8,128)(2,1)S(1)} %fusion.2), channel_id=1, source_target_pairs={{0,3},{1,0},{2,1},{3,2},{4,7},{5,4},{6,5},{7,6},{8,11},{9,8},{10,9... | collective-permute-start | bytes 393224 | tf_op jit(solution)/shard_map/ppermute | solution.py:197
  65.2 6.2 %collective-permute-start.10 = (bf16[512,128]{1,0:T(8,128)(2,1)S(1)}, bf16[512,128]{1,0:T(8,128)(2,1)S(1)}, u32[]{:S(2)}, u32[]{:S(2)}) collective-permute-start(bf16[512,128]{1,0:T(8,128)(2,1)S(1)} %fusion.2), channel_id=1, source_target_pairs={{0,1},{1,2},{2,3},{3,0},{4,5},{5,6},{6,7},{7,4},{8,9},{9,10},{10,1... | collective-permute-start | bytes 393224 | tf_op jit(solution)/shard_map/ppermute | solution.py:197

commit v4 on v3

v4 whole, which is shorter than its diff:
```python
import functools

import jax
import jax.numpy as jnp
from jax import lax
from jax.experimental import pallas as pl
from jax.experimental.pallas import tpu as pltpu
from jax.sharding import Mesh
from jax.sharding import PartitionSpec as P

BLK = 128
BF = jnp.bfloat16
F32 = jnp.float32
MIB = 2**20
CHUNKS = 2
DEPTH = 4
PARTS = (
    tuple(("far", i) for i in range(4)),
    tuple(("one", i) for i in range(4)) + tuple(("two", i) for i in range(4)),
    tuple(("own", i) for i in range(4)),
)
SEND_SLOT = ((0, 2, 1, 3), (0, 2, 1, 3, 4, 6, 5, 7), (0, 2, 1, 3))


def partner(which, i, core):
    flip = lax.bitwise_xor(i, 1)
    turn = 3 - i
    return jnp.where(core == which, flip, turn)


def ring_pairs(which, shape, ring, core):
    def linear(pos):
        out = 0
        for p, n in zip(pos, shape):
            out = out * n + p
        return out

    pairs = []
    for r in range(4):
        for c in range(2):
            src, dst = [0, 0], [0, 0]
            src[ring], src[core] = r, c
            dst[ring], dst[core] = (r ^ 1 if c == which else 3 - r), c
            pairs.append((linear(src), linear(dst)))
    return pairs


def squash(v):
    m = jnp.sum(jnp.abs(v), axis=1, keepdims=True) * (1.0 / BLK) + 1e-6
    return (m * jnp.tanh(v * (1.0 / m))).astype(BF)


def items_of(pos, kind):
    zh, y, core = pos[0], pos[1], pos[2]
    other = 1 - core
    zs = (zh, partner(1, zh, core), partner(0, zh, core), lax.bitwise_xor(zh, 2))
    y1, y2 = partner(0, y, core), partner(1, y, core)
    if kind in ("far", "own"):
        whole = y if kind == "own" else lax.bitwise_xor(y, 2)
        return [[(z * 4 + whole) * 256] for z in zs]
    left, right = (y1, y2) if kind == "one" else (y2, y1)
    return [[((z * 4 + left) * 2 + core) * BLK, ((z * 4 + right) * 2 + other) * BLK] for z in zs]


def windows(starts):
    width = 256 // len(starts)
    for k, start in enumerate(starts):
        yield k, pl.ds(pl.multiple_of(start, width), width), pl.ds(k * width, width)


def grad_kernel(pos, kc, acts, err, *refs, part):
    if part == 0:
        send, keep, ev, kct, kcv, av, gv, asem, ksem = refs
    else:
        send, keep, ev, av, gv, asem = refs
        kct = kc
    core = pos[2]
    kinds = {kind: items_of(pos, kind) for kind, _ in PARTS[part]}
    items = [kinds[kind][i] for kind, i in PARTS[part]]
    n = len(items)

    def loads(i):
        for k, col, half in windows(items[i]):
            yield pltpu.make_async_copy(acts.at[:, col], av.at[i, :, half], asem.at[i, k, 0])
            yield pltpu.make_async_copy(err.at[:, col], ev.at[i, :, half], asem.at[i, k, 1])

    if part == 0:
        load_kc = pltpu.make_async_copy(kc, kcv, ksem)
        load_kc.start()
    for i in range(DEPTH):
        for copy in loads(i):
            copy.start()
    if part == 0:
        load_kc.wait()
        kct[...] = kcv[...].T
    for copy in loads(0):
        copy.wait()
    gv[0] = jnp.dot(kct[...], av[0], preferred_element_type=F32)
    for i in range(n):
        if i + DEPTH < n:
            for copy in loads(i + DEPTH):
                copy.start()
        if i + 1 < n:
            for copy in loads(i + 1):
                copy.wait()
        for r in range(0, 512, 256):
            rows = slice(r, r + 256)
            if i + 1 < n:
                gv[(i + 1) % 2, rows] = jnp.dot(kct[rows], av[i + 1], preferred_element_type=F32)
            q = []
            for k in range(2):
                s = slice(k * BLK, (k + 1) * BLK)
                v = gv[i % 2, rows, s] + ev[i, rows, s].astype(F32)
                q.append(squash(v))
                ev[i, rows, s] = (v - q[k].astype(F32)).astype(BF)
            if len(items[i]) == 1:
                q = [jnp.where(core == 0, q[0], q[1]), jnp.where(core == 0, q[1], q[0])]
            keep[i, rows] = q[0]
            send[SEND_SLOT[part][i], rows] = q[1]


def grad_part(pos, kc, acts, err, part):
    n = len(PARTS[part])
    in_hbm = pl.BlockSpec(memory_space=pl.ANY)
    near = pl.BlockSpec(memory_space=pltpu.VMEM)
    in_smem = pl.BlockSpec(memory_space=pltpu.SMEM)
    pin = lambda o: pltpu.with_memory_space_constraint(o, pltpu.HBM)
    half = pltpu.VMEM((n, 512, BLK), BF)
    outs = [half, half, pltpu.VMEM((n, 512, 256), BF)]
    scratch = [
        pltpu.VMEM((n, 512, 256), BF),
        pltpu.VMEM((2, 512, 256), F32),
        pltpu.SemaphoreType.DMA((n, 2, 2)),
    ]
    if part == 0:
        outs.append(pltpu.VMEM((512, 512), BF))
        scratch = [pltpu.VMEM((512, 512), BF), *scratch, pltpu.SemaphoreType.DMA]
    return pl.pallas_call(
        functools.partial(grad_kernel, part=part),
        in_specs=[in_smem, in_hbm if part == 0 else near, in_hbm, in_hbm],
        out_specs=[near] * len(outs),
        out_shape=outs,
        scratch_shapes=scratch,
        compiler_params=pltpu.CompilerParams(vmem_limit_bytes=24 * MIB),
        cost_estimate=pl.CostEstimate(
            flops=10**6, bytes_accessed=10**4, transcendentals=0
        ),
    )(pos, pin(kc) if part == 0 else kc, pin(acts), pin(err))


def store_kernel(pos, *refs):
    blocks, (newerr, sem) = refs[: len(PARTS)], refs[len(PARTS) :]
    copies = []
    for part, members in enumerate(PARTS):
        for i, (kind, item) in enumerate(members):
            for k, col, half in windows(items_of(pos, kind)[item]):
                copies.append(
                    pltpu.make_async_copy(
                        blocks[part].at[i, :, half], newerr.at[:, col], sem.at[part, i, k]
                    )
                )
    for copy in copies:
        copy.start()
    for copy in copies:
        copy.wait()


def store_residual(pos, blocks):
    near = pl.BlockSpec(memory_space=pltpu.VMEM)
    return pl.pallas_call(
        store_kernel,
        in_specs=[pl.BlockSpec(memory_space=pltpu.SMEM)] + [near] * len(PARTS),
        out_specs=pl.BlockSpec(memory_space=pl.ANY),
        out_shape=pltpu.HBM((512, 4096), BF),
        scratch_shapes=[pltpu.SemaphoreType.DMA((len(PARTS), max(map(len, PARTS)), 2))],
        compiler_params=pltpu.CompilerParams(vmem_limit_bytes=24 * MIB),
        cost_estimate=pl.CostEstimate(flops=0, bytes_accessed=8 * MIB, transcendentals=0),
    )(pos, *blocks)


def add(*terms):
    total = terms[0].astype(F32)
    for term in terms[1:]:
        total = total + term.astype(F32)
    return total


def y_step(x, which):
    return lax.ppermute(x, ("y", "core"), ring_pairs(which, (4, 2), 0, 1))


def z_step(x, which):
    pairs = []
    for s, d in ring_pairs(which, (4, 2), 0, 1):
        for y in range(4):
            pairs.append(((s // 2 * 4 + y) * 2 + s % 2, (d // 2 * 4 + y) * 2 + d % 2))
    return lax.ppermute(x, ("zh", "y", "core"), pairs)


def swap(x, axis):
    return lax.ppermute(x, axis, [(0, 1), (1, 0)])


def body(acts, key_cotangent, error_rows, error_cols):
    pos = jnp.stack([lax.axis_index(a) for a in ("zh", "y", "core")]).astype(jnp.int32)
    err = error_rows[0, 0]
    parts = [slice(r, r + 512 // CHUNKS) for r in range(0, 512, 512 // CHUNKS)]
    tie = lax.optimization_barrier
    send, keep, err_0, kct = grad_part(pos, key_cotangent, acts, err, 0)
    ahead = add(keep, swap(send, "core")).astype(BF)
    pos, ahead = tie((pos, ahead))
    got_0 = y_step(ahead, 0)
    send, keep, err_1 = grad_part(pos, kct, acts, err, 1)
    near = [swap(send[k : k + 2], "core") for k in range(0, 8, 2)]
    one, two = jnp.concatenate(near[: 2]), near[2 :]
    ahead = add(keep[:4], one).astype(BF)
    ahead, two = tie((ahead, two))
    got_1 = y_step(ahead, 0)
    ahead = add(keep[4:], jnp.concatenate(two), got_0).astype(BF)
    pos, ahead = tie((pos, ahead))
    got_2 = y_step(ahead, 1)
    send, keep, err_2 = grad_part(pos, kct, acts, err, 2)
    got = tie(add(got_1, got_2))
    swapped = swap(send, "core")
    mine = [add(keep[:, p], swapped[:, p], got[:, p]) for p in parts]
    pos, *mine = tie((pos, *mine))
    newerr = store_residual(pos, (err_0, err_1, err_2))
    got = [z_step(m[2:].astype(BF), 0) for m in mine]
    mine = [add(m[:2], g) for m, g in zip(mine, got)]
    got = [z_step(m[1].astype(BF), 1) for m in mine]
    summed = jnp.concatenate([add(m[0], g) for m, g in zip(mine, got)])

    carried_two = summed * (1.0 / 32.0) + error_cols[0]
    sent_two = lax.optimization_barrier(squash(carried_two))
    new_cols = carried_two - sent_two.astype(F32)
    total = add(sent_two, swap(sent_two, "zl"))
    near = [
        lax.ppermute(total.astype(BF), "x", [(i, (i + d) % 4) for i in range(4)]) for d in (1, 3, 2)
    ]
    averaged = (add(total, *near) * 0.125).astype(BF)
    return averaged, newerr[None, None], new_cols[None]


def solution(mesh):
    fine = Mesh(mesh.devices.reshape(4, 4, 2, 2, 4), ("zh", "y", "core", "zl", "x"))
    row, col = ("zh", "y", "core"), ("zl", "x")
    in_specs = (
        P(row + col, None),
        P(row + col, None),
        P(row, col, None, None),
        P(col, None, row),
    )
    out_specs = (P(None, row), P(row, col, None, None), P(col, None, row))
    return jax.shard_map(body, mesh=fine, in_specs=in_specs, out_specs=out_specs, check_vma=False)
```

time: 72.4 us -> 69.1 us (0.954)
  starting transfers between devices: 29.7 us -> 24.3 us
  Pallas kernels: 14.1 us -> 16 us
    ppermute x4, starting transfers between devices: 17.9 us -> 10.9 us  [z_step(): return lax.ppermute(x, ('zh', 'y', 'core'), pairs)]
    ppermute x4, waiting for transfers between devices: 3.49 us -> 7.58 us  [z_step(): return lax.ppermute(x, ('zh', 'y', 'core'), pairs)]
    ppermute x3, waiting for transfers between devices: 5.3 us -> 2.29 us  [body(): lax.ppermute(total.astype(BF), 'x', [(i, (i + d) % 4) for i in range(4)])]
    ppermute x3 -> x7, starting transfers between devices: 1.57 us -> 4.03 us  [swap(): return lax.ppermute(x, axis, [(0, 1), (1, 0)])]
    pallas_call x2 -> x4, Pallas kernels: 14.1 us -> 16 us  [the longest x3 13.1 us: grad_part(): pl.pallas_call(functools.partial(grad_kernel, part=part), in_specs=[in_sm...]
    ppermute x3 -> x7, waiting for transfers between devices: 7.6 us -> 6.8 us  [swap(): return lax.ppermute(x, axis, [(0, 1), (1, 0)])]
    ppermute x3, starting transfers between devices: 5.07 us -> 4.29 us  [y_step(): return lax.ppermute(x, ('y', 'core'), ring_pairs(which, (4, 2), 0, 1))]
  transfers between devices with their start and end apart: 13 -> 17, of which waited for: 9 -> 11; matrix products, arithmetic and copies ran while one was open for 0% -> 1% of each run, Pallas kernels for 10% -> 17%
where the time goes in v4:
time: 69.1 us; the launch traced here: 68.9 us
  waiting for transfers between devices  25.4 us (37%)
  starting transfers between devices  24.3 us (35%)
  Pallas kernels  16 us (23%)
  other arithmetic  2.19 us (3%)
  between operations  0.82 us (1%)
    pallas_call x3, Pallas kernels, grad_part(): pl.pallas_call(functools.partial(grad_kernel, part=part), in_specs=[in_sm...  13.1 us
    ppermute x4, starting transfers between devices, z_step(): return lax.ppermute(x, ('zh', 'y', 'core'), pairs)  10.9 us
    ppermute x3, waiting for transfers between devices, y_step(): return lax.ppermute(x, ('y', 'core'), ring_pairs(which, (4, 2), 0, 1))  8.7 us
    ppermute x4, waiting for transfers between devices, z_step(): return lax.ppermute(x, ('zh', 'y', 'core'), pairs)  7.58 us
    ppermute x7, waiting for transfers between devices, swap(): return lax.ppermute(x, axis, [(0, 1), (1, 0)])  6.8 us
    ppermute x3, starting transfers between devices, body(): lax.ppermute(total.astype(BF), 'x', [(i, (i + d) % 4) for i in range(4)])  5.14 us
    ppermute x3, starting transfers between devices, y_step(): return lax.ppermute(x, ('y', 'core'), ring_pairs(which, (4, 2), 0, 1))  4.29 us
    ppermute x7, starting transfers between devices, swap(): return lax.ppermute(x, axis, [(0, 1), (1, 0)])  4.03 us
  transfers between devices with their start and end apart: 17, of which 11 were waited for; matrix products, arithmetic and copies ran while one was open for 1% of the time, Pallas kernels for 17%

profile of v4, /device:TPU:32, one launch (start us, length us, event | category | flops | bytes accessed | tf_op | source)
XLA Modules:
  0.0 68.9 jit_solution(11726360055022964701)
XLA Ops:
  0.7 4.4 %shard_map.67 = (bf16[4,512,128]{2,1,0:T(8,128)(2,1)S(1)}, bf16[4,512,128]{2,1,0:T(8,128)(2,1)S(1)}, bf16[4,512,256]{2,1,0:T(8,128)(2,1)S(1)}, bf16[512,512]{1,0:T(8,128)(2,1)S(1)}) custom-call(s32[3]{0:T(128)S(1)} %pad_add_fusion.pos, bf16[512,512]{1,0:T(8,128)(2,1)} %kc.1, bf16[512,4096]{1,0:T(8,128)(2,1)} %acts.5, bf16[512,4096]{1,0:T(8,128)(2,1)} %bitcast.27), custom_call_target="tpu_custom_call" | custom-call | flops 1000000 | bytes 10000 | tf_op jit(solution)/shard_map/pallas_call | solution.py:138
  5.2 1.9 %collective-permute-done = bf16[4,512,128]{2,1,0:T(8,128)(2,1)S(1)} collective-permute-done((bf16[4,512,128]{2,1,0:T(8,128)(2,1)S(1)}, bf16[4,512,128]{2,1,0:T(8,128)(2,1)S(1)}, u32[]{:S(2)}, u32[]{:S(2)}) %collective-permute-start) | collective-permute-done | bytes 524320 | tf_op jit(solution)/shard_map/ppermute | solution.py:201
  7.2 1.7 %collective-permute-start.5 = (bf16[4,512,128]{2,1,0:T(8,128)(2,1)S(1)}, bf16[4,512,128]{2,1,0:T(8,128)(2,1)S(1)}, u32[]{:S(2)}, u32[]{:S(2)}) collective-permute-start(bf16[4,512,128]{2,1,0:T(8,128)(2,1)S(1)} %add_convert_fusion.2), channel_id=1, source_target_pairs={{0,16},{8,56},{16,0},{24,40},{32,48},{40,24},{48,32},{56,8},{1,17}... | collective-permute-start | bytes 1572872 | tf_op jit(solution)/shard_map/ppermute | solution.py:189
  8.9 5.1 %shard_map.68 = (bf16[8,512,128]{2,1,0:T(8,128)(2,1)S(1)}, bf16[8,512,128]{2,1,0:T(8,128)(2,1)S(1)}, bf16[8,512,256]{2,1,0:T(8,128)(2,1)S(1)}) custom-call(s32[3]{0:T(128)S(1)} %pad_add_fusion.pos, bf16[512,512]{1,0:T(8,128)(2,1)S(1)} %get-tuple-element.26.kc, bf16[512,4096]{1,0:T(8,128)(2,1)} %acts.5, bf16[512,4096]{1,0:T(8,128)(2,1)} %bitcast.28), custom_call_target="tpu_custom_call" | custom-call | flops 1000000 | bytes 10000 | tf_op jit(solution)/shard_map/pallas_call | solution.py:138
  14.1 1.4 %collective-permute-start.2 = (bf16[2,512,128]{2,1,0:T(8,128)(2,1)S(1)}, bf16[2,512,128]{2,1,0:T(8,128)(2,1)S(1)}, u32[]{:S(2)}, u32[]{:S(2)}) collective-permute-start(bf16[2,512,128]{2,1,0:T(8,128)(2,1)S(1)} %get-tuple-element.47), channel_id=1, source_target_pairs={{0,8},{8,0},{1,9},{9,1},{2,10},{10,2},{3,11},{11,3},{4,12},{12,4},... | collective-permute-start | bytes 786440 | tf_op jit(solution)/shard_map/ppermute | solution.py:201
  15.6 0.4 collective-permute-start.3
  16.1 0.6 collective-permute-done.2
  18.1 2.5 %collective-permute-start.8 = (bf16[4,512,128]{2,1,0:T(8,128)(2,1)S(1)}, bf16[4,512,128]{2,1,0:T(8,128)(2,1)S(1)}, u32[]{:S(2)}, u32[]{:S(2)}) collective-permute-start(bf16[4,512,128]{2,1,0:T(8,128)(2,1)S(1)} %add_convert_fusion), channel_id=1, source_target_pairs={{0,48},{8,24},{16,32},{24,8},{32,16},{40,56},{48,0},{56,40},{1,49}... | collective-permute-start | bytes 1572872 | tf_op jit(solution)/shard_map/ppermute | solution.py:189
  20.6 3.6 %shard_map.69 = (bf16[4,512,128]{2,1,0:T(8,128)(2,1)S(1)}, bf16[4,512,128]{2,1,0:T(8,128)(2,1)S(1)}, bf16[4,512,256]{2,1,0:T(8,128)(2,1)S(1)}) custom-call(s32[3]{0:T(128)S(1)} %pad_add_fusion.pos, bf16[512,512]{1,0:T(8,128)(2,1)S(1)} %get-tuple-element.26.kc, bf16[512,4096]{1,0:T(8,128)(2,1)} %acts.5, bf16[512,4096]{1,0:T(8,128)(2,1)} %bitcast.29), custom_call_target="tpu_custom_call" | custom-call | flops 1000000 | bytes 10000 | tf_op jit(solution)/shard_map/pallas_call | solution.py:138
  24.5 7.7 %collective-permute-done.7 = bf16[4,512,128]{2,1,0:T(8,128)(2,1)S(1)} collective-permute-done((bf16[4,512,128]{2,1,0:T(8,128)(2,1)S(1)}, bf16[4,512,128]{2,1,0:T(8,128)(2,1)S(1)}, u32[]{:S(2)}, u32[]{:S(2)}) %collective-permute-start.7) | collective-permute-done | bytes 524320 | tf_op jit(solution)/shard_map/ppermute | solution.py:189
  32.2 1.0 %collective-permute-done.8 = bf16[4,512,128]{2,1,0:T(8,128)(2,1)S(1)} collective-permute-done((bf16[4,512,128]{2,1,0:T(8,128)(2,1)S(1)}, bf16[4,512,128]{2,1,0:T(8,128)(2,1)S(1)}, u32[]{:S(2)}, u32[]{:S(2)}) %collective-permute-start.8) | collective-permute-done | bytes 524320 | tf_op jit(solution)/shard_map/ppermute | solution.py:189
  33.5 3.4 %collective-permute-start.11 = (bf16[2,256,128]{2,1,0:T(8,128)(2,1)S(1)}, bf16[2,256,128]{2,1,0:T(8,128)(2,1)S(1)}, u32[]{:S(2)}, u32[]{:S(2)}) collective-permute-start(bf16[2,256,128]{2,1,0:T(8,128)(2,1)S(1)} %slice.118), channel_id=1, source_target_pairs={{0,64},{16,80},{32,96},{48,112},{8,200},{24,216},{40,232},{56,248}... | collective-permute-start | bytes 393224 | tf_op jit(solution)/shard_map/ppermute | solution.py:197
  37.0 4.2 %collective-permute-done.11 = bf16[2,256,128]{2,1,0:T(8,128)(2,1)S(1)} collective-permute-done((bf16[2,256,128]{2,1,0:T(8,128)(2,1)S(1)}, bf16[2,256,128]{2,1,0:T(8,128)(2,1)S(1)}, u32[]{:S(2)}, u32[]{:S(2)}) %collective-permute-start.11) | collective-permute-done | bytes 131104 | tf_op jit(solution)/shard_map/ppermute | solution.py:197
  41.2 4.3 %collective-permute-start.12 = (bf16[256,128]{1,0:T(8,128)(2,1)S(1)}, bf16[256,128]{1,0:T(8,128)(2,1)S(1)}, u32[]{:S(2)}, u32[]{:S(2)}) collective-permute-start(bf16[256,128]{1,0:T(8,128)(2,1)S(1)} %fusion.6), channel_id=1, source_target_pairs={{0,192},{16,208},{32,224},{48,240},{8,72},{24,88},{40,104},{56,120... | collective-permute-start | bytes 196616 | tf_op jit(solution)/shard_map/ppermute | solution.py:197
  45.6 3.1 %collective-permute-start.10 = (bf16[256,128]{1,0:T(8,128)(2,1)S(1)}, bf16[256,128]{1,0:T(8,128)(2,1)S(1)}, u32[]{:S(2)}, u32[]{:S(2)}) collective-permute-start(bf16[256,128]{1,0:T(8,128)(2,1)S(1)} %fusion.5), channel_id=1, source_target_pairs={{0,192},{16,208},{32,224},{48,240},{8,72},{24,88},{40,104},{56,120... | collective-permute-start | bytes 196616 | tf_op jit(solution)/shard_map/ppermute | solution.py:197
  48.7 3.4 %collective-permute-done.10 = bf16[256,128]{1,0:T(8,128)(2,1)S(1)} collective-permute-done((bf16[256,128]{1,0:T(8,128)(2,1)S(1)}, bf16[256,128]{1,0:T(8,128)(2,1)S(1)}, u32[]{:S(2)}, u32[]{:S(2)}) %collective-permute-start.10) | collective-permute-done | bytes 65568 | tf_op jit(solution)/shard_map/ppermute | solution.py:197
  52.5 1.7 %collective-permute-start.13 = (bf16[512,128]{1,0:T(8,128)(2,1)S(1)}, bf16[512,128]{1,0:T(8,128)(2,1)S(1)}, u32[]{:S(2)}, u32[]{:S(2)}) collective-permute-start(bf16[512,128]{1,0:T(8,128)(2,1)S(1)} %multiply_convert_fusion.1), channel_id=1, source_target_pairs={{0,4},{4,0},{1,5},{5,1},{2,6},{6,2},{3,7},{7,3},{8,12},{12,8},{9,1... | collective-permute-start | bytes 393224 | tf_op jit(solution)/shard_map/ppermute | solution.py:201
  54.2 3.4 %collective-permute-done.13 = bf16[512,128]{1,0:T(8,128)(2,1)S(1)} collective-permute-done((bf16[512,128]{1,0:T(8,128)(2,1)S(1)}, bf16[512,128]{1,0:T(8,128)(2,1)S(1)}, u32[]{:S(2)}, u32[]{:S(2)}) %collective-permute-start.13) | collective-permute-done | bytes 131104 | tf_op jit(solution)/shard_map/ppermute | solution.py:201
  57.6 3.1 %collective-permute-start.16 = (bf16[512,128]{1,0:T(8,128)(2,1)S(1)}, bf16[512,128]{1,0:T(8,128)(2,1)S(1)}, u32[]{:S(2)}, u32[]{:S(2)}) collective-permute-start(bf16[512,128]{1,0:T(8,128)(2,1)S(1)} %fusion.2), channel_id=1, source_target_pairs={{0,2},{1,3},{2,0},{3,1},{4,6},{5,7},{6,4},{7,5},{8,10},{9,11},{10,... | collective-permute-start | bytes 393224 | tf_op jit(solution)/shard_map/ppermute | solution.py:238
  60.7 1.1 %collective-permute-start.15 = (bf16[512,128]{1,0:T(8,128)(2,1)S(1)}, bf16[512,128]{1,0:T(8,128)(2,1)S(1)}, u32[]{:S(2)}, u32[]{:S(2)}) collective-permute-start(bf16[512,128]{1,0:T(8,128)(2,1)S(1)} %fusion.2), channel_id=1, source_target_pairs={{0,3},{1,0},{2,1},{3,2},{4,7},{5,4},{6,5},{7,6},{8,11},{9,8},{10,9... | collective-permute-start | bytes 393224 | tf_op jit(solution)/shard_map/ppermute | solution.py:238
  61.8 0.9 %collective-permute-start.14 = (bf16[512,128]{1,0:T(8,128)(2,1)S(1)}, bf16[512,128]{1,0:T(8,128)(2,1)S(1)}, u32[]{:S(2)}, u32[]{:S(2)}) collective-permute-start(bf16[512,128]{1,0:T(8,128)(2,1)S(1)} %fusion.2), channel_id=1, source_target_pairs={{0,1},{1,2},{2,3},{3,0},{4,5},{5,6},{6,7},{7,4},{8,9},{9,10},{10,1... | collective-permute-start | bytes 393224 | tf_op jit(solution)/shard_map/ppermute | solution.py:238
  62.7 3.0 %shard_map.70 = bf16[512,4096]{1,0:T(8,128)(2,1)} custom-call(s32[3]{0:T(128)S(1)} %pad_add_fusion.pos, bf16[4,512,256]{2,1,0:T(8,128)(2,1)S(1)} %get-tuple-element.40.refs_0_, bf16[8,512,256]{2,1,0:T(8,128)(2,1)S(1)} %get-tuple-element.41.refs_1_, bf16[4,512,256]{2,1,0:T(8,128)(2,1)S(1)} %get-tuple-element.42.refs_2_), custom_call_target="tpu_custom_call" | custom-call | bytes 8388608 | tf_op jit(solution)/shard_map/pallas_call | solution.py:170
  65.7 2.3 %collective-permute-done.14 = bf16[512,128]{1,0:T(8,128)(2,1)S(1)} collective-permute-done((bf16[512,128]{1,0:T(8,128)(2,1)S(1)}, bf16[512,128]{1,0:T(8,128)(2,1)S(1)}, u32[]{:S(2)}, u32[]{:S(2)}) %collective-permute-start.14) | collective-permute-done | bytes 131104 | tf_op jit(solution)/shard_map/ppermute | solution.py:238
  68.0 0.9 %fusion = (f32[1,512,128]{2,1,0:T(8,128)}, bf16[512,128]{1,0:T(8,128)(2,1)}) fusion(bf16[512,128]{1,0:T(8,128)(2,1)S(1)} %multiply_convert_fusion.1, f32[1,512,128]{2,1,0:T(8,128)S(1)} %copy-done, f32[256,128]{1,0:T(8,128)S(1)} %fusion.3, f32[256,128]{1,0:T(8,128)S(1)} %fusion.4, bf16[512,128]{1,0:T(8,128)(2,1)S(1)} %collective-permute-done.16, ...), kind=kLoop, calls=%fused_computation.8 | loop fusion | flops 983040 | bytes 1572864 | tf_op jit(solution)/shard_map/broadcast_in_dim | solution.py:241
  (36 shorter events, 3.3 us)
Async XLA Ops:
  5.1 2.0 %collective-permute-start = (bf16[4,512,128]{2,1,0:T(8,128)(2,1)S(1)}, bf16[4,512,128]{2,1,0:T(8,128)(2,1)S(1)}, u32[]{:S(2)}, u32[]{:S(2)}) collective-permute-start(bf16[4,512,128]{2,1,0:T(8,128)(2,1)S(1)} %get-tuple-element.24), channel_id=1, source_target_pairs={{0,8},{8,0},{1,9},{9,1},{2,10},{10,2},{3,11},{11,3},{4,12},{12,4},... | collective-permute-start | bytes 1572872 | tf_op jit(solution)/shard_map/ppermute | solution.py:201
  7.2 10.7 %collective-permute-start.5 = (bf16[4,512,128]{2,1,0:T(8,128)(2,1)S(1)}, bf16[4,512,128]{2,1,0:T(8,128)(2,1)S(1)}, u32[]{:S(2)}, u32[]{:S(2)}) collective-permute-start(bf16[4,512,128]{2,1,0:T(8,128)(2,1)S(1)} %add_convert_fusion.2), channel_id=1, source_target_pairs={{0,16},{8,56},{16,0},{24,40},{32,48},{40,24},{48,32},{56,8},{1,17}... | collective-permute-start | bytes 1572872 | tf_op jit(solution)/shard_map/ppermute | solution.py:189
  14.1 2.5 %collective-permute-start.2 = (bf16[2,512,128]{2,1,0:T(8,128)(2,1)S(1)}, bf16[2,512,128]{2,1,0:T(8,128)(2,1)S(1)}, u32[]{:S(2)}, u32[]{:S(2)}) collective-permute-start(bf16[2,512,128]{2,1,0:T(8,128)(2,1)S(1)} %get-tuple-element.47), channel_id=1, source_target_pairs={{0,8},{8,0},{1,9},{9,1},{2,10},{10,2},{3,11},{11,3},{4,12},{12,4},... | collective-permute-start | bytes 786440 | tf_op jit(solution)/shard_map/ppermute | solution.py:201
  15.5 1.5 %collective-permute-start.1 = (bf16[2,512,128]{2,1,0:T(8,128)(2,1)S(1)}, bf16[2,512,128]{2,1,0:T(8,128)(2,1)S(1)}, u32[]{:S(2)}, u32[]{:S(2)}) collective-permute-start(bf16[2,512,128]{2,1,0:T(8,128)(2,1)S(1)} %get-tuple-element.48), channel_id=1, source_target_pairs={{0,8},{8,0},{1,9},{9,1},{2,10},{10,2},{3,11},{11,3},{4,12},{12,4},... | collective-permute-start | bytes 786440 | tf_op jit(solution)/shard_map/ppermute | solution.py:201
  15.6 1.8 %collective-permute-start.3 = (bf16[2,512,128]{2,1,0:T(8,128)(2,1)S(1)}, bf16[2,512,128]{2,1,0:T(8,128)(2,1)S(1)}, u32[]{:S(2)}, u32[]{:S(2)}) collective-permute-start(bf16[2,512,128]{2,1,0:T(8,128)(2,1)S(1)} %get-tuple-element.46), channel_id=1, source_target_pairs={{0,8},{8,0},{1,9},{9,1},{2,10},{10,2},{3,11},{11,3},{4,12},{12,4},... | collective-permute-start | bytes 786440 | tf_op jit(solution)/shard_map/ppermute | solution.py:201
  16.0 1.8 %collective-permute-start.4 = (bf16[2,512,128]{2,1,0:T(8,128)(2,1)S(1)}, bf16[2,512,128]{2,1,0:T(8,128)(2,1)S(1)}, u32[]{:S(2)}, u32[]{:S(2)}) collective-permute-start(bf16[2,512,128]{2,1,0:T(8,128)(2,1)S(1)} %get-tuple-element.45), channel_id=1, source_target_pairs={{0,8},{8,0},{1,9},{9,1},{2,10},{10,2},{3,11},{11,3},{4,12},{12,4},... | collective-permute-start | bytes 786440 | tf_op jit(solution)/shard_map/ppermute | solution.py:201
  17.8 14.4 %collective-permute-start.7 = (bf16[4,512,128]{2,1,0:T(8,128)(2,1)S(1)}, bf16[4,512,128]{2,1,0:T(8,128)(2,1)S(1)}, u32[]{:S(2)}, u32[]{:S(2)}) collective-permute-start(bf16[4,512,128]{2,1,0:T(8,128)(2,1)S(1)} %add_convert_fusion.1), channel_id=1, source_target_pairs={{0,16},{8,56},{16,0},{24,40},{32,48},{40,24},{48,32},{56,8},{1,17}... | collective-permute-start | bytes 1572872 | tf_op jit(solution)/shard_map/ppermute | solution.py:189
  18.1 15.1 %collective-permute-start.8 = (bf16[4,512,128]{2,1,0:T(8,128)(2,1)S(1)}, bf16[4,512,128]{2,1,0:T(8,128)(2,1)S(1)}, u32[]{:S(2)}, u32[]{:S(2)}) collective-permute-start(bf16[4,512,128]{2,1,0:T(8,128)(2,1)S(1)} %add_convert_fusion), channel_id=1, source_target_pairs={{0,48},{8,24},{16,32},{24,8},{32,16},{40,56},{48,0},{56,40},{1,49}... | collective-permute-start | bytes 1572872 | tf_op jit(solution)/shard_map/ppermute | solution.py:189
  24.2 27.9 %copy-start = (f32[1,512,128]{2,1,0:T(8,128)S(1)}, f32[1,512,128]{2,1,0:T(8,128)}, u32[]{:S(2)}) copy-start(f32[1,512,128]{2,1,0:T(8,128)} %param.7) | copy-start | bytes 786436
  24.2 9.1 %collective-permute-start.6 = (bf16[4,512,128]{2,1,0:T(8,128)(2,1)S(1)}, bf16[4,512,128]{2,1,0:T(8,128)(2,1)S(1)}, u32[]{:S(2)}, u32[]{:S(2)}) collective-permute-start(bf16[4,512,128]{2,1,0:T(8,128)(2,1)S(1)} %get-tuple-element.34), channel_id=1, source_target_pairs={{0,8},{8,0},{1,9},{9,1},{2,10},{10,2},{3,11},{11,3},{4,12},{12,4},... | collective-permute-start | bytes 1572872 | tf_op jit(solution)/shard_map/ppermute | solution.py:201
  33.5 7.7 %collective-permute-start.11 = (bf16[2,256,128]{2,1,0:T(8,128)(2,1)S(1)}, bf16[2,256,128]{2,1,0:T(8,128)(2,1)S(1)}, u32[]{:S(2)}, u32[]{:S(2)}) collective-permute-start(bf16[2,256,128]{2,1,0:T(8,128)(2,1)S(1)} %slice.118), channel_id=1, source_target_pairs={{0,64},{16,80},{32,96},{48,112},{8,200},{24,216},{40,232},{56,248}... | collective-permute-start | bytes 393224 | tf_op jit(solution)/shard_map/ppermute | solution.py:197
  36.8 8.7 %collective-permute-start.9 = (bf16[2,256,128]{2,1,0:T(8,128)(2,1)S(1)}, bf16[2,256,128]{2,1,0:T(8,128)(2,1)S(1)}, u32[]{:S(2)}, u32[]{:S(2)}) collective-permute-start(bf16[2,256,128]{2,1,0:T(8,128)(2,1)S(1)} %slice.119), channel_id=1, source_target_pairs={{0,64},{16,80},{32,96},{48,112},{8,200},{24,216},{40,232},{56,248}... | collective-permute-start | bytes 393224 | tf_op jit(solution)/shard_map/ppermute | solution.py:197
  41.2 7.5 %collective-permute-start.12 = (bf16[256,128]{1,0:T(8,128)(2,1)S(1)}, bf16[256,128]{1,0:T(8,128)(2,1)S(1)}, u32[]{:S(2)}, u32[]{:S(2)}) collective-permute-start(bf16[256,128]{1,0:T(8,128)(2,1)S(1)} %fusion.6), channel_id=1, source_target_pairs={{0,192},{16,208},{32,224},{48,240},{8,72},{24,88},{40,104},{56,120... | collective-permute-start | bytes 196616 | tf_op jit(solution)/shard_map/ppermute | solution.py:197
  45.6 6.5 %collective-permute-start.10 = (bf16[256,128]{1,0:T(8,128)(2,1)S(1)}, bf16[256,128]{1,0:T(8,128)(2,1)S(1)}, u32[]{:S(2)}, u32[]{:S(2)}) collective-permute-start(bf16[256,128]{1,0:T(8,128)(2,1)S(1)} %fusion.5), channel_id=1, source_target_pairs={{0,192},{16,208},{32,224},{48,240},{8,72},{24,88},{40,104},{56,120... | collective-permute-start | bytes 196616 | tf_op jit(solution)/shard_map/ppermute | solution.py:197
  52.5 5.1 %collective-permute-start.13 = (bf16[512,128]{1,0:T(8,128)(2,1)S(1)}, bf16[512,128]{1,0:T(8,128)(2,1)S(1)}, u32[]{:S(2)}, u32[]{:S(2)}) collective-permute-start(bf16[512,128]{1,0:T(8,128)(2,1)S(1)} %multiply_convert_fusion.1), channel_id=1, source_target_pairs={{0,4},{4,0},{1,5},{5,1},{2,6},{6,2},{3,7},{7,3},{8,12},{12,8},{9,1... | collective-permute-start | bytes 393224 | tf_op jit(solution)/shard_map/ppermute | solution.py:201
  57.6 8.1 %collective-permute-start.16 = (bf16[512,128]{1,0:T(8,128)(2,1)S(1)}, bf16[512,128]{1,0:T(8,128)(2,1)S(1)}, u32[]{:S(2)}, u32[]{:S(2)}) collective-permute-start(bf16[512,128]{1,0:T(8,128)(2,1)S(1)} %fusion.2), channel_id=1, source_target_pairs={{0,2},{1,3},{2,0},{3,1},{4,6},{5,7},{6,4},{7,5},{8,10},{9,11},{10,... | collective-permute-start | bytes 393224 | tf_op jit(solution)/shard_map/ppermute | solution.py:238
  60.7 5.0 %collective-permute-start.15 = (bf16[512,128]{1,0:T(8,128)(2,1)S(1)}, bf16[512,128]{1,0:T(8,128)(2,1)S(1)}, u32[]{:S(2)}, u32[]{:S(2)}) collective-permute-start(bf16[512,128]{1,0:T(8,128)(2,1)S(1)} %fusion.2), channel_id=1, source_target_pairs={{0,3},{1,0},{2,1},{3,2},{4,7},{5,4},{6,5},{7,6},{8,11},{9,8},{10,9... | collective-permute-start | bytes 393224 | tf_op jit(solution)/shard_map/ppermute | solution.py:238
  61.8 6.2 %collective-permute-start.14 = (bf16[512,128]{1,0:T(8,128)(2,1)S(1)}, bf16[512,128]{1,0:T(8,128)(2,1)S(1)}, u32[]{:S(2)}, u32[]{:S(2)}) collective-permute-start(bf16[512,128]{1,0:T(8,128)(2,1)S(1)} %fusion.2), channel_id=1, source_target_pairs={{0,1},{1,2},{2,3},{3,0},{4,5},{5,6},{6,7},{7,4},{8,9},{9,10},{10,1... | collective-permute-start | bytes 393224 | tf_op jit(solution)/shard_map/ppermute | solution.py:238

commit v5 on v4

--- a/solution.py
+++ b/solution.py
@@ -14,6 +14,8 @@
 MIB = 2**20
 CHUNKS = 2
 DEPTH = 4
+GROUP = (2, 1, 1)
+READY = 4
 PARTS = (
     tuple(("far", i) for i in range(4)),
     tuple(("one", i) for i in range(4)) + tuple(("two", i) for i in range(4)),
@@ -62,65 +64,99 @@
     return [[((z * 4 + left) * 2 + core) * BLK, ((z * 4 + right) * 2 + other) * BLK] for z in zs]
 
 
-def windows(starts):
+def columns_of(pos, part):
+    kinds = {kind: items_of(pos, kind) for kind, _ in PARTS[part]}
+    return [kinds[kind][i] for kind, i in PARTS[part]]
+
+
+def windows(starts, offset=0):
     width = 256 // len(starts)
     for k, start in enumerate(starts):
-        yield k, pl.ds(pl.multiple_of(start, width), width), pl.ds(k * width, width)
+        yield k, pl.ds(pl.multiple_of(start, width), width), pl.ds(offset + k * width, width)
 
 
 def grad_kernel(pos, kc, acts, err, *refs, part):
     if part == 0:
-        send, keep, ev, kct, kcv, av, gv, asem, ksem = refs
+        send, keep, ev, kct, ready_a, ready_e, kcv, av, gv, asem, rsem, ksem = refs
+    elif part == 1:
+        ready_a, ready_e, send, keep, ev, av, gv, asem = refs
+        kct = kc
     else:
         send, keep, ev, av, gv, asem = refs
         kct = kc
     core = pos[2]
-    kinds = {kind: items_of(pos, kind) for kind, _ in PARTS[part]}
-    items = [kinds[kind][i] for kind, i in PARTS[part]]
-    n = len(items)
+    items = columns_of(pos, part)
+    n, group = len(items), GROUP[part]
+    first = READY if part == 1 else 0
 
     def loads(i):
+        for k, col, half in windows(items[i], 256 * (i % group)):
+            yield pltpu.make_async_copy(acts.at[:, col], av.at[i // group, :, half], asem.at[i, k, 0])
         for k, col, half in windows(items[i]):
-            yield pltpu.make_async_copy(acts.at[:, col], av.at[i, :, half], asem.at[i, k, 0])
             yield pltpu.make_async_copy(err.at[:, col], ev.at[i, :, half], asem.at[i, k, 1])
+
+    def loads_ahead():
+        for i, item in enumerate(columns_of(pos, 1)[:READY]):
+            for k, col, half in windows(item):
+                yield pltpu.make_async_copy(acts.at[:, col], ready_a.at[i, :, half], rsem.at[i, k, 0])
+                yield pltpu.make_async_copy(err.at[:, col], ready_e.at[i, :, half], rsem.at[i, k, 1])
+
+    def ready(p):
+        for i in range(p * group, (p + 1) * group):
+            if i >= first:
+                for copy in loads(i):
+                    copy.wait()
+
+    def source(p):
+        return ready_a[p] if p < first else av[p]
 
     if part == 0:
         load_kc = pltpu.make_async_copy(kc, kcv, ksem)
         load_kc.start()
-    for i in range(DEPTH):
+    for i in range(first, first + DEPTH):
         for copy in loads(i):
             copy.start()
     if part == 0:
         load_kc.wait()
         kct[...] = kcv[...].T
-    for copy in loads(0):
-        copy.wait()
-    gv[0] = jnp.dot(kct[...], av[0], preferred_element_type=F32)
-    for i in range(n):
-        if i + DEPTH < n:
-            for copy in loads(i + DEPTH):
-                copy.start()
-        if i + 1 < n:
-            for copy in loads(i + 1):
-                copy.wait()
+    ready(0)
+    if part == 0:
+        for copy in loads_ahead():
+            copy.start()
+    gv[0] = jnp.dot(kct[...], source(0), preferred_element_type=F32)
+    for p in range(n // group):
+        members = range(p * group, (p + 1) * group)
+        for i in members:
+            if i >= first and i + DEPTH < n:
+                for copy in loads(i + DEPTH):
+                    copy.start()
+        more = p + 1 < n // group
+        if more:
+            ready(p + 1)
         for r in range(0, 512, 256):
             rows = slice(r, r + 256)
-            if i + 1 < n:
-                gv[(i + 1) % 2, rows] = jnp.dot(kct[rows], av[i + 1], preferred_element_type=F32)
-            q = []
-            for k in range(2):
-                s = slice(k * BLK, (k + 1) * BLK)
-                v = gv[i % 2, rows, s] + ev[i, rows, s].astype(F32)
-                q.append(squash(v))
-                ev[i, rows, s] = (v - q[k].astype(F32)).astype(BF)
-            if len(items[i]) == 1:
-                q = [jnp.where(core == 0, q[0], q[1]), jnp.where(core == 0, q[1], q[0])]
-            keep[i, rows] = q[0]
-            send[SEND_SLOT[part][i], rows] = q[1]
-
-
-def grad_part(pos, kc, acts, err, part):
-    n = len(PARTS[part])
+            if more:
+                gv[(p + 1) % 2, rows] = jnp.dot(kct[rows], source(p + 1), preferred_element_type=F32)
+            for i in members:
+                q = []
+                for k in range(2):
+                    s = slice(k * BLK, (k + 1) * BLK)
+                    t = 256 * (i % group) + k * BLK
+                    residual = (ready_e if i < first else ev)[i, rows, s]
+                    v = gv[p % 2, rows, t : t + BLK] + residual.astype(F32)
+                    q.append(squash(v))
+                    ev[i, rows, s] = (v - q[k].astype(F32)).astype(BF)
+                if len(items[i]) == 1:
+                    q = [jnp.where(core == 0, q[0], q[1]), jnp.where(core == 0, q[1], q[0])]
+                keep[i, rows] = q[0]
+                send[SEND_SLOT[part][i], rows] = q[1]
+    if part == 0:
+        for copy in loads_ahead():
+            copy.wait()
+
+
+def grad_part(pos, kc, acts, err, part, ahead=()):
+    n, group = len(PARTS[part]), GROUP[part]
     in_hbm = pl.BlockSpec(memory_space=pl.ANY)
     near = pl.BlockSpec(memory_space=pltpu.VMEM)
     in_smem = pl.BlockSpec(memory_space=pltpu.SMEM)
@@ -128,16 +164,21 @@
     half = pltpu.VMEM((n, 512, BLK), BF)
     outs = [half, half, pltpu.VMEM((n, 512, 256), BF)]
     scratch = [
-        pltpu.VMEM((n, 512, 256), BF),
-        pltpu.VMEM((2, 512, 256), F32),
+        pltpu.VMEM((n // group, 512, 256 * group), BF),
+        pltpu.VMEM((2, 512, 256 * group), F32),
         pltpu.SemaphoreType.DMA((n, 2, 2)),
     ]
     if part == 0:
-        outs.append(pltpu.VMEM((512, 512), BF))
-        scratch = [pltpu.VMEM((512, 512), BF), *scratch, pltpu.SemaphoreType.DMA]
+        outs += [pltpu.VMEM((512, 512), BF)] + [pltpu.VMEM((READY, 512, 256), BF)] * 2
+        scratch = [
+            pltpu.VMEM((512, 512), BF),
+            *scratch,
+            pltpu.SemaphoreType.DMA((READY, 2, 2)),
+            pltpu.SemaphoreType.DMA,
+        ]
     return pl.pallas_call(
         functools.partial(grad_kernel, part=part),
-        in_specs=[in_smem, in_hbm if part == 0 else near, in_hbm, in_hbm],
+        in_specs=[in_smem, in_hbm if part == 0 else near, in_hbm, in_hbm] + [near] * len(ahead),
         out_specs=[near] * len(outs),
         out_shape=outs,
         scratch_shapes=scratch,
@@ -145,15 +186,15 @@
         cost_estimate=pl.CostEstimate(
             flops=10**6, bytes_accessed=10**4, transcendentals=0
         ),
-    )(pos, pin(kc) if part == 0 else kc, pin(acts), pin(err))
+    )(pos, pin(kc) if part == 0 else kc, pin(acts), pin(err), *ahead)
 
 
 def store_kernel(pos, *refs):
     blocks, (newerr, sem) = refs[: len(PARTS)], refs[len(PARTS) :]
     copies = []
-    for part, members in enumerate(PARTS):
-        for i, (kind, item) in enumerate(members):
-            for k, col, half in windows(items_of(pos, kind)[item]):
+    for part in range(len(PARTS)):
+        for i, item in enumerate(columns_of(pos, part)):
+            for k, col, half in windows(item):
                 copies.append(
                     pltpu.make_async_copy(
                         blocks[part].at[i, :, half], newerr.at[:, col], sem.at[part, i, k]
@@ -206,15 +247,15 @@
     err = error_rows[0, 0]
     parts = [slice(r, r + 512 // CHUNKS) for r in range(0, 512, 512 // CHUNKS)]
     tie = lax.optimization_barrier
-    send, keep, err_0, kct = grad_part(pos, key_cotangent, acts, err, 0)
+    send, keep, err_0, kct, *loaded = grad_part(pos, key_cotangent, acts, err, 0)
     ahead = add(keep, swap(send, "core")).astype(BF)
     pos, ahead = tie((pos, ahead))
     got_0 = y_step(ahead, 0)
-    send, keep, err_1 = grad_part(pos, kct, acts, err, 1)
+    send, keep, err_1 = grad_part(pos, kct, acts, err, 1, loaded)
     near = [swap(send[k : k + 2], "core") for k in range(0, 8, 2)]
     one, two = jnp.concatenate(near[: 2]), near[2 :]
     ahead = add(keep[:4], one).astype(BF)
-    ahead, two = tie((ahead, two))
+    _, two = tie((ahead, two))
     got_1 = y_step(ahead, 0)
     ahead = add(keep[4:], jnp.concatenate(two), got_0).astype(BF)
     pos, ahead = tie((pos, ahead))
@@ -233,7 +274,9 @@
     carried_two = summed * (1.0 / 32.0) + error_cols[0]
     sent_two = lax.optimization_barrier(squash(carried_two))
     new_cols = carried_two - sent_two.astype(F32)
-    total = add(sent_two, swap(sent_two, "zl"))
+    swapped = swap(sent_two, "zl")
+    sent_two, new_cols = tie((sent_two, new_cols))
+    total = add(sent_two, swapped)
     near = [
         lax.ppermute(total.astype(BF), "x", [(i, (i + d) % 4) for i in range(4)]) for d in (1, 3, 2)
     ]

time: 69.1 us -> 67.1 us (0.971)
  waiting for transfers between devices: 25.4 us -> 23.7 us
  Pallas kernels: 16 us -> 14.5 us
  starting transfers between devices: 24.3 us -> 25 us
    pallas_call x3, Pallas kernels: 13.1 us -> 11.5 us  [grad_part(): pl.pallas_call(functools.partial(grad_kernel, part=part), in_specs=[in_sm...]
    broadcast_in_dim x1 -> x0, other arithmetic: 0.87 us -> none  [body(): return (averaged, newerr[None, None], new_cols[None])]
    ppermute x7, waiting for transfers between devices: 6.8 us -> 5.93 us  [swap(): return lax.ppermute(x, axis, [(0, 1), (1, 0)])]
    ppermute x3, waiting for transfers between devices: 8.7 us -> 7.89 us  [y_step(): return lax.ppermute(x, ('y', 'core'), ring_pairs(which, (4, 2), 0, 1))]
    convert_element_type x0 -> x1, other arithmetic: none -> 0.75 us  [body(): averaged = (add(total, *near) * 0.125).astype(BF)]
    sub x0 -> x1, other arithmetic: none -> 0.74 us  [body(): new_cols = carried_two - sent_two.astype(F32)]
    ppermute x3, starting transfers between devices: 4.29 us -> 4.99 us  [y_step(): return lax.ppermute(x, ('y', 'core'), ring_pairs(which, (4, 2), 0, 1))]
  transfers between devices with their start and end apart: 17 -> 17, of which waited for: 11 -> 11; matrix products, arithmetic and copies ran while one was open for 1% -> 2% of each run, Pallas kernels for 17% -> 15%
where the time goes in v5:
time: 67.1 us; the launch traced here: 66.9 us
  starting transfers between devices  25 us (37%)
  waiting for transfers between devices  23.7 us (35%)
  Pallas kernels  14.5 us (22%)
  other arithmetic  2.78 us (4%)
  between operations  0.82 us (1%)
    pallas_call x3, Pallas kernels, grad_part(): pl.pallas_call(functools.partial(grad_kernel, part=part), in_specs=[in_sm...  11.5 us
    ppermute x4, starting transfers between devices, z_step(): return lax.ppermute(x, ('zh', 'y', 'core'), pairs)  11.1 us
    ppermute x3, waiting for transfers between devices, y_step(): return lax.ppermute(x, ('y', 'core'), ring_pairs(which, (4, 2), 0, 1))  7.89 us
    ppermute x4, waiting for transfers between devices, z_step(): return lax.ppermute(x, ('zh', 'y', 'core'), pairs)  7.52 us
    ppermute x7, waiting for transfers between devices, swap(): return lax.ppermute(x, axis, [(0, 1), (1, 0)])  5.93 us
    ppermute x3, starting transfers between devices, body(): lax.ppermute(total.astype(BF), 'x', [(i, (i + d) % 4) for i in range(4)])  5.13 us
    ppermute x3, starting transfers between devices, y_step(): return lax.ppermute(x, ('y', 'core'), ring_pairs(which, (4, 2), 0, 1))  4.99 us
    ppermute x7, starting transfers between devices, swap(): return lax.ppermute(x, axis, [(0, 1), (1, 0)])  3.77 us
  transfers between devices with their start and end apart: 17, of which 11 were waited for; matrix products, arithmetic and copies ran while one was open for 2% of the time, Pallas kernels for 15%

profile of v5, /device:TPU:32, one launch (start us, length us, event | category | flops | bytes accessed | tf_op | source)
XLA Modules:
  0.0 66.9 jit_solution(1019193814021515959)
XLA Ops:
  0.7 4.4 %shard_map.67 = (bf16[4,512,128]{2,1,0:T(8,128)(2,1)S(1)}, bf16[4,512,128]{2,1,0:T(8,128)(2,1)S(1)}, bf16[4,512,256]{2,1,0:T(8,128)(2,1)S(1)}, bf16[512,512]{1,0...) custom-call(s32[3]{0:T(128)S(1)} %pad_add_fusion.pos, bf16[512,512]{1,0:T(8,128)(2,1)} %kc.1, ...), custom_call_target="tpu_custom_call" | custom-call | flops 1000000 | bytes 10000 | tf_op jit(solution)/shard_map/pallas_call | solution.py:179
  5.2 1.9 %collective-permute-done = bf16[4,512,128]{2,1,0:T(8,128)(2,1)S(1)} collective-permute-done((bf16[4,512,128]{2,1,0:T(8,128)(2,1)S(1)}, bf16[4,512,128]{2,1,0:T(8,128)(2,1)S(1)}, u32[]{:S(2)}, u32[]{:S(2)}) %collective-permute-start) | collective-permute-done | bytes 524320 | tf_op jit(solution)/shard_map/ppermute | solution.py:242
  7.3 1.7 %collective-permute-start.5 = (bf16[4,512,128]{2,1,0:T(8,128)(2,1)S(1)}, bf16[4,512,128]{2,1,0:T(8,128)(2,1)S(1)}, u32[]{:S(2)}, u32[]{:S(2)}) collective-permute-start(bf16[4,512,128]{2,1,0:T(8,128)(2,1)S(1)} %add_convert_fusion.2), channel_id=1, source_target_pairs={{0,16},{8,56},{16,0},{24,40},{32,48},{40,24},{48,32},{56,8},{1,17}... | collective-permute-start | bytes 1572872 | tf_op jit(solution)/shard_map/ppermute | solution.py:230
  8.9 3.6 %shard_map.68 = (bf16[8,512,128]{2,1,0:T(8,128)(2,1)S(1)}, bf16[8,512,128]{2,1,0:T(8,128)(2,1)S(1)}, bf16[8,512,256]{2,1,0:T(8,128)(2,1)S(1)}) custom-call(s32[3]{0:T(128)S(1)} %pad_add_fusion.pos, bf16[512,512]{1,0:T(8,128)(2,1)S(1)} %get-tuple-element.29.kc, bf16[512,4096]{1,0:T(8,128)(2,1)} %acts.5, bf16[512,4096]{1,0:T(8,128)(2,1)} %bitcast.27, ...), custom_call_target="tpu_custom_call" | custom-call | flops 1000000 | bytes 10000 | tf_op jit(solution)/shard_map/pallas_call | solution.py:179
  12.6 1.4 %collective-permute-start.2 = (bf16[2,512,128]{2,1,0:T(8,128)(2,1)S(1)}, bf16[2,512,128]{2,1,0:T(8,128)(2,1)S(1)}, u32[]{:S(2)}, u32[]{:S(2)}) collective-permute-start(bf16[2,512,128]{2,1,0:T(8,128)(2,1)S(1)} %get-tuple-element.53), channel_id=1, source_target_pairs={{0,8},{8,0},{1,9},{9,1},{2,10},{10,2},{3,11},{11,3},{4,12},{12,4},... | collective-permute-start | bytes 786440 | tf_op jit(solution)/shard_map/ppermute | solution.py:242
  14.6 0.6 collective-permute-done.2
  16.7 3.1 %collective-permute-start.8 = (bf16[4,512,128]{2,1,0:T(8,128)(2,1)S(1)}, bf16[4,512,128]{2,1,0:T(8,128)(2,1)S(1)}, u32[]{:S(2)}, u32[]{:S(2)}) collective-permute-start(bf16[4,512,128]{2,1,0:T(8,128)(2,1)S(1)} %add_convert_fusion), channel_id=1, source_target_pairs={{0,48},{8,24},{16,32},{24,8},{32,16},{40,56},{48,0},{56,40},{1,49}... | collective-permute-start | bytes 1572872 | tf_op jit(solution)/shard_map/ppermute | solution.py:230
  19.8 3.6 %shard_map.69 = (bf16[4,512,128]{2,1,0:T(8,128)(2,1)S(1)}, bf16[4,512,128]{2,1,0:T(8,128)(2,1)S(1)}, bf16[4,512,256]{2,1,0:T(8,128)(2,1)S(1)}) custom-call(s32[3]{0:T(128)S(1)} %pad_add_fusion.pos, bf16[512,512]{1,0:T(8,128)(2,1)S(1)} %get-tuple-element.29.kc, bf16[512,4096]{1,0:T(8,128)(2,1)} %acts.5, bf16[512,4096]{1,0:T(8,128)(2,1)} %bitcast.28), custom_call_target="tpu_custom_call" | custom-call | flops 1000000 | bytes 10000 | tf_op jit(solution)/shard_map/pallas_call | solution.py:179
  23.5 6.6 %collective-permute-done.7 = bf16[4,512,128]{2,1,0:T(8,128)(2,1)S(1)} collective-permute-done((bf16[4,512,128]{2,1,0:T(8,128)(2,1)S(1)}, bf16[4,512,128]{2,1,0:T(8,128)(2,1)S(1)}, u32[]{:S(2)}, u32[]{:S(2)}) %collective-permute-start.7) | collective-permute-done | bytes 524320 | tf_op jit(solution)/shard_map/ppermute | solution.py:230
  30.1 1.0 %collective-permute-done.8 = bf16[4,512,128]{2,1,0:T(8,128)(2,1)S(1)} collective-permute-done((bf16[4,512,128]{2,1,0:T(8,128)(2,1)S(1)}, bf16[4,512,128]{2,1,0:T(8,128)(2,1)S(1)}, u32[]{:S(2)}, u32[]{:S(2)}) %collective-permute-start.8) | collective-permute-done | bytes 524320 | tf_op jit(solution)/shard_map/ppermute | solution.py:230
  31.4 3.5 %collective-permute-start.11 = (bf16[2,256,128]{2,1,0:T(8,128)(2,1)S(1)}, bf16[2,256,128]{2,1,0:T(8,128)(2,1)S(1)}, u32[]{:S(2)}, u32[]{:S(2)}) collective-permute-start(bf16[2,256,128]{2,1,0:T(8,128)(2,1)S(1)} %slice.118), channel_id=1, source_target_pairs={{0,64},{16,80},{32,96},{48,112},{8,200},{24,216},{40,232},{56,248}... | collective-permute-start | bytes 393224 | tf_op jit(solution)/shard_map/ppermute | solution.py:238
  35.1 4.2 %collective-permute-done.11 = bf16[2,256,128]{2,1,0:T(8,128)(2,1)S(1)} collective-permute-done((bf16[2,256,128]{2,1,0:T(8,128)(2,1)S(1)}, bf16[2,256,128]{2,1,0:T(8,128)(2,1)S(1)}, u32[]{:S(2)}, u32[]{:S(2)}) %collective-permute-start.11) | collective-permute-done | bytes 131104 | tf_op jit(solution)/shard_map/ppermute | solution.py:238
  39.3 4.3 %collective-permute-start.12 = (bf16[256,128]{1,0:T(8,128)(2,1)S(1)}, bf16[256,128]{1,0:T(8,128)(2,1)S(1)}, u32[]{:S(2)}, u32[]{:S(2)}) collective-permute-start(bf16[256,128]{1,0:T(8,128)(2,1)S(1)} %fusion.5), channel_id=1, source_target_pairs={{0,192},{16,208},{32,224},{48,240},{8,72},{24,88},{40,104},{56,120... | collective-permute-start | bytes 196616 | tf_op jit(solution)/shard_map/ppermute | solution.py:238
  43.7 3.1 %collective-permute-start.10 = (bf16[256,128]{1,0:T(8,128)(2,1)S(1)}, bf16[256,128]{1,0:T(8,128)(2,1)S(1)}, u32[]{:S(2)}, u32[]{:S(2)}) collective-permute-start(bf16[256,128]{1,0:T(8,128)(2,1)S(1)} %fusion.4), channel_id=1, source_target_pairs={{0,192},{16,208},{32,224},{48,240},{8,72},{24,88},{40,104},{56,120... | collective-permute-start | bytes 196616 | tf_op jit(solution)/shard_map/ppermute | solution.py:238
  46.9 3.3 %collective-permute-done.10 = bf16[256,128]{1,0:T(8,128)(2,1)S(1)} collective-permute-done((bf16[256,128]{1,0:T(8,128)(2,1)S(1)}, bf16[256,128]{1,0:T(8,128)(2,1)S(1)}, u32[]{:S(2)}, u32[]{:S(2)}) %collective-permute-start.10) | collective-permute-done | bytes 65568 | tf_op jit(solution)/shard_map/ppermute | solution.py:238
  50.6 1.6 %collective-permute-start.13 = (bf16[512,128]{1,0:T(8,128)(2,1)S(1)}, bf16[512,128]{1,0:T(8,128)(2,1)S(1)}, u32[]{:S(2)}, u32[]{:S(2)}) collective-permute-start(bf16[512,128]{1,0:T(8,128)(2,1)S(1)} %multiply_convert_fusion.1), channel_id=1, source_target_pairs={{0,4},{4,0},{1,5},{5,1},{2,6},{6,2},{3,7},{7,3},{8,12},{12,8},{9,1... | collective-permute-start | bytes 393224 | tf_op jit(solution)/shard_map/ppermute | solution.py:242
  52.2 0.7 %convert_subtract_fusion = f32[512,128]{1,0:T(8,128)} fusion(bf16[512,128]{1,0:T(8,128)(2,1)S(1)} %multiply_convert_fusion.1, f32[1,512,128]{2,1,0:T(8,128)S(1)} %copy-done, f32[256,128]{1,0:T(8,128)S(1)} %fusion.2, f32[256,128]{1,0:T(8,128)S(1)} %fusion.3), kind=kLoop, calls=%fused_computation.12 | loop fusion | flops 327680 | bytes 917504 | tf_op jit(solution)/shard_map/sub | solution.py:276
  52.9 2.7 %collective-permute-done.13 = bf16[512,128]{1,0:T(8,128)(2,1)S(1)} collective-permute-done((bf16[512,128]{1,0:T(8,128)(2,1)S(1)}, bf16[512,128]{1,0:T(8,128)(2,1)S(1)}, u32[]{:S(2)}, u32[]{:S(2)}) %collective-permute-start.13) | collective-permute-done | bytes 131104 | tf_op jit(solution)/shard_map/ppermute | solution.py:242
  55.7 3.1 %collective-permute-start.16 = (bf16[512,128]{1,0:T(8,128)(2,1)S(1)}, bf16[512,128]{1,0:T(8,128)(2,1)S(1)}, u32[]{:S(2)}, u32[]{:S(2)}) collective-permute-start(bf16[512,128]{1,0:T(8,128)(2,1)S(1)} %fusion.1), channel_id=1, source_target_pairs={{0,2},{1,3},{2,0},{3,1},{4,6},{5,7},{6,4},{7,5},{8,10},{9,11},{10,... | collective-permute-start | bytes 393224 | tf_op jit(solution)/shard_map/ppermute | solution.py:281
  58.8 1.2 %collective-permute-start.15 = (bf16[512,128]{1,0:T(8,128)(2,1)S(1)}, bf16[512,128]{1,0:T(8,128)(2,1)S(1)}, u32[]{:S(2)}, u32[]{:S(2)}) collective-permute-start(bf16[512,128]{1,0:T(8,128)(2,1)S(1)} %fusion.1), channel_id=1, source_target_pairs={{0,3},{1,0},{2,1},{3,2},{4,7},{5,4},{6,5},{7,6},{8,11},{9,8},{10,9... | collective-permute-start | bytes 393224 | tf_op jit(solution)/shard_map/ppermute | solution.py:281
  60.0 0.9 %collective-permute-start.14 = (bf16[512,128]{1,0:T(8,128)(2,1)S(1)}, bf16[512,128]{1,0:T(8,128)(2,1)S(1)}, u32[]{:S(2)}, u32[]{:S(2)}) collective-permute-start(bf16[512,128]{1,0:T(8,128)(2,1)S(1)} %fusion.1), channel_id=1, source_target_pairs={{0,1},{1,2},{2,3},{3,0},{4,5},{5,6},{6,7},{7,4},{8,9},{9,10},{10,1... | collective-permute-start | bytes 393224 | tf_op jit(solution)/shard_map/ppermute | solution.py:281
  60.8 3.0 %shard_map.70 = bf16[512,4096]{1,0:T(8,128)(2,1)} custom-call(s32[3]{0:T(128)S(1)} %pad_add_fusion.pos, bf16[4,512,256]{2,1,0:T(8,128)(2,1)S(1)} %get-tuple-element.45.refs_0_, bf16[8,512,256]{2,1,0:T(8,128)(2,1)S(1)} %get-tuple-element.46.refs_1_, bf16[4,512,256]{2,1,0:T(8,128)(2,1)S(1)} %get-tuple-element.47.refs_2_), custom_call_target="tpu_custom_call" | custom-call | bytes 8388608 | tf_op jit(solution)/shard_map/pallas_call | solution.py:211
  63.8 2.3 %collective-permute-done.14 = bf16[512,128]{1,0:T(8,128)(2,1)S(1)} collective-permute-done((bf16[512,128]{1,0:T(8,128)(2,1)S(1)}, bf16[512,128]{1,0:T(8,128)(2,1)S(1)}, u32[]{:S(2)}, u32[]{:S(2)}) %collective-permute-start.14) | collective-permute-done | bytes 131104 | tf_op jit(solution)/shard_map/ppermute | solution.py:281
  66.1 0.8 %multiply_convert_fusion = bf16[512,128]{1,0:T(8,128)(2,1)} fusion(bf16[512,128]{1,0:T(8,128)(2,1)S(1)} %collective-permute-done.16, bf16[512,128]{1,0:T(8,128)(2,1)S(1)} %collective-permute-done.15, bf16[512,128]{1,0:T(8,128)(2,1)S(1)} %collective-permute-done.14, bf16[512,128]{1,0:T(8,128)(2,1)S(1)} %collective-permute-done.13, ...), kind=kLoop, calls=%fused_computation.10 | loop fusion | flops 720896 | bytes 786432 | tf_op jit(solution)/shard_map/convert_element_type | solution.py:283
  (37 shorter events, 3.6 us)
Async XLA Ops:
  5.1 2.0 %collective-permute-start = (bf16[4,512,128]{2,1,0:T(8,128)(2,1)S(1)}, bf16[4,512,128]{2,1,0:T(8,128)(2,1)S(1)}, u32[]{:S(2)}, u32[]{:S(2)}) collective-permute-start(bf16[4,512,128]{2,1,0:T(8,128)(2,1)S(1)} %get-tuple-element.27), channel_id=1, source_target_pairs={{0,8},{8,0},{1,9},{9,1},{2,10},{10,2},{3,11},{11,3},{4,12},{12,4},... | collective-permute-start | bytes 1572872 | tf_op jit(solution)/shard_map/ppermute | solution.py:242
  7.3 9.3 %collective-permute-start.5 = (bf16[4,512,128]{2,1,0:T(8,128)(2,1)S(1)}, bf16[4,512,128]{2,1,0:T(8,128)(2,1)S(1)}, u32[]{:S(2)}, u32[]{:S(2)}) collective-permute-start(bf16[4,512,128]{2,1,0:T(8,128)(2,1)S(1)} %add_convert_fusion.2), channel_id=1, source_target_pairs={{0,16},{8,56},{16,0},{24,40},{32,48},{40,24},{48,32},{56,8},{1,17}... | collective-permute-start | bytes 1572872 | tf_op jit(solution)/shard_map/ppermute | solution.py:230
  12.6 2.5 %collective-permute-start.2 = (bf16[2,512,128]{2,1,0:T(8,128)(2,1)S(1)}, bf16[2,512,128]{2,1,0:T(8,128)(2,1)S(1)}, u32[]{:S(2)}, u32[]{:S(2)}) collective-permute-start(bf16[2,512,128]{2,1,0:T(8,128)(2,1)S(1)} %get-tuple-element.53), channel_id=1, source_target_pairs={{0,8},{8,0},{1,9},{9,1},{2,10},{10,2},{3,11},{11,3},{4,12},{12,4},... | collective-permute-start | bytes 786440 | tf_op jit(solution)/shard_map/ppermute | solution.py:242
  14.0 1.5 %collective-permute-start.1 = (bf16[2,512,128]{2,1,0:T(8,128)(2,1)S(1)}, bf16[2,512,128]{2,1,0:T(8,128)(2,1)S(1)}, u32[]{:S(2)}, u32[]{:S(2)}) collective-permute-start(bf16[2,512,128]{2,1,0:T(8,128)(2,1)S(1)} %get-tuple-element.54), channel_id=1, source_target_pairs={{0,8},{8,0},{1,9},{9,1},{2,10},{10,2},{3,11},{11,3},{4,12},{12,4},... | collective-permute-start | bytes 786440 | tf_op jit(solution)/shard_map/ppermute | solution.py:242
  14.1 1.8 %collective-permute-start.3 = (bf16[2,512,128]{2,1,0:T(8,128)(2,1)S(1)}, bf16[2,512,128]{2,1,0:T(8,128)(2,1)S(1)}, u32[]{:S(2)}, u32[]{:S(2)}) collective-permute-start(bf16[2,512,128]{2,1,0:T(8,128)(2,1)S(1)} %get-tuple-element.52), channel_id=1, source_target_pairs={{0,8},{8,0},{1,9},{9,1},{2,10},{10,2},{3,11},{11,3},{4,12},{12,4},... | collective-permute-start | bytes 786440 | tf_op jit(solution)/shard_map/ppermute | solution.py:242
  14.5 1.8 %collective-permute-start.4 = (bf16[2,512,128]{2,1,0:T(8,128)(2,1)S(1)}, bf16[2,512,128]{2,1,0:T(8,128)(2,1)S(1)}, u32[]{:S(2)}, u32[]{:S(2)}) collective-permute-start(bf16[2,512,128]{2,1,0:T(8,128)(2,1)S(1)} %get-tuple-element.51), channel_id=1, source_target_pairs={{0,8},{8,0},{1,9},{9,1},{2,10},{10,2},{3,11},{11,3},{4,12},{12,4},... | collective-permute-start | bytes 786440 | tf_op jit(solution)/shard_map/ppermute | solution.py:242
  15.6 14.5 %collective-permute-start.7 = (bf16[4,512,128]{2,1,0:T(8,128)(2,1)S(1)}, bf16[4,512,128]{2,1,0:T(8,128)(2,1)S(1)}, u32[]{:S(2)}, u32[]{:S(2)}) collective-permute-start(bf16[4,512,128]{2,1,0:T(8,128)(2,1)S(1)} %add_convert_fusion.1), channel_id=1, source_target_pairs={{0,16},{8,56},{16,0},{24,40},{32,48},{40,24},{48,32},{56,8},{1,17}... | collective-permute-start | bytes 1572872 | tf_op jit(solution)/shard_map/ppermute | solution.py:230
  16.7 14.4 %collective-permute-start.8 = (bf16[4,512,128]{2,1,0:T(8,128)(2,1)S(1)}, bf16[4,512,128]{2,1,0:T(8,128)(2,1)S(1)}, u32[]{:S(2)}, u32[]{:S(2)}) collective-permute-start(bf16[4,512,128]{2,1,0:T(8,128)(2,1)S(1)} %add_convert_fusion), channel_id=1, source_target_pairs={{0,48},{8,24},{16,32},{24,8},{32,16},{40,56},{48,0},{56,40},{1,49}... | collective-permute-start | bytes 1572872 | tf_op jit(solution)/shard_map/ppermute | solution.py:230
  23.4 26.8 %copy-start = (f32[1,512,128]{2,1,0:T(8,128)S(1)}, f32[1,512,128]{2,1,0:T(8,128)}, u32[]{:S(2)}) copy-start(f32[1,512,128]{2,1,0:T(8,128)} %param.7) | copy-start | bytes 786436
  23.4 7.8 %collective-permute-start.6 = (bf16[4,512,128]{2,1,0:T(8,128)(2,1)S(1)}, bf16[4,512,128]{2,1,0:T(8,128)(2,1)S(1)}, u32[]{:S(2)}, u32[]{:S(2)}) collective-permute-start(bf16[4,512,128]{2,1,0:T(8,128)(2,1)S(1)} %get-tuple-element.39), channel_id=1, source_target_pairs={{0,8},{8,0},{1,9},{9,1},{2,10},{10,2},{3,11},{11,3},{4,12},{12,4},... | collective-permute-start | bytes 1572872 | tf_op jit(solution)/shard_map/ppermute | solution.py:242
  31.4 7.9 %collective-permute-start.11 = (bf16[2,256,128]{2,1,0:T(8,128)(2,1)S(1)}, bf16[2,256,128]{2,1,0:T(8,128)(2,1)S(1)}, u32[]{:S(2)}, u32[]{:S(2)}) collective-permute-start(bf16[2,256,128]{2,1,0:T(8,128)(2,1)S(1)} %slice.118), channel_id=1, source_target_pairs={{0,64},{16,80},{32,96},{48,112},{8,200},{24,216},{40,232},{56,248}... | collective-permute-start | bytes 393224 | tf_op jit(solution)/shard_map/ppermute | solution.py:238
  35.0 8.7 %collective-permute-start.9 = (bf16[2,256,128]{2,1,0:T(8,128)(2,1)S(1)}, bf16[2,256,128]{2,1,0:T(8,128)(2,1)S(1)}, u32[]{:S(2)}, u32[]{:S(2)}) collective-permute-start(bf16[2,256,128]{2,1,0:T(8,128)(2,1)S(1)} %slice.119), channel_id=1, source_target_pairs={{0,64},{16,80},{32,96},{48,112},{8,200},{24,216},{40,232},{56,248}... | collective-permute-start | bytes 393224 | tf_op jit(solution)/shard_map/ppermute | solution.py:238
  39.3 7.5 %collective-permute-start.12 = (bf16[256,128]{1,0:T(8,128)(2,1)S(1)}, bf16[256,128]{1,0:T(8,128)(2,1)S(1)}, u32[]{:S(2)}, u32[]{:S(2)}) collective-permute-start(bf16[256,128]{1,0:T(8,128)(2,1)S(1)} %fusion.5), channel_id=1, source_target_pairs={{0,192},{16,208},{32,224},{48,240},{8,72},{24,88},{40,104},{56,120... | collective-permute-start | bytes 196616 | tf_op jit(solution)/shard_map/ppermute | solution.py:238
  43.7 6.5 %collective-permute-start.10 = (bf16[256,128]{1,0:T(8,128)(2,1)S(1)}, bf16[256,128]{1,0:T(8,128)(2,1)S(1)}, u32[]{:S(2)}, u32[]{:S(2)}) collective-permute-start(bf16[256,128]{1,0:T(8,128)(2,1)S(1)} %fusion.4), channel_id=1, source_target_pairs={{0,192},{16,208},{32,224},{48,240},{8,72},{24,88},{40,104},{56,120... | collective-permute-start | bytes 196616 | tf_op jit(solution)/shard_map/ppermute | solution.py:238
  50.6 5.1 %collective-permute-start.13 = (bf16[512,128]{1,0:T(8,128)(2,1)S(1)}, bf16[512,128]{1,0:T(8,128)(2,1)S(1)}, u32[]{:S(2)}, u32[]{:S(2)}) collective-permute-start(bf16[512,128]{1,0:T(8,128)(2,1)S(1)} %multiply_convert_fusion.1), channel_id=1, source_target_pairs={{0,4},{4,0},{1,5},{5,1},{2,6},{6,2},{3,7},{7,3},{8,12},{12,8},{9,1... | collective-permute-start | bytes 393224 | tf_op jit(solution)/shard_map/ppermute | solution.py:242
  55.7 8.1 %collective-permute-start.16 = (bf16[512,128]{1,0:T(8,128)(2,1)S(1)}, bf16[512,128]{1,0:T(8,128)(2,1)S(1)}, u32[]{:S(2)}, u32[]{:S(2)}) collective-permute-start(bf16[512,128]{1,0:T(8,128)(2,1)S(1)} %fusion.1), channel_id=1, source_target_pairs={{0,2},{1,3},{2,0},{3,1},{4,6},{5,7},{6,4},{7,5},{8,10},{9,11},{10,... | collective-permute-start | bytes 393224 | tf_op jit(solution)/shard_map/ppermute | solution.py:281
  58.8 5.0 %collective-permute-start.15 = (bf16[512,128]{1,0:T(8,128)(2,1)S(1)}, bf16[512,128]{1,0:T(8,128)(2,1)S(1)}, u32[]{:S(2)}, u32[]{:S(2)}) collective-permute-start(bf16[512,128]{1,0:T(8,128)(2,1)S(1)} %fusion.1), channel_id=1, source_target_pairs={{0,3},{1,0},{2,1},{3,2},{4,7},{5,4},{6,5},{7,6},{8,11},{9,8},{10,9... | collective-permute-start | bytes 393224 | tf_op jit(solution)/shard_map/ppermute | solution.py:281
  60.0 6.2 %collective-permute-start.14 = (bf16[512,128]{1,0:T(8,128)(2,1)S(1)}, bf16[512,128]{1,0:T(8,128)(2,1)S(1)}, u32[]{:S(2)}, u32[]{:S(2)}) collective-permute-start(bf16[512,128]{1,0:T(8,128)(2,1)S(1)} %fusion.1), channel_id=1, source_target_pairs={{0,1},{1,2},{2,3},{3,0},{4,5},{5,6},{6,7},{7,4},{8,9},{9,10},{10,1... | collective-permute-start | bytes 393224 | tf_op jit(solution)/shard_map/ppermute | solution.py:281

commit v6 on v5

--- a/solution.py
+++ b/solution.py
@@ -14,7 +14,7 @@
 MIB = 2**20
 CHUNKS = 2
 DEPTH = 4
-GROUP = (2, 1, 1)
+GROUP = (2, 2, 1)
 READY = 4
 PARTS = (
     tuple(("far", i) for i in range(4)),
@@ -97,8 +97,9 @@
 
     def loads_ahead():
         for i, item in enumerate(columns_of(pos, 1)[:READY]):
+            for k, col, half in windows(item, 256 * (i % 2)):
+                yield pltpu.make_async_copy(acts.at[:, col], ready_a.at[i // 2, :, half], rsem.at[i, k, 0])
             for k, col, half in windows(item):
-                yield pltpu.make_async_copy(acts.at[:, col], ready_a.at[i, :, half], rsem.at[i, k, 0])
                 yield pltpu.make_async_copy(err.at[:, col], ready_e.at[i, :, half], rsem.at[i, k, 1])
 
     def ready(p):
@@ -108,7 +109,7 @@
                     copy.wait()
 
     def source(p):
-        return ready_a[p] if p < first else av[p]
+        return ready_a[p] if p * group < first else av[p]
 
     if part == 0:
         load_kc = pltpu.make_async_copy(kc, kcv, ksem)
@@ -169,7 +170,7 @@
         pltpu.SemaphoreType.DMA((n, 2, 2)),
     ]
     if part == 0:
-        outs += [pltpu.VMEM((512, 512), BF)] + [pltpu.VMEM((READY, 512, 256), BF)] * 2
+        outs += [pltpu.VMEM((512, 512), BF)] + [pltpu.VMEM((READY // 2, 512, 512), BF), pltpu.VMEM((READY, 512, 256), BF)]
         scratch = [
             pltpu.VMEM((512, 512), BF),
             *scratch,

time: 67.1 us -> 67.3 us (level)
  no operation moved by 1% of the time
where the time goes in v6:
time: 67.3 us; the launch traced here: 67.1 us
  starting transfers between devices  25 us (37%)
  waiting for transfers between devices  23.6 us (35%)
  Pallas kernels  14.7 us (22%)
  other arithmetic  2.78 us (4%)
  between operations  0.82 us (1%)
    pallas_call x3, Pallas kernels, grad_part(): pl.pallas_call(functools.partial(grad_kernel, part=part), in_specs=[in_sm...  11.7 us
    ppermute x4, starting transfers between devices, z_step(): return lax.ppermute(x, ('zh', 'y', 'core'), pairs)  11.1 us
    ppermute x3, waiting for transfers between devices, y_step(): return lax.ppermute(x, ('y', 'core'), ring_pairs(which, (4, 2), 0, 1))  7.89 us
    ppermute x4, waiting for transfers between devices, z_step(): return lax.ppermute(x, ('zh', 'y', 'core'), pairs)  7.52 us
    ppermute x7, waiting for transfers between devices, swap(): return lax.ppermute(x, axis, [(0, 1), (1, 0)])  5.91 us
    ppermute x3, starting transfers between devices, body(): lax.ppermute(total.astype(BF), 'x', [(i, (i + d) % 4) for i in range(4)])  5.16 us
    ppermute x3, starting transfers between devices, y_step(): return lax.ppermute(x, ('y', 'core'), ring_pairs(which, (4, 2), 0, 1))  4.99 us
    ppermute x7, starting transfers between devices, swap(): return lax.ppermute(x, axis, [(0, 1), (1, 0)])  3.78 us
  transfers between devices with their start and end apart: 17, of which 11 were waited for; matrix products, arithmetic and copies ran while one was open for 2% of the time, Pallas kernels for 15%

profile of v6, /device:TPU:32, one launch (start us, length us, event | category | flops | bytes accessed | tf_op | source)
XLA Modules:
  0.0 67.1 jit_solution(17486019919316505495)
XLA Ops:
  0.7 4.4 %shard_map.67 = (bf16[4,512,128]{2,1,0:T(8,128)(2,1)S(1)}, bf16[4,512,128]{2,1,0:T(8,128)(2,1)S(1)}, bf16[4,512,256]{2,1,0:T(8,128)(2,1)S(1)}, bf16[512,512]{1,0...) custom-call(s32[3]{0:T(128)S(1)} %pad_add_fusion.pos, bf16[512,512]{1,0:T(8,128)(2,1)} %kc.1, ...), custom_call_target="tpu_custom_call" | custom-call | flops 1000000 | bytes 10000 | tf_op jit(solution)/shard_map/pallas_call | solution.py:180
  5.2 1.9 %collective-permute-done = bf16[4,512,128]{2,1,0:T(8,128)(2,1)S(1)} collective-permute-done((bf16[4,512,128]{2,1,0:T(8,128)(2,1)S(1)}, bf16[4,512,128]{2,1,0:T(8,128)(2,1)S(1)}, u32[]{:S(2)}, u32[]{:S(2)}) %collective-permute-start) | collective-permute-done | bytes 524320 | tf_op jit(solution)/shard_map/ppermute | solution.py:243
  7.3 1.7 %collective-permute-start.5 = (bf16[4,512,128]{2,1,0:T(8,128)(2,1)S(1)}, bf16[4,512,128]{2,1,0:T(8,128)(2,1)S(1)}, u32[]{:S(2)}, u32[]{:S(2)}) collective-permute-start(bf16[4,512,128]{2,1,0:T(8,128)(2,1)S(1)} %add_convert_fusion.2), channel_id=1, source_target_pairs={{0,16},{8,56},{16,0},{24,40},{32,48},{40,24},{48,32},{56,8},{1,17}... | collective-permute-start | bytes 1572872 | tf_op jit(solution)/shard_map/ppermute | solution.py:231
  8.9 3.8 %shard_map.68 = (bf16[8,512,128]{2,1,0:T(8,128)(2,1)S(1)}, bf16[8,512,128]{2,1,0:T(8,128)(2,1)S(1)}, bf16[8,512,256]{2,1,0:T(8,128)(2,1)S(1)}) custom-call(s32[3]{0:T(128)S(1)} %pad_add_fusion.pos, bf16[512,512]{1,0:T(8,128)(2,1)S(1)} %get-tuple-element.29.kc, bf16[512,4096]{1,0:T(8,128)(2,1)} %acts.5, bf16[512,4096]{1,0:T(8,128)(2,1)} %bitcast.27, ...), custom_call_target="tpu_custom_call" | custom-call | flops 1000000 | bytes 10000 | tf_op jit(solution)/shard_map/pallas_call | solution.py:180
  12.8 1.4 %collective-permute-start.2 = (bf16[2,512,128]{2,1,0:T(8,128)(2,1)S(1)}, bf16[2,512,128]{2,1,0:T(8,128)(2,1)S(1)}, u32[]{:S(2)}, u32[]{:S(2)}) collective-permute-start(bf16[2,512,128]{2,1,0:T(8,128)(2,1)S(1)} %get-tuple-element.53), channel_id=1, source_target_pairs={{0,8},{8,0},{1,9},{9,1},{2,10},{10,2},{3,11},{11,3},{4,12},{12,4},... | collective-permute-start | bytes 786440 | tf_op jit(solution)/shard_map/ppermute | solution.py:243
  14.8 0.6 collective-permute-done.2
  16.7 3.1 %collective-permute-start.8 = (bf16[4,512,128]{2,1,0:T(8,128)(2,1)S(1)}, bf16[4,512,128]{2,1,0:T(8,128)(2,1)S(1)}, u32[]{:S(2)}, u32[]{:S(2)}) collective-permute-start(bf16[4,512,128]{2,1,0:T(8,128)(2,1)S(1)} %add_convert_fusion), channel_id=1, source_target_pairs={{0,48},{8,24},{16,32},{24,8},{32,16},{40,56},{48,0},{56,40},{1,49}... | collective-permute-start | bytes 1572872 | tf_op jit(solution)/shard_map/ppermute | solution.py:231
  19.8 3.6 %shard_map.69 = (bf16[4,512,128]{2,1,0:T(8,128)(2,1)S(1)}, bf16[4,512,128]{2,1,0:T(8,128)(2,1)S(1)}, bf16[4,512,256]{2,1,0:T(8,128)(2,1)S(1)}) custom-call(s32[3]{0:T(128)S(1)} %pad_add_fusion.pos, bf16[512,512]{1,0:T(8,128)(2,1)S(1)} %get-tuple-element.29.kc, bf16[512,4096]{1,0:T(8,128)(2,1)} %acts.5, bf16[512,4096]{1,0:T(8,128)(2,1)} %bitcast.28), custom_call_target="tpu_custom_call" | custom-call | flops 1000000 | bytes 10000 | tf_op jit(solution)/shard_map/pallas_call | solution.py:180
  23.5 6.8 %collective-permute-done.7 = bf16[4,512,128]{2,1,0:T(8,128)(2,1)S(1)} collective-permute-done((bf16[4,512,128]{2,1,0:T(8,128)(2,1)S(1)}, bf16[4,512,128]{2,1,0:T(8,128)(2,1)S(1)}, u32[]{:S(2)}, u32[]{:S(2)}) %collective-permute-start.7) | collective-permute-done | bytes 524320 | tf_op jit(solution)/shard_map/ppermute | solution.py:231
  30.3 1.0 %collective-permute-done.8 = bf16[4,512,128]{2,1,0:T(8,128)(2,1)S(1)} collective-permute-done((bf16[4,512,128]{2,1,0:T(8,128)(2,1)S(1)}, bf16[4,512,128]{2,1,0:T(8,128)(2,1)S(1)}, u32[]{:S(2)}, u32[]{:S(2)}) %collective-permute-start.8) | collective-permute-done | bytes 524320 | tf_op jit(solution)/shard_map/ppermute | solution.py:231
  31.6 3.5 %collective-permute-start.11 = (bf16[2,256,128]{2,1,0:T(8,128)(2,1)S(1)}, bf16[2,256,128]{2,1,0:T(8,128)(2,1)S(1)}, u32[]{:S(2)}, u32[]{:S(2)}) collective-permute-start(bf16[2,256,128]{2,1,0:T(8,128)(2,1)S(1)} %slice.118), channel_id=1, source_target_pairs={{0,64},{16,80},{32,96},{48,112},{8,200},{24,216},{40,232},{56,248}... | collective-permute-start | bytes 393224 | tf_op jit(solution)/shard_map/ppermute | solution.py:239
  35.3 4.2 %collective-permute-done.11 = bf16[2,256,128]{2,1,0:T(8,128)(2,1)S(1)} collective-permute-done((bf16[2,256,128]{2,1,0:T(8,128)(2,1)S(1)}, bf16[2,256,128]{2,1,0:T(8,128)(2,1)S(1)}, u32[]{:S(2)}, u32[]{:S(2)}) %collective-permute-start.11) | collective-permute-done | bytes 131104 | tf_op jit(solution)/shard_map/ppermute | solution.py:239
  39.6 4.3 %collective-permute-start.12 = (bf16[256,128]{1,0:T(8,128)(2,1)S(1)}, bf16[256,128]{1,0:T(8,128)(2,1)S(1)}, u32[]{:S(2)}, u32[]{:S(2)}) collective-permute-start(bf16[256,128]{1,0:T(8,128)(2,1)S(1)} %fusion.5), channel_id=1, source_target_pairs={{0,192},{16,208},{32,224},{48,240},{8,72},{24,88},{40,104},{56,120... | collective-permute-start | bytes 196616 | tf_op jit(solution)/shard_map/ppermute | solution.py:239
  43.9 3.1 %collective-permute-start.10 = (bf16[256,128]{1,0:T(8,128)(2,1)S(1)}, bf16[256,128]{1,0:T(8,128)(2,1)S(1)}, u32[]{:S(2)}, u32[]{:S(2)}) collective-permute-start(bf16[256,128]{1,0:T(8,128)(2,1)S(1)} %fusion.4), channel_id=1, source_target_pairs={{0,192},{16,208},{32,224},{48,240},{8,72},{24,88},{40,104},{56,120... | collective-permute-start | bytes 196616 | tf_op jit(solution)/shard_map/ppermute | solution.py:239
  47.1 3.3 %collective-permute-done.10 = bf16[256,128]{1,0:T(8,128)(2,1)S(1)} collective-permute-done((bf16[256,128]{1,0:T(8,128)(2,1)S(1)}, bf16[256,128]{1,0:T(8,128)(2,1)S(1)}, u32[]{:S(2)}, u32[]{:S(2)}) %collective-permute-start.10) | collective-permute-done | bytes 65568 | tf_op jit(solution)/shard_map/ppermute | solution.py:239
  50.8 1.6 %collective-permute-start.13 = (bf16[512,128]{1,0:T(8,128)(2,1)S(1)}, bf16[512,128]{1,0:T(8,128)(2,1)S(1)}, u32[]{:S(2)}, u32[]{:S(2)}) collective-permute-start(bf16[512,128]{1,0:T(8,128)(2,1)S(1)} %multiply_convert_fusion.1), channel_id=1, source_target_pairs={{0,4},{4,0},{1,5},{5,1},{2,6},{6,2},{3,7},{7,3},{8,12},{12,8},{9,1... | collective-permute-start | bytes 393224 | tf_op jit(solution)/shard_map/ppermute | solution.py:243
  52.4 0.7 %convert_subtract_fusion = f32[512,128]{1,0:T(8,128)} fusion(bf16[512,128]{1,0:T(8,128)(2,1)S(1)} %multiply_convert_fusion.1, f32[1,512,128]{2,1,0:T(8,128)S(1)} %copy-done, f32[256,128]{1,0:T(8,128)S(1)} %fusion.2, f32[256,128]{1,0:T(8,128)S(1)} %fusion.3), kind=kLoop, calls=%fused_computation.12 | loop fusion | flops 327680 | bytes 917504 | tf_op jit(solution)/shard_map/sub | solution.py:277
  53.1 2.7 %collective-permute-done.13 = bf16[512,128]{1,0:T(8,128)(2,1)S(1)} collective-permute-done((bf16[512,128]{1,0:T(8,128)(2,1)S(1)}, bf16[512,128]{1,0:T(8,128)(2,1)S(1)}, u32[]{:S(2)}, u32[]{:S(2)}) %collective-permute-start.13) | collective-permute-done | bytes 131104 | tf_op jit(solution)/shard_map/ppermute | solution.py:243
  55.9 3.1 %collective-permute-start.16 = (bf16[512,128]{1,0:T(8,128)(2,1)S(1)}, bf16[512,128]{1,0:T(8,128)(2,1)S(1)}, u32[]{:S(2)}, u32[]{:S(2)}) collective-permute-start(bf16[512,128]{1,0:T(8,128)(2,1)S(1)} %fusion.1), channel_id=1, source_target_pairs={{0,2},{1,3},{2,0},{3,1},{4,6},{5,7},{6,4},{7,5},{8,10},{9,11},{10,... | collective-permute-start | bytes 393224 | tf_op jit(solution)/shard_map/ppermute | solution.py:282
  59.0 1.1 %collective-permute-start.15 = (bf16[512,128]{1,0:T(8,128)(2,1)S(1)}, bf16[512,128]{1,0:T(8,128)(2,1)S(1)}, u32[]{:S(2)}, u32[]{:S(2)}) collective-permute-start(bf16[512,128]{1,0:T(8,128)(2,1)S(1)} %fusion.1), channel_id=1, source_target_pairs={{0,3},{1,0},{2,1},{3,2},{4,7},{5,4},{6,5},{7,6},{8,11},{9,8},{10,9... | collective-permute-start | bytes 393224 | tf_op jit(solution)/shard_map/ppermute | solution.py:282
  60.2 0.9 %collective-permute-start.14 = (bf16[512,128]{1,0:T(8,128)(2,1)S(1)}, bf16[512,128]{1,0:T(8,128)(2,1)S(1)}, u32[]{:S(2)}, u32[]{:S(2)}) collective-permute-start(bf16[512,128]{1,0:T(8,128)(2,1)S(1)} %fusion.1), channel_id=1, source_target_pairs={{0,1},{1,2},{2,3},{3,0},{4,5},{5,6},{6,7},{7,4},{8,9},{9,10},{10,1... | collective-permute-start | bytes 393224 | tf_op jit(solution)/shard_map/ppermute | solution.py:282
  61.1 3.0 %shard_map.70 = bf16[512,4096]{1,0:T(8,128)(2,1)} custom-call(s32[3]{0:T(128)S(1)} %pad_add_fusion.pos, bf16[4,512,256]{2,1,0:T(8,128)(2,1)S(1)} %get-tuple-element.45.refs_0_, bf16[8,512,256]{2,1,0:T(8,128)(2,1)S(1)} %get-tuple-element.46.refs_1_, bf16[4,512,256]{2,1,0:T(8,128)(2,1)S(1)} %get-tuple-element.47.refs_2_), custom_call_target="tpu_custom_call" | custom-call | bytes 8388608 | tf_op jit(solution)/shard_map/pallas_call | solution.py:212
  64.0 2.3 %collective-permute-done.14 = bf16[512,128]{1,0:T(8,128)(2,1)S(1)} collective-permute-done((bf16[512,128]{1,0:T(8,128)(2,1)S(1)}, bf16[512,128]{1,0:T(8,128)(2,1)S(1)}, u32[]{:S(2)}, u32[]{:S(2)}) %collective-permute-start.14) | collective-permute-done | bytes 131104 | tf_op jit(solution)/shard_map/ppermute | solution.py:282
  66.3 0.8 %multiply_convert_fusion = bf16[512,128]{1,0:T(8,128)(2,1)} fusion(bf16[512,128]{1,0:T(8,128)(2,1)S(1)} %collective-permute-done.16, bf16[512,128]{1,0:T(8,128)(2,1)S(1)} %collective-permute-done.15, bf16[512,128]{1,0:T(8,128)(2,1)S(1)} %collective-permute-done.14, bf16[512,128]{1,0:T(8,128)(2,1)S(1)} %collective-permute-done.13, ...), kind=kLoop, calls=%fused_computation.10 | loop fusion | flops 720896 | bytes 786432 | tf_op jit(solution)/shard_map/convert_element_type | solution.py:284
  (37 shorter events, 3.4 us)
Async XLA Ops:
  5.1 2.0 %collective-permute-start = (bf16[4,512,128]{2,1,0:T(8,128)(2,1)S(1)}, bf16[4,512,128]{2,1,0:T(8,128)(2,1)S(1)}, u32[]{:S(2)}, u32[]{:S(2)}) collective-permute-start(bf16[4,512,128]{2,1,0:T(8,128)(2,1)S(1)} %get-tuple-element.27), channel_id=1, source_target_pairs={{0,8},{8,0},{1,9},{9,1},{2,10},{10,2},{3,11},{11,3},{4,12},{12,4},... | collective-permute-start | bytes 1572872 | tf_op jit(solution)/shard_map/ppermute | solution.py:243
  7.3 9.3 %collective-permute-start.5 = (bf16[4,512,128]{2,1,0:T(8,128)(2,1)S(1)}, bf16[4,512,128]{2,1,0:T(8,128)(2,1)S(1)}, u32[]{:S(2)}, u32[]{:S(2)}) collective-permute-start(bf16[4,512,128]{2,1,0:T(8,128)(2,1)S(1)} %add_convert_fusion.2), channel_id=1, source_target_pairs={{0,16},{8,56},{16,0},{24,40},{32,48},{40,24},{48,32},{56,8},{1,17}... | collective-permute-start | bytes 1572872 | tf_op jit(solution)/shard_map/ppermute | solution.py:231
  12.8 2.5 %collective-permute-start.2 = (bf16[2,512,128]{2,1,0:T(8,128)(2,1)S(1)}, bf16[2,512,128]{2,1,0:T(8,128)(2,1)S(1)}, u32[]{:S(2)}, u32[]{:S(2)}) collective-permute-start(bf16[2,512,128]{2,1,0:T(8,128)(2,1)S(1)} %get-tuple-element.53), channel_id=1, source_target_pairs={{0,8},{8,0},{1,9},{9,1},{2,10},{10,2},{3,11},{11,3},{4,12},{12,4},... | collective-permute-start | bytes 786440 | tf_op jit(solution)/shard_map/ppermute | solution.py:243
  14.2 1.5 %collective-permute-start.1 = (bf16[2,512,128]{2,1,0:T(8,128)(2,1)S(1)}, bf16[2,512,128]{2,1,0:T(8,128)(2,1)S(1)}, u32[]{:S(2)}, u32[]{:S(2)}) collective-permute-start(bf16[2,512,128]{2,1,0:T(8,128)(2,1)S(1)} %get-tuple-element.54), channel_id=1, source_target_pairs={{0,8},{8,0},{1,9},{9,1},{2,10},{10,2},{3,11},{11,3},{4,12},{12,4},... | collective-permute-start | bytes 786440 | tf_op jit(solution)/shard_map/ppermute | solution.py:243
  14.3 1.8 %collective-permute-start.3 = (bf16[2,512,128]{2,1,0:T(8,128)(2,1)S(1)}, bf16[2,512,128]{2,1,0:T(8,128)(2,1)S(1)}, u32[]{:S(2)}, u32[]{:S(2)}) collective-permute-start(bf16[2,512,128]{2,1,0:T(8,128)(2,1)S(1)} %get-tuple-element.52), channel_id=1, source_target_pairs={{0,8},{8,0},{1,9},{9,1},{2,10},{10,2},{3,11},{11,3},{4,12},{12,4},... | collective-permute-start | bytes 786440 | tf_op jit(solution)/shard_map/ppermute | solution.py:243
  14.7 1.8 %collective-permute-start.4 = (bf16[2,512,128]{2,1,0:T(8,128)(2,1)S(1)}, bf16[2,512,128]{2,1,0:T(8,128)(2,1)S(1)}, u32[]{:S(2)}, u32[]{:S(2)}) collective-permute-start(bf16[2,512,128]{2,1,0:T(8,128)(2,1)S(1)} %get-tuple-element.51), channel_id=1, source_target_pairs={{0,8},{8,0},{1,9},{9,1},{2,10},{10,2},{3,11},{11,3},{4,12},{12,4},... | collective-permute-start | bytes 786440 | tf_op jit(solution)/shard_map/ppermute | solution.py:243
  15.8 14.5 %collective-permute-start.7 = (bf16[4,512,128]{2,1,0:T(8,128)(2,1)S(1)}, bf16[4,512,128]{2,1,0:T(8,128)(2,1)S(1)}, u32[]{:S(2)}, u32[]{:S(2)}) collective-permute-start(bf16[4,512,128]{2,1,0:T(8,128)(2,1)S(1)} %add_convert_fusion.1), channel_id=1, source_target_pairs={{0,16},{8,56},{16,0},{24,40},{32,48},{40,24},{48,32},{56,8},{1,17}... | collective-permute-start | bytes 1572872 | tf_op jit(solution)/shard_map/ppermute | solution.py:231
  16.7 14.6 %collective-permute-start.8 = (bf16[4,512,128]{2,1,0:T(8,128)(2,1)S(1)}, bf16[4,512,128]{2,1,0:T(8,128)(2,1)S(1)}, u32[]{:S(2)}, u32[]{:S(2)}) collective-permute-start(bf16[4,512,128]{2,1,0:T(8,128)(2,1)S(1)} %add_convert_fusion), channel_id=1, source_target_pairs={{0,48},{8,24},{16,32},{24,8},{32,16},{40,56},{48,0},{56,40},{1,49}... | collective-permute-start | bytes 1572872 | tf_op jit(solution)/shard_map/ppermute | solution.py:231
  23.4 27.0 %copy-start = (f32[1,512,128]{2,1,0:T(8,128)S(1)}, f32[1,512,128]{2,1,0:T(8,128)}, u32[]{:S(2)}) copy-start(f32[1,512,128]{2,1,0:T(8,128)} %param.7) | copy-start | bytes 786436
  23.4 8.0 %collective-permute-start.6 = (bf16[4,512,128]{2,1,0:T(8,128)(2,1)S(1)}, bf16[4,512,128]{2,1,0:T(8,128)(2,1)S(1)}, u32[]{:S(2)}, u32[]{:S(2)}) collective-permute-start(bf16[4,512,128]{2,1,0:T(8,128)(2,1)S(1)} %get-tuple-element.39), channel_id=1, source_target_pairs={{0,8},{8,0},{1,9},{9,1},{2,10},{10,2},{3,11},{11,3},{4,12},{12,4},... | collective-permute-start | bytes 1572872 | tf_op jit(solution)/shard_map/ppermute | solution.py:243
  31.6 7.9 %collective-permute-start.11 = (bf16[2,256,128]{2,1,0:T(8,128)(2,1)S(1)}, bf16[2,256,128]{2,1,0:T(8,128)(2,1)S(1)}, u32[]{:S(2)}, u32[]{:S(2)}) collective-permute-start(bf16[2,256,128]{2,1,0:T(8,128)(2,1)S(1)} %slice.118), channel_id=1, source_target_pairs={{0,64},{16,80},{32,96},{48,112},{8,200},{24,216},{40,232},{56,248}... | collective-permute-start | bytes 393224 | tf_op jit(solution)/shard_map/ppermute | solution.py:239
  35.2 8.7 %collective-permute-start.9 = (bf16[2,256,128]{2,1,0:T(8,128)(2,1)S(1)}, bf16[2,256,128]{2,1,0:T(8,128)(2,1)S(1)}, u32[]{:S(2)}, u32[]{:S(2)}) collective-permute-start(bf16[2,256,128]{2,1,0:T(8,128)(2,1)S(1)} %slice.119), channel_id=1, source_target_pairs={{0,64},{16,80},{32,96},{48,112},{8,200},{24,216},{40,232},{56,248}... | collective-permute-start | bytes 393224 | tf_op jit(solution)/shard_map/ppermute | solution.py:239
  39.6 7.5 %collective-permute-start.12 = (bf16[256,128]{1,0:T(8,128)(2,1)S(1)}, bf16[256,128]{1,0:T(8,128)(2,1)S(1)}, u32[]{:S(2)}, u32[]{:S(2)}) collective-permute-start(bf16[256,128]{1,0:T(8,128)(2,1)S(1)} %fusion.5), channel_id=1, source_target_pairs={{0,192},{16,208},{32,224},{48,240},{8,72},{24,88},{40,104},{56,120... | collective-permute-start | bytes 196616 | tf_op jit(solution)/shard_map/ppermute | solution.py:239
  43.9 6.5 %collective-permute-start.10 = (bf16[256,128]{1,0:T(8,128)(2,1)S(1)}, bf16[256,128]{1,0:T(8,128)(2,1)S(1)}, u32[]{:S(2)}, u32[]{:S(2)}) collective-permute-start(bf16[256,128]{1,0:T(8,128)(2,1)S(1)} %fusion.4), channel_id=1, source_target_pairs={{0,192},{16,208},{32,224},{48,240},{8,72},{24,88},{40,104},{56,120... | collective-permute-start | bytes 196616 | tf_op jit(solution)/shard_map/ppermute | solution.py:239
  50.8 5.1 %collective-permute-start.13 = (bf16[512,128]{1,0:T(8,128)(2,1)S(1)}, bf16[512,128]{1,0:T(8,128)(2,1)S(1)}, u32[]{:S(2)}, u32[]{:S(2)}) collective-permute-start(bf16[512,128]{1,0:T(8,128)(2,1)S(1)} %multiply_convert_fusion.1), channel_id=1, source_target_pairs={{0,4},{4,0},{1,5},{5,1},{2,6},{6,2},{3,7},{7,3},{8,12},{12,8},{9,1... | collective-permute-start | bytes 393224 | tf_op jit(solution)/shard_map/ppermute | solution.py:243
  55.9 8.1 %collective-permute-start.16 = (bf16[512,128]{1,0:T(8,128)(2,1)S(1)}, bf16[512,128]{1,0:T(8,128)(2,1)S(1)}, u32[]{:S(2)}, u32[]{:S(2)}) collective-permute-start(bf16[512,128]{1,0:T(8,128)(2,1)S(1)} %fusion.1), channel_id=1, source_target_pairs={{0,2},{1,3},{2,0},{3,1},{4,6},{5,7},{6,4},{7,5},{8,10},{9,11},{10,... | collective-permute-start | bytes 393224 | tf_op jit(solution)/shard_map/ppermute | solution.py:282
  59.0 5.0 %collective-permute-start.15 = (bf16[512,128]{1,0:T(8,128)(2,1)S(1)}, bf16[512,128]{1,0:T(8,128)(2,1)S(1)}, u32[]{:S(2)}, u32[]{:S(2)}) collective-permute-start(bf16[512,128]{1,0:T(8,128)(2,1)S(1)} %fusion.1), channel_id=1, source_target_pairs={{0,3},{1,0},{2,1},{3,2},{4,7},{5,4},{6,5},{7,6},{8,11},{9,8},{10,9... | collective-permute-start | bytes 393224 | tf_op jit(solution)/shard_map/ppermute | solution.py:282
  60.2 6.2 %collective-permute-start.14 = (bf16[512,128]{1,0:T(8,128)(2,1)S(1)}, bf16[512,128]{1,0:T(8,128)(2,1)S(1)}, u32[]{:S(2)}, u32[]{:S(2)}) collective-permute-start(bf16[512,128]{1,0:T(8,128)(2,1)S(1)} %fusion.1), channel_id=1, source_target_pairs={{0,1},{1,2},{2,3},{3,0},{4,5},{5,6},{6,7},{7,4},{8,9},{9,10},{10,1... | collective-permute-start | bytes 393224 | tf_op jit(solution)/shard_map/ppermute | solution.py:282
